TPU v7x, 256 devices: a whole 4x4x8 slice. The times are simulated.
256 devices in a mesh: sub: 64 (over z, y, x_lo), fold: 4 (over x_hi, core).
Axes of the slice: x: 4 (x_hi: 2, x_lo: 2; x = x_hi * 2 + x_lo), y: 4, z: 8, core: 2. Of those that a mesh axis runs over, the one named last changes fastest.
Arguments:
- right_side: float32 [32768, 64], P(('sub', 'fold')), may hold values from -6 to 6
- blocks: float32 [256, 7, 128, 128], P('sub'), may hold values from -2 to 9, as said below
- block_cols: int32 [256, 7], P('sub'), may hold values from 0 to 7, as said below
- send_lists: int32 [64, 2, 2], P('sub'), may hold values from 0 to 3, as said below
Outputs:
- correction: float32 [32768, 64], P(('sub', 'fold'))
- residual: float32 [32768, 64], P(('sub', 'fold'))
Inputs may be any that keep to these rules, and one draw needn't show every extreme that they name: `block_cols`: entry 0 of each block row is the row's own block (its device index). Values below 4 name the device's own blocks, 4 + j the j-th block of the previous device's list to its next neighbour, 6 + j the j-th block of the next device's list to its previous neighbour; the first subset device names no previous neighbour's block and the last none of the next. `send_lists`: each list holds 2 distinct block indices of the device's own blocks. `blocks`: the operator is nonsingular and well conditioned.
All inputs are finite; a program needn't handle non-finite values.
Results may differ from a plain program's by a relative error of at most 0.0003.
Values sent between devices are 32-bit elements; how exact they have to be, the bound alone decides.
No kernel may reach another device: no remote copies, remote signals or barrier semaphores. Data moves between devices by JAX's collectives and lax.ppermute only.
A program may use at most 64 MiB of HBM per device.

v0:
```python
import functools

import jax
import jax.numpy as jnp
from jax import lax
from jax.experimental import pallas as pl
from jax.experimental.pallas import tpu as pltpu
from jax.sharding import PartitionSpec as P

STEPS = 4
CYCLES = 3
CENTER = 4.5
RADIUS = 3.5
BS = 128
NB = 4
HALO = 2
EXT = NB + 2 * HALO
ROWS = NB * BS
COLS = 32
PAIRS = [(i, j) for i in range(STEPS + 1) for j in range(i, STEPS + 1)]
GROUP = 128 // COLS
GRAM_ROWS = (len(PAIRS) + GROUP - 1) // GROUP

COUNT = STEPS * CYCLES + 1
SUBLANES = 8
PART = 8
TILES = -(-COUNT * (COUNT + 1) // 2 // (SUBLANES * GROUP))
SUM_ROWS = TILES * SUBLANES
LIMIT = 2000.0

VMEM = pl.BlockSpec(memory_space=pltpu.VMEM)
SMEM = pl.BlockSpec(memory_space=pltpu.SMEM)
PARAMS = pltpu.CompilerParams(vmem_limit_bytes=32 * 1024 * 1024)


def f32(*shape):
    return jax.ShapeDtypeStruct(shape, jnp.float32)


def bf16(*shape):
    return jax.ShapeDtypeStruct(shape, jnp.bfloat16)


def split(value):
    high = value.astype(jnp.bfloat16)
    value = value - high.astype(jnp.float32)
    middle = value.astype(jnp.bfloat16)
    low = (value - middle.astype(jnp.float32)).astype(jnp.bfloat16)
    return high, middle, low


def product(vector, high, middle, low):
    parts = split(vector)
    first = jnp.dot(
        jnp.concatenate(parts, 0), high[...], preferred_element_type=jnp.float32
    )
    second = jnp.dot(
        jnp.concatenate(parts[:2], 0), middle[...], preferred_element_type=jnp.float32
    )
    third = jnp.dot(parts[0], low[...], preferred_element_type=jnp.float32)
    small = first[2 * COLS :] + second[COLS:] + third
    return first[:COLS] + (first[COLS : 2 * COLS] + second[:COLS] + small)


def mask_kernel(lists, masks):
    for side in range(2):
        for slot in range(HALO):
            for block in range(NB):
                chosen = jnp.full((SUBLANES, BS), lists[side, slot], jnp.int32) == block
                masks[side * HALO + slot, block] = jnp.where(chosen, 1.0, 0.0)


def operator_kernel(cols, blocks, *refs):
    own, received, dense = refs[:3], refs[3:6], refs[6]
    dense[...] = jnp.zeros_like(dense)
    for row in range(NB):
        for slot in range(blocks.shape[1]):
            start = pl.multiple_of(cols[row, slot] * BS, BS)
            place = (pl.ds(start, BS), slice(row * BS, (row + 1) * BS))
            dense[place] = dense[place] + blocks[row, slot].T
    unit = (
        lax.broadcasted_iota(jnp.int32, (BS, BS), 0) == lax.broadcasted_iota(jnp.int32, (BS, BS), 1)
    ).astype(jnp.float32)
    for row in range(NB):
        for column in range(EXT):
            place = (slice(column * BS, (column + 1) * BS), slice(row * BS, (row + 1) * BS))
            value = dense[place]
            if row == column:
                value = value - CENTER * unit
            targets = own if column < NB else received
            start = (column % NB) * BS
            for target, part in zip(targets, split(value * (1.0 / RADIUS))):
                target[start : start + BS, row * BS : (row + 1) * BS] = part


def write_chosen(masks, vector, to_next, to_previous):
    repeats = vector.shape[0] // SUBLANES
    for slot in range(HALO):
        for side, target in ((0, to_next), (1, to_previous)):
            total = None
            for block in range(NB):
                mask = jnp.concatenate([masks[side * HALO + slot, block]] * repeats, 0)
                value = vector[:, block * BS : (block + 1) * BS]
                total = value if total is None else jnp.where(mask > 0.5, value, total)
            target[:, slot * BS : (slot + 1) * BS] = total


def start_kernel(masks, parts, result, to_next, to_previous):
    vector = jnp.concatenate([parts[block] for block in range(NB)], 1)
    result[...] = vector
    write_chosen(masks, vector, to_next, to_previous)


def step_kernel(masks, partial, from_previous, from_next, *refs):
    parts, (result, to_next, to_previous) = refs[:3], refs[3:]
    received = jnp.concatenate([from_previous[...], from_next[...]], 1)
    vector = partial[...] + product(received, *parts)
    result[...] = vector
    write_chosen(masks, vector, to_next, to_previous)


def small_solve(matrix, target):
    count = len(target)
    lower = [[None] * count for unused in range(count)]
    inverse = [None] * count
    for outer in range(count):
        for inner in range(outer + 1):
            total = matrix[outer][inner]
            for other in range(inner):
                total = total - lower[outer][other] * lower[inner][other]
            if outer == inner:
                inverse[outer] = 1.0 / jnp.sqrt(total)
            else:
                lower[outer][inner] = total * inverse[inner]
    solved = []
    for outer in range(count):
        total = target[outer]
        for other in range(outer):
            total = total - lower[outer][other] * solved[other]
        solved.append(total * inverse[outer])
    result = [None] * count
    for outer in reversed(range(count)):
        total = solved[outer]
        for other in range(outer + 1, count):
            total = total - lower[other][outer] * result[other]
        result[outer] = total * inverse[outer]
    return result


def two_sum(left, right):
    total = left + right
    shadow = total - left
    return total, (left - (total - shadow)) + (right - shadow)


def coarse_split(value):
    grid = jnp.max(jnp.abs(value), 0, keepdims=True) * (1.5 * 2.0**15)
    coarse = (value + grid) - grid
    return coarse, value - coarse


def gram_row(vector, earlier):
    turned = jnp.concatenate([vector[:, i * BS : (i + 1) * BS] for i in range(NB)], 0).T
    coarse, rest = coarse_split(turned)
    row = []
    for other, other_rest in [*earlier, (coarse, rest)]:
        high = low = None
        for start in range(0, BS, SUBLANES):
            place = slice(start, start + SUBLANES)
            main = other[place] * coarse[place]
            side = other[place] * rest[place] + other_rest[place] * turned[place]
            high = main if high is None else high + main
            low = side if low is None else low + side
        row.append((high, low))
    return coarse, rest, row


def round_kernel(*refs):
    vector, parts, earlier = refs[0], refs[1:4], refs[4:-5]
    partial, coarse, rest, high, low = refs[-5:]
    value = vector[...]
    partial[...] = product(value, *parts)
    earlier = [(earlier[i], earlier[i + 1]) for i in range(0, len(earlier), 2)]
    coarse[...], rest[...], row = gram_row(value, earlier)
    for index, (one, other) in enumerate(row):
        high[index], low[index] = one, other


def pack_kernel(*refs):
    vector, earlier = refs[0], refs[1 : 1 + 2 * (COUNT - 1)]
    sums, packed = refs[1 + 2 * (COUNT - 1) : -1], refs[-1]
    earlier = [(earlier[i], earlier[i + 1]) for i in range(0, len(earlier), 2)]
    pairs = []
    for index in range(0, len(sums), 2):
        for i in range(sums[index].shape[0]):
            pairs.append((sums[index][i], sums[index + 1][i]))
    pairs += gram_row(vector[...], earlier)[2]
    sublane = lax.broadcasted_iota(jnp.int32, (SUBLANES, BS), 0)
    lane = lax.broadcasted_iota(jnp.int32, (SUBLANES, BS), 1) // COLS

    def folded(high, low, shift, axis):
        high, error = two_sum(high, pltpu.roll(high, shift, axis))
        return high, low + pltpu.roll(low, shift, axis) + error

    zero = jnp.zeros((SUBLANES, BS), jnp.float32)
    for tile in range(TILES):
        tile_high, tile_low = zero, zero
        for group in range(GROUP):
            high, low = zero, zero
            for row in range(SUBLANES):
                index = (tile * GROUP + group) * SUBLANES + row
                if index < len(pairs):
                    one, other = pairs[index]
                    for shift in (4, 2, 1):
                        one, other = folded(one, other, shift, 0)
                    high = jnp.where(sublane == row, one, high)
                    low = jnp.where(sublane == row, other, low)
            for shift in (2 * COLS, COLS):
                high, low = folded(high, low, shift, 1)
            tile_high = jnp.where(lane == group, high, tile_high)
            tile_low = jnp.where(lane == group, low, tile_low)
        tile_high, tile_low = two_sum(tile_high, tile_low)
        for copy in range(PART):
            packed[copy, tile * SUBLANES : (tile + 1) * SUBLANES] = tile_high
            packed[copy, SUM_ROWS + tile * SUBLANES : SUM_ROWS + (tile + 1) * SUBLANES] = tile_low


def summed(parts):
    high, low = parts[0, :SUM_ROWS], parts[0, SUM_ROWS:]
    for index in range(1, PART):
        high, error = two_sum(high, parts[index, :SUM_ROWS])
        low = low + parts[index, SUM_ROWS:] + error
    return two_sum(high, low)


def sum_kernel(parts, total):
    high, low = summed(parts)
    for copy in range(PART):
        total[copy, :SUM_ROWS] = high
        total[copy, SUM_ROWS:] = low


def halves(value):
    scaled = value * 4097.0
    high = scaled - (scaled - value)
    return high, value - high


def added_product(total, factor, value):
    factor, factor_high, factor_low = factor
    value, low, value_high, value_low = value
    main = factor_high * value_high
    side = factor_high * value_low + (factor_low * value + factor * low)
    if total is None:
        return main, side
    high, error = two_sum(total[0], main)
    return high, total[1] + (error + side)


def basis_gram(coefficients, gram):
    depth = gram[0][0].shape[0]
    index = lax.broadcasted_iota(jnp.int32, (depth, BS), 0)
    wide = [jnp.concatenate([value] * (depth // SUBLANES), 0) for value in coefficients]
    factors = [(value, *halves(value)) for value in wide]
    rows = []
    for i in range(STEPS + 1):
        total = None
        for a, factor in enumerate(factors):
            total = added_product(total, factor, gram[a + i])
        high, low = two_sum(*total)
        rows.append((high, low, *halves(high)))
    result = [[None] * (STEPS + 1) for unused in range(STEPS + 1)]
    for j in range(STEPS + 1):
        shifted = jnp.zeros((depth, BS), jnp.float32)
        for a, value in enumerate(wide):
            shifted = jnp.where(index == a + j, value, shifted)
        factor = (shifted, *halves(shifted))
        for i in range(j + 1):
            high, low = added_product(None, factor, rows[i])
            size = depth
            while size > SUBLANES:
                size //= 2
                high, error = two_sum(high[:size], high[size:])
                low = low[:size] + low[size:] + error
            for shift in (4, 2, 1):
                high, error = two_sum(high, pltpu.roll(high, shift, 0))
                low = low + pltpu.roll(low, shift, 0) + error
            result[i][j] = result[j][i] = high + low
    return result


def solved_weights(gram):
    combined = [
        [CENTER * gram[i][j] + RADIUS * gram[i + 1][j] for j in range(STEPS + 1)]
        for i in range(STEPS)
    ]
    normal = [
        [CENTER * combined[i][j] + RADIUS * combined[i][j + 1] for j in range(STEPS)]
        for i in range(STEPS)
    ]
    weights = small_solve(normal, [combined[i][0] for i in range(STEPS)])
    left = [1.0 - CENTER * weights[0]]
    for i in range(1, STEPS):
        left.append(-(CENTER * weights[i] + RADIUS * weights[i - 1]))
    left.append(-(RADIUS * weights[STEPS - 1]))
    return weights, left


def convolved(left, right):
    result = [None] * (len(left) + len(right) - 1)
    for i, one in enumerate(left):
        for j, other in enumerate(right):
            term = one * other
            result[i + j] = term if result[i + j] is None else result[i + j] + term
    return result


def all_cycles_kernel(fold, parts, *refs):
    vectors, own, other = refs[:COUNT], refs[COUNT], refs[COUNT + 1]
    high, low = summed(parts)
    rolled = [(high, low)]
    for group in range(1, GROUP):
        shift = BS - group * COLS
        rolled.append((pltpu.roll(high, shift, 1), pltpu.roll(low, shift, 1)))

    def entry(i, j):
        index = max(i, j) * (max(i, j) + 1) // 2 + min(i, j)
        tile, rest = divmod(index, SUBLANES * GROUP)
        group, row = divmod(rest, SUBLANES)
        row += tile * SUBLANES
        return [value[row : row + 1] for value in rolled[group]]

    depth = 2 * SUBLANES
    padding = [jnp.zeros((depth - COUNT, BS), jnp.float32)]
    gram = []
    for i in range(COUNT):
        entries = [entry(i, j) for j in range(COUNT)]
        value = jnp.concatenate([one for one, unused in entries] + padding, 0)
        rest = jnp.concatenate([one for unused, one in entries] + padding, 0)
        gram.append((value, rest, *halves(value)))

    def spread(value):
        return jnp.broadcast_to(value, (SUBLANES, BS))

    here = [[spread(entry(i, j)[0]) for j in range(STEPS + 1)] for i in range(STEPS + 1)]
    weights, polynomial = solved_weights(here)
    solution_part = list(weights)
    for cycle in range(1, CYCLES):
        here = basis_gram(polynomial, gram)
        weights, left = solved_weights(here)
        update = convolved(polynomial, weights)
        solution_part = [
            one + solution_part[i] if i < len(solution_part) else one
            for i, one in enumerate(update)
        ]
        polynomial = convolved(polynomial, left)
    remaining = None
    for i in range(STEPS + 1):
        for j in range(STEPS + 1):
            term = (left[i] * left[j]) * here[i][j]
            remaining = term if remaining is None else remaining + term
    reach = None
    for i in range(COUNT):
        term = jnp.abs(polynomial[i]) * jnp.sqrt(spread(entry(i, i)[0]))
        reach = term if reach is None else reach + term
    lane = lax.broadcasted_iota(jnp.int32, (SUBLANES, BS), 1)
    fine = (reach < LIMIT * jnp.sqrt(remaining)) | (lane >= COLS)
    bad = jnp.max(jnp.where(fine, 0.0, 1.0), axis=(0, 1), keepdims=True)
    other[2 * COLS :] = jnp.broadcast_to(bad, (SUBLANES, BS))
    index = lax.broadcasted_iota(jnp.int32, (depth, BS), 0)
    stacked = []
    for values in (solution_part, polynomial):
        total = jnp.zeros((depth, BS), jnp.float32)
        for i, value in enumerate(values):
            value = jnp.concatenate([value] * (depth // SUBLANES), 0)
            total = jnp.where(index == i, value, total)
        stacked.append(total)
    turned = jnp.concatenate(stacked, 0).T
    place = fold[0]
    partner = place + 1 - 2 * (place % 2)
    for output in range(2):
        sums = [None, None]
        for i in range(COUNT - 1 + output):
            column = output * depth + i
            weight = jnp.broadcast_to(turned[:COLS, column : column + 1], (COLS, BS))
            for side, block in enumerate((place, partner)):
                value = vectors[i][:, pl.ds(pl.multiple_of(block * BS, BS), BS)]
                term = weight * value
                sums[side] = term if sums[side] is None else sums[side] + term
        own[output * COLS : (output + 1) * COLS] = sums[0]
        other[output * COLS : (output + 1) * COLS] = sums[1]


def join_kernel(core, own, other, arrived, correction, residual, bad):
    for output, target in enumerate((correction, residual)):
        place = slice(output * COLS, (output + 1) * COLS)
        target[pl.ds(pl.multiple_of(core[0] * COLS, COLS), COLS)] = own[place]
        target[pl.ds(pl.multiple_of((1 - core[0]) * COLS, COLS), COLS)] = arrived[place]
    worst = jnp.max(jnp.maximum(other[2 * COLS :], arrived[2 * COLS :]))
    bad[0] = (worst > 0.5).astype(jnp.int32)


def call(kernel, out_shape, smem, vmem, scratch=(), flops=10**6, out_specs=None):
    return pl.pallas_call(
        kernel,
        out_shape=out_shape,
        in_specs=[SMEM] * len(smem) + [VMEM] * len(vmem),
        out_specs=out_specs or jax.tree.map(lambda unused: VMEM, out_shape),
        scratch_shapes=scratch,
        compiler_params=PARAMS,
        cost_estimate=pl.CostEstimate(flops=flops, bytes_accessed=2**20, transcendentals=0),
    )(*smem, *vmem)


def exchanged_over(groups):
    def exchanged(value):
        return lax.all_to_all(value, "sub", 0, 0, axis_index_groups=groups)

    return exchanged


def passed(value, by):
    subs = lax.axis_size("sub")
    return lax.ppermute(value, "sub", [(i, (i + by) % subs) for i in range(subs)])


VECTOR = f32(COLS, ROWS)
HALO_PART = f32(COLS, HALO * BS)


def cycle_by_cycle(right_side, blocks, block_cols, lists, fold):
    gathered = lax.all_gather(right_side, "fold", axis=0, tiled=True)

    def applied(vector):
        own = vector.reshape(NB, BS, -1)
        received = [passed(own[lists[0]], 1), passed(own[lists[1]], -1)]
        extended = jnp.concatenate([own, *received], 0)

        def added(slot, total):
            stored = lax.dynamic_index_in_dim(blocks, slot, 1, False)
            source = extended[lax.dynamic_index_in_dim(block_cols, slot, 1, False)]
            return total + jnp.einsum(
                "bij,bjc->bic", stored, source, precision=lax.Precision.HIGHEST
            )

        return lax.fori_loop(0, blocks.shape[1], added, jnp.zeros_like(own)).reshape(vector.shape)

    def grown(power, basis):
        latest = lax.dynamic_index_in_dim(basis, power, 0, False)
        following = (applied(latest) - CENTER * latest) / RADIUS
        return lax.dynamic_update_index_in_dim(basis, following, power + 1, 0)

    def cycle(unused, state):
        correction, residual = state
        basis = jnp.zeros((STEPS + 1,) + residual.shape, jnp.float32).at[0].set(residual)
        basis = lax.fori_loop(0, STEPS, grown, basis)
        gram = jnp.einsum("irc,jrc->ijc", basis, basis, precision=lax.Precision.HIGHEST)
        weights, left = solved_weights(lax.psum(gram, "sub"))
        correction = correction + sum(weights[i] * basis[i] for i in range(STEPS))
        return correction, sum(left[i] * basis[i] for i in range(STEPS + 1))

    results = lax.fori_loop(0, CYCLES, cycle, (jnp.zeros_like(gathered), gathered))
    return tuple(lax.dynamic_slice_in_dim(value, fold * BS, BS, 0).T for value in results)


def on_device(right_side, blocks, block_cols, send_lists):
    subs = lax.axis_size("sub")
    lists = send_lists[0]
    fold = lax.axis_index("fold").astype(jnp.int32)
    core = (fold % 2).reshape(1)
    halves_of_columns = right_side.T.reshape(2, COLS, BS)
    parts = lax.all_to_all(jnp.concatenate([halves_of_columns] * 2, 0), "fold", 0, 0)
    masks = call(mask_kernel, f32(2 * HALO, NB, SUBLANES, BS), [lists], [], flops=10**8)
    operator = call(
        operator_kernel,
        (bf16(ROWS, ROWS),) * 6,
        [block_cols],
        [blocks],
        [pltpu.VMEM((EXT * BS, ROWS), jnp.float32)],
        flops=10**9,
    )
    sends = call(start_kernel, (VECTOR, HALO_PART, HALO_PART), [], [masks, parts])
    square = f32(BS, BS)
    vectors, earlier, sums = [sends[0]], [], []
    for power in range(COUNT - 1):
        row = f32(power + 1, SUBLANES, BS)
        partial, coarse, rest, high, low = call(
            round_kernel,
            (VECTOR, square, square, row, row),
            [],
            [sends[0], *operator[:3], *earlier],
            flops=10**9,
        )
        earlier += [coarse, rest]
        sums += [high, low]
        received = [passed(sends[1], 1), passed(sends[2], -1)]
        sends = call(
            step_kernel,
            (VECTOR, HALO_PART, HALO_PART),
            [],
            [masks, partial, *received, *operator[3:]],
        )
        vectors.append(sends[0])
    packed = f32(PART, 2 * SUM_ROWS, BS)
    sums = call(pack_kernel, packed, [], [vectors[-1], *earlier, *sums])
    strided = [[i + PART * j for j in range(subs // PART)] for i in range(PART)]
    runs = [[PART * i + j for j in range(PART)] for i in range(subs // PART)]
    sums = call(sum_kernel, packed, [], [exchanged_over(strided)(sums)])
    own, other = call(
        all_cycles_kernel,
        (f32(2 * COLS, BS), f32(2 * COLS + SUBLANES, BS)),
        [fold.reshape(1)],
        [exchanged_over(runs)(sums), *vectors],
    )
    arrived = lax.ppermute(other, "fold", [(0, 1), (1, 0), (2, 3), (3, 2)])
    correction, residual, bad = call(
        join_kernel,
        (f32(2 * COLS, BS), f32(2 * COLS, BS), jax.ShapeDtypeStruct((1,), jnp.int32)),
        [core],
        [own, other, arrived],
        out_specs=(VMEM, VMEM, SMEM),
    )
    correction, residual = lax.cond(
        bad[0] > 0,
        lambda correction, residual, *rest: cycle_by_cycle(*rest),
        lambda correction, residual, *rest: (correction, residual),
        correction,
        residual,
        right_side,
        blocks,
        block_cols,
        lists,
        fold,
    )
    return (correction.T, residual.T)


def solution(mesh):
    placed = (
        P(("sub", "fold"), None),
        P("sub", None, None, None),
        P("sub", None),
        P("sub", None, None),
    )
    return jax.shard_map(
        on_device,
        mesh=mesh,
        in_specs=placed,
        out_specs=(P(("sub", "fold"), None), P(("sub", "fold"), None)),
        check_vma=False,
    )
```

profile of v0, /device:TPU:1, one launch (start us, length us, event | category | flops | bytes accessed | tf_op | source)
XLA Modules:
  0.0 154.7 jit_solution(7292048453184522169)
XLA Ops:
  0.6 1.5 pad_maximum_fusion.1
  2.1 6.5 %all-to-all-start = ((f32[4,32,128]{2,1,0:T(8,128)}), f32[4,32,128]{2,1,0:T(8,128)S(1)}, u32[]{:S(2)}, u32[]{:S(2)}) async-start(f32[4,32,128]{2,1,0:T(8,128)} %pad_maximum_fusion.1), calls=%async_computation | async-start | bytes 131072 | tf_op jit(solution)/shard_map/all_to_all | solution.py:472
  8.6 3.0 %shard_map.61 = (bf16[512,512]{1,0:T(8,128)(2,1)S(1)}, bf16[512,512]{1,0:T(8,128)(2,1)S(1)}, bf16[512,512]{1,0:T(8,128)(2,1)S(1)}, bf16[512,512]{1,0:T(8,128)(2,...) custom-call(s32[4,7]{1,0:T(4,128)} %cols.1, f32[4,7,128,128]{3,2,1,0:T(8,128)} %blocks.1), custom_call_target="tpu_custom_call" | custom-call | flops 1000000000 | bytes 1048576 | tf_op jit(solution)/shard_map/pallas_call | solution.py:404
  12.2 1.2 all-to-all-done.parts
  13.5 7.4 %collective-permute-start.3 = (f32[32,256]{1,0:T(8,128)S(1)}, f32[32,256]{1,0:T(8,128)S(1)}, u32[]{:S(2)}, u32[]{:S(2)}) collective-permute-start(f32[32,256]{1,0:T(8,128)S(1)} %get-tuple-element.484), channel_id=1, source_target_pairs={{0,252},{4,0},{8,4},{12,8},{16,12},{20,16},{24,20},{28,24},{32,28}... | collective-permute-start | bytes 98312 | tf_op jit(solution)/shard_map/ppermute | solution.py:424
  21.3 0.8 collective-permute-done.2.from_previous
  22.6 5.8 %collective-permute-start.5 = (f32[32,256]{1,0:T(8,128)S(1)}, f32[32,256]{1,0:T(8,128)S(1)}, u32[]{:S(2)}, u32[]{:S(2)}) collective-permute-start(f32[32,256]{1,0:T(8,128)S(1)} %get-tuple-element.493), channel_id=1, source_target_pairs={{0,252},{4,0},{8,4},{12,8},{16,12},{20,16},{24,20},{28,24},{32,28}... | collective-permute-start | bytes 98312 | tf_op jit(solution)/shard_map/ppermute | solution.py:424
  28.8 0.9 collective-permute-done.4.from_previous
  30.1 5.8 %collective-permute-start.7 = (f32[32,256]{1,0:T(8,128)S(1)}, f32[32,256]{1,0:T(8,128)S(1)}, u32[]{:S(2)}, u32[]{:S(2)}) collective-permute-start(f32[32,256]{1,0:T(8,128)S(1)} %get-tuple-element.499), channel_id=1, source_target_pairs={{0,252},{4,0},{8,4},{12,8},{16,12},{20,16},{24,20},{28,24},{32,28}... | collective-permute-start | bytes 98312 | tf_op jit(solution)/shard_map/ppermute | solution.py:424
  36.3 1.0 collective-permute-done.6.from_previous
  37.8 5.7 %collective-permute-start.9 = (f32[32,256]{1,0:T(8,128)S(1)}, f32[32,256]{1,0:T(8,128)S(1)}, u32[]{:S(2)}, u32[]{:S(2)}) collective-permute-start(f32[32,256]{1,0:T(8,128)S(1)} %get-tuple-element.505), channel_id=1, source_target_pairs={{0,252},{4,0},{8,4},{12,8},{16,12},{20,16},{24,20},{28,24},{32,28}... | collective-permute-start | bytes 98312 | tf_op jit(solution)/shard_map/ppermute | solution.py:424
  43.9 1.0 collective-permute-done.8.from_previous
  45.3 5.7 %collective-permute-start.11 = (f32[32,256]{1,0:T(8,128)S(1)}, f32[32,256]{1,0:T(8,128)S(1)}, u32[]{:S(2)}, u32[]{:S(2)}) collective-permute-start(f32[32,256]{1,0:T(8,128)S(1)} %get-tuple-element.511), channel_id=1, source_target_pairs={{0,252},{4,0},{8,4},{12,8},{16,12},{20,16},{24,20},{28,24},{32,28}... | collective-permute-start | bytes 98312 | tf_op jit(solution)/shard_map/ppermute | solution.py:424
  51.4 1.0 collective-permute-done.10.from_previous
  52.9 5.9 %collective-permute-start.13 = (f32[32,256]{1,0:T(8,128)S(1)}, f32[32,256]{1,0:T(8,128)S(1)}, u32[]{:S(2)}, u32[]{:S(2)}) collective-permute-start(f32[32,256]{1,0:T(8,128)S(1)} %get-tuple-element.517), channel_id=1, source_target_pairs={{0,252},{4,0},{8,4},{12,8},{16,12},{20,16},{24,20},{28,24},{32,28}... | collective-permute-start | bytes 98312 | tf_op jit(solution)/shard_map/ppermute | solution.py:424
  59.1 0.8 collective-permute-done.12.from_previous
  60.4 5.8 %collective-permute-start.15 = (f32[32,256]{1,0:T(8,128)S(1)}, f32[32,256]{1,0:T(8,128)S(1)}, u32[]{:S(2)}, u32[]{:S(2)}) collective-permute-start(f32[32,256]{1,0:T(8,128)S(1)} %get-tuple-element.523), channel_id=1, source_target_pairs={{0,252},{4,0},{8,4},{12,8},{16,12},{20,16},{24,20},{28,24},{32,28}... | collective-permute-start | bytes 98312 | tf_op jit(solution)/shard_map/ppermute | solution.py:424
  66.7 0.9 collective-permute-done.14.from_previous
  68.1 5.7 %collective-permute-start.17 = (f32[32,256]{1,0:T(8,128)S(1)}, f32[32,256]{1,0:T(8,128)S(1)}, u32[]{:S(2)}, u32[]{:S(2)}) collective-permute-start(f32[32,256]{1,0:T(8,128)S(1)} %get-tuple-element.529), channel_id=1, source_target_pairs={{0,252},{4,0},{8,4},{12,8},{16,12},{20,16},{24,20},{28,24},{32,28}... | collective-permute-start | bytes 98312 | tf_op jit(solution)/shard_map/ppermute | solution.py:424
  74.2 0.9 collective-permute-done.16.from_previous
  75.6 5.8 %collective-permute-start.19 = (f32[32,256]{1,0:T(8,128)S(1)}, f32[32,256]{1,0:T(8,128)S(1)}, u32[]{:S(2)}, u32[]{:S(2)}) collective-permute-start(f32[32,256]{1,0:T(8,128)S(1)} %get-tuple-element.535), channel_id=1, source_target_pairs={{0,252},{4,0},{8,4},{12,8},{16,12},{20,16},{24,20},{28,24},{32,28}... | collective-permute-start | bytes 98312 | tf_op jit(solution)/shard_map/ppermute | solution.py:424
  81.7 0.8 collective-permute-done.18.from_previous
  83.0 5.8 %collective-permute-start.21 = (f32[32,256]{1,0:T(8,128)S(1)}, f32[32,256]{1,0:T(8,128)S(1)}, u32[]{:S(2)}, u32[]{:S(2)}) collective-permute-start(f32[32,256]{1,0:T(8,128)S(1)} %get-tuple-element.541), channel_id=1, source_target_pairs={{0,252},{4,0},{8,4},{12,8},{16,12},{20,16},{24,20},{28,24},{32,28}... | collective-permute-start | bytes 98312 | tf_op jit(solution)/shard_map/ppermute | solution.py:424
  90.6 5.8 %collective-permute-start.23 = (f32[32,256]{1,0:T(8,128)S(1)}, f32[32,256]{1,0:T(8,128)S(1)}, u32[]{:S(2)}, u32[]{:S(2)}) collective-permute-start(f32[32,256]{1,0:T(8,128)S(1)} %get-tuple-element.547), channel_id=1, source_target_pairs={{0,252},{4,0},{8,4},{12,8},{16,12},{20,16},{24,20},{28,24},{32,28}... | collective-permute-start | bytes 98312 | tf_op jit(solution)/shard_map/ppermute | solution.py:424
  98.1 6.1 %collective-permute-start.25 = (f32[32,256]{1,0:T(8,128)S(1)}, f32[32,256]{1,0:T(8,128)S(1)}, u32[]{:S(2)}, u32[]{:S(2)}) collective-permute-start(f32[32,256]{1,0:T(8,128)S(1)} %get-tuple-element.553), channel_id=1, source_target_pairs={{0,252},{4,0},{8,4},{12,8},{16,12},{20,16},{24,20},{28,24},{32,28}... | collective-permute-start | bytes 98312 | tf_op jit(solution)/shard_map/ppermute | solution.py:424
  105.2 1.0 shard_map.85
  107.0 14.5 %all_to_all.15.parts = f32[8,48,128]{2,1,0:T(8,128)S(1)} all-to-all(f32[8,48,128]{2,1,0:T(8,128)S(1)} %shard_map.86), channel_id=1, replica_groups={{0,32,64,96,128,160,192,224},{4,36,68,100,132,164,196,228},{8,40,72,104..., dimensions={0} | all-to-all | bytes 393216 | tf_op jit(solution)/shard_map/all_to_all | solution.py:417
  122.2 4.6 %all-to-all-start.2 = ((f32[8,48,128]{2,1,0:T(8,128)}), f32[8,48,128]{2,1,0:T(8,128)S(1)}, u32[]{:S(2)}, u32[]{:S(2)}) async-start(f32[8,48,128]{2,1,0:T(8,128)} %shard_map.87), calls=%async_computation.2 | async-start | bytes 393216 | tf_op jit(solution)/shard_map/all_to_all | solution.py:417
  126.8 5.8 %all-to-all-done.2.parts = f32[8,48,128]{2,1,0:T(8,128)S(1)} async-done(((f32[8,48,128]{2,1,0:T(8,128)}), f32[8,48,128]{2,1,0:T(8,128)S(1)}, u32[]{:S(2)}, u32[]{:S(2)}) %all-to-all-start.2) | async-done | bytes 196640 | tf_op jit(solution)/shard_map/all_to_all | solution.py:417
  132.6 1.2 shard_map.88
  133.8 18.1 %collective-permute-start.26 = (f32[72,128]{1,0:T(8,128)S(1)}, f32[72,128]{1,0:T(8,128)S(1)}, u32[]{:S(2)}, u32[]{:S(2)}) collective-permute-start(f32[72,128]{1,0:T(8,128)S(1)} %get-tuple-element.582.other), channel_id=1, source_target_pairs={{0,1},{1,0},{2,3},{3,2},{4,5},{5,4},{6,7},{7,6},{8,9},{9,8},{10,11... | collective-permute-start | bytes 110600 | tf_op jit(solution)/shard_map/ppermute | solution.py:515
  151.9 0.9 collective-permute-done.26.arrived
  (70 shorter events, 15.3 us)
Async XLA Ops:
  2.1 11.3 %all-to-all-start = ((f32[4,32,128]{2,1,0:T(8,128)}), f32[4,32,128]{2,1,0:T(8,128)S(1)}, u32[]{:S(2)}, u32[]{:S(2)}) async-start(f32[4,32,128]{2,1,0:T(8,128)} %pad_maximum_fusion.1), calls=%async_computation | async-start | bytes 131072 | tf_op jit(solution)/shard_map/all_to_all | solution.py:472
  8.6 3.0 %copy-start.2 = (s32[1,2,2]{2,1,0:T(2,128)S(1)}, s32[1,2,2]{2,1,0:T(2,128)}, u32[]{:S(2)}) copy-start(s32[1,2,2]{2,1,0:T(2,128)} %param.17) | copy-start | bytes 52
  11.6 31.9 %copy-start = (bf16[512,512]{1,0:T(8,128)(2,1)}, bf16[512,512]{1,0:T(8,128)(2,1)S(1)}, u32[]{:S(2)}) copy-start(bf16[512,512]{1,0:T(8,128)(2,1)S(1)} %get-tuple-element.481.refs_3_) | copy-start | bytes 1572868
  13.4 8.7 %collective-permute-start.2 = (f32[32,256]{1,0:T(8,128)S(1)}, f32[32,256]{1,0:T(8,128)S(1)}, u32[]{:S(2)}, u32[]{:S(2)}) collective-permute-start(f32[32,256]{1,0:T(8,128)S(1)} %get-tuple-element.483), channel_id=1, source_target_pairs={{0,4},{4,8},{8,12},{12,16},{16,20},{20,24},{24,28},{28,32},{32,36}... | collective-permute-start | bytes 98312 | tf_op jit(solution)/shard_map/ppermute | solution.py:424
  13.5 8.7 %collective-permute-start.3 = (f32[32,256]{1,0:T(8,128)S(1)}, f32[32,256]{1,0:T(8,128)S(1)}, u32[]{:S(2)}, u32[]{:S(2)}) collective-permute-start(f32[32,256]{1,0:T(8,128)S(1)} %get-tuple-element.484), channel_id=1, source_target_pairs={{0,252},{4,0},{8,4},{12,8},{16,12},{20,16},{24,20},{28,24},{32,28}... | collective-permute-start | bytes 98312 | tf_op jit(solution)/shard_map/ppermute | solution.py:424
  22.5 7.2 %collective-permute-start.4 = (f32[32,256]{1,0:T(8,128)S(1)}, f32[32,256]{1,0:T(8,128)S(1)}, u32[]{:S(2)}, u32[]{:S(2)}) collective-permute-start(f32[32,256]{1,0:T(8,128)S(1)} %get-tuple-element.492), channel_id=1, source_target_pairs={{0,4},{4,8},{8,12},{12,16},{16,20},{20,24},{24,28},{28,32},{32,36}... | collective-permute-start | bytes 98312 | tf_op jit(solution)/shard_map/ppermute | solution.py:424
  22.6 7.1 %collective-permute-start.5 = (f32[32,256]{1,0:T(8,128)S(1)}, f32[32,256]{1,0:T(8,128)S(1)}, u32[]{:S(2)}, u32[]{:S(2)}) collective-permute-start(f32[32,256]{1,0:T(8,128)S(1)} %get-tuple-element.493), channel_id=1, source_target_pairs={{0,252},{4,0},{8,4},{12,8},{16,12},{20,16},{24,20},{28,24},{32,28}... | collective-permute-start | bytes 98312 | tf_op jit(solution)/shard_map/ppermute | solution.py:424
  30.0 7.3 %collective-permute-start.6 = (f32[32,256]{1,0:T(8,128)S(1)}, f32[32,256]{1,0:T(8,128)S(1)}, u32[]{:S(2)}, u32[]{:S(2)}) collective-permute-start(f32[32,256]{1,0:T(8,128)S(1)} %get-tuple-element.498), channel_id=1, source_target_pairs={{0,4},{4,8},{8,12},{12,16},{16,20},{20,24},{24,28},{28,32},{32,36}... | collective-permute-start | bytes 98312 | tf_op jit(solution)/shard_map/ppermute | solution.py:424
  30.1 7.2 %collective-permute-start.7 = (f32[32,256]{1,0:T(8,128)S(1)}, f32[32,256]{1,0:T(8,128)S(1)}, u32[]{:S(2)}, u32[]{:S(2)}) collective-permute-start(f32[32,256]{1,0:T(8,128)S(1)} %get-tuple-element.499), channel_id=1, source_target_pairs={{0,252},{4,0},{8,4},{12,8},{16,12},{20,16},{24,20},{28,24},{32,28}... | collective-permute-start | bytes 98312 | tf_op jit(solution)/shard_map/ppermute | solution.py:424
  37.7 7.2 %collective-permute-start.8 = (f32[32,256]{1,0:T(8,128)S(1)}, f32[32,256]{1,0:T(8,128)S(1)}, u32[]{:S(2)}, u32[]{:S(2)}) collective-permute-start(f32[32,256]{1,0:T(8,128)S(1)} %get-tuple-element.504), channel_id=1, source_target_pairs={{0,4},{4,8},{8,12},{12,16},{16,20},{20,24},{24,28},{28,32},{32,36}... | collective-permute-start | bytes 98312 | tf_op jit(solution)/shard_map/ppermute | solution.py:424
  37.8 7.1 %collective-permute-start.9 = (f32[32,256]{1,0:T(8,128)S(1)}, f32[32,256]{1,0:T(8,128)S(1)}, u32[]{:S(2)}, u32[]{:S(2)}) collective-permute-start(f32[32,256]{1,0:T(8,128)S(1)} %get-tuple-element.505), channel_id=1, source_target_pairs={{0,252},{4,0},{8,4},{12,8},{16,12},{20,16},{24,20},{28,24},{32,28}... | collective-permute-start | bytes 98312 | tf_op jit(solution)/shard_map/ppermute | solution.py:424
  43.9 7.2 %copy-start.1 = (bf16[512,512]{1,0:T(8,128)(2,1)S(1)}, bf16[512,512]{1,0:T(8,128)(2,1)}, u32[]{:S(2)}) copy-start(bf16[512,512]{1,0:T(8,128)(2,1)} %copy-done) | copy-start | bytes 1572868
  45.2 7.2 %collective-permute-start.10 = (f32[32,256]{1,0:T(8,128)S(1)}, f32[32,256]{1,0:T(8,128)S(1)}, u32[]{:S(2)}, u32[]{:S(2)}) collective-permute-start(f32[32,256]{1,0:T(8,128)S(1)} %get-tuple-element.510), channel_id=1, source_target_pairs={{0,4},{4,8},{8,12},{12,16},{16,20},{20,24},{24,28},{28,32},{32,36}... | collective-permute-start | bytes 98312 | tf_op jit(solution)/shard_map/ppermute | solution.py:424
  45.3 7.1 %collective-permute-start.11 = (f32[32,256]{1,0:T(8,128)S(1)}, f32[32,256]{1,0:T(8,128)S(1)}, u32[]{:S(2)}, u32[]{:S(2)}) collective-permute-start(f32[32,256]{1,0:T(8,128)S(1)} %get-tuple-element.511), channel_id=1, source_target_pairs={{0,252},{4,0},{8,4},{12,8},{16,12},{20,16},{24,20},{28,24},{32,28}... | collective-permute-start | bytes 98312 | tf_op jit(solution)/shard_map/ppermute | solution.py:424
  52.8 7.2 %collective-permute-start.12 = (f32[32,256]{1,0:T(8,128)S(1)}, f32[32,256]{1,0:T(8,128)S(1)}, u32[]{:S(2)}, u32[]{:S(2)}) collective-permute-start(f32[32,256]{1,0:T(8,128)S(1)} %get-tuple-element.516), channel_id=1, source_target_pairs={{0,4},{4,8},{8,12},{12,16},{16,20},{20,24},{24,28},{28,32},{32,36}... | collective-permute-start | bytes 98312 | tf_op jit(solution)/shard_map/ppermute | solution.py:424
  52.9 7.1 %collective-permute-start.13 = (f32[32,256]{1,0:T(8,128)S(1)}, f32[32,256]{1,0:T(8,128)S(1)}, u32[]{:S(2)}, u32[]{:S(2)}) collective-permute-start(f32[32,256]{1,0:T(8,128)S(1)} %get-tuple-element.517), channel_id=1, source_target_pairs={{0,252},{4,0},{8,4},{12,8},{16,12},{20,16},{24,20},{28,24},{32,28}... | collective-permute-start | bytes 98312 | tf_op jit(solution)/shard_map/ppermute | solution.py:424
  60.3 7.3 %collective-permute-start.14 = (f32[32,256]{1,0:T(8,128)S(1)}, f32[32,256]{1,0:T(8,128)S(1)}, u32[]{:S(2)}, u32[]{:S(2)}) collective-permute-start(f32[32,256]{1,0:T(8,128)S(1)} %get-tuple-element.522), channel_id=1, source_target_pairs={{0,4},{4,8},{8,12},{12,16},{16,20},{20,24},{24,28},{28,32},{32,36}... | collective-permute-start | bytes 98312 | tf_op jit(solution)/shard_map/ppermute | solution.py:424
  60.4 7.2 %collective-permute-start.15 = (f32[32,256]{1,0:T(8,128)S(1)}, f32[32,256]{1,0:T(8,128)S(1)}, u32[]{:S(2)}, u32[]{:S(2)}) collective-permute-start(f32[32,256]{1,0:T(8,128)S(1)} %get-tuple-element.523), channel_id=1, source_target_pairs={{0,252},{4,0},{8,4},{12,8},{16,12},{20,16},{24,20},{28,24},{32,28}... | collective-permute-start | bytes 98312 | tf_op jit(solution)/shard_map/ppermute | solution.py:424
  68.0 7.1 %collective-permute-start.16 = (f32[32,256]{1,0:T(8,128)S(1)}, f32[32,256]{1,0:T(8,128)S(1)}, u32[]{:S(2)}, u32[]{:S(2)}) collective-permute-start(f32[32,256]{1,0:T(8,128)S(1)} %get-tuple-element.528), channel_id=1, source_target_pairs={{0,4},{4,8},{8,12},{12,16},{16,20},{20,24},{24,28},{28,32},{32,36}... | collective-permute-start | bytes 98312 | tf_op jit(solution)/shard_map/ppermute | solution.py:424
  68.1 7.0 %collective-permute-start.17 = (f32[32,256]{1,0:T(8,128)S(1)}, f32[32,256]{1,0:T(8,128)S(1)}, u32[]{:S(2)}, u32[]{:S(2)}) collective-permute-start(f32[32,256]{1,0:T(8,128)S(1)} %get-tuple-element.529), channel_id=1, source_target_pairs={{0,252},{4,0},{8,4},{12,8},{16,12},{20,16},{24,20},{28,24},{32,28}... | collective-permute-start | bytes 98312 | tf_op jit(solution)/shard_map/ppermute | solution.py:424
  75.5 7.1 %collective-permute-start.18 = (f32[32,256]{1,0:T(8,128)S(1)}, f32[32,256]{1,0:T(8,128)S(1)}, u32[]{:S(2)}, u32[]{:S(2)}) collective-permute-start(f32[32,256]{1,0:T(8,128)S(1)} %get-tuple-element.534), channel_id=1, source_target_pairs={{0,4},{4,8},{8,12},{12,16},{16,20},{20,24},{24,28},{28,32},{32,36}... | collective-permute-start | bytes 98312 | tf_op jit(solution)/shard_map/ppermute | solution.py:424
  75.6 7.0 %collective-permute-start.19 = (f32[32,256]{1,0:T(8,128)S(1)}, f32[32,256]{1,0:T(8,128)S(1)}, u32[]{:S(2)}, u32[]{:S(2)}) collective-permute-start(f32[32,256]{1,0:T(8,128)S(1)} %get-tuple-element.535), channel_id=1, source_target_pairs={{0,252},{4,0},{8,4},{12,8},{16,12},{20,16},{24,20},{28,24},{32,28}... | collective-permute-start | bytes 98312 | tf_op jit(solution)/shard_map/ppermute | solution.py:424
  83.0 7.2 %collective-permute-start.20 = (f32[32,256]{1,0:T(8,128)S(1)}, f32[32,256]{1,0:T(8,128)S(1)}, u32[]{:S(2)}, u32[]{:S(2)}) collective-permute-start(f32[32,256]{1,0:T(8,128)S(1)} %get-tuple-element.540), channel_id=1, source_target_pairs={{0,4},{4,8},{8,12},{12,16},{16,20},{20,24},{24,28},{28,32},{32,36}... | collective-permute-start | bytes 98312 | tf_op jit(solution)/shard_map/ppermute | solution.py:424
  83.0 7.1 %collective-permute-start.21 = (f32[32,256]{1,0:T(8,128)S(1)}, f32[32,256]{1,0:T(8,128)S(1)}, u32[]{:S(2)}, u32[]{:S(2)}) collective-permute-start(f32[32,256]{1,0:T(8,128)S(1)} %get-tuple-element.541), channel_id=1, source_target_pairs={{0,252},{4,0},{8,4},{12,8},{16,12},{20,16},{24,20},{28,24},{32,28}... | collective-permute-start | bytes 98312 | tf_op jit(solution)/shard_map/ppermute | solution.py:424
  90.5 7.1 %collective-permute-start.22 = (f32[32,256]{1,0:T(8,128)S(1)}, f32[32,256]{1,0:T(8,128)S(1)}, u32[]{:S(2)}, u32[]{:S(2)}) collective-permute-start(f32[32,256]{1,0:T(8,128)S(1)} %get-tuple-element.546), channel_id=1, source_target_pairs={{0,4},{4,8},{8,12},{12,16},{16,20},{20,24},{24,28},{28,32},{32,36}... | collective-permute-start | bytes 98312 | tf_op jit(solution)/shard_map/ppermute | solution.py:424
  90.6 7.0 %collective-permute-start.23 = (f32[32,256]{1,0:T(8,128)S(1)}, f32[32,256]{1,0:T(8,128)S(1)}, u32[]{:S(2)}, u32[]{:S(2)}) collective-permute-start(f32[32,256]{1,0:T(8,128)S(1)} %get-tuple-element.547), channel_id=1, source_target_pairs={{0,252},{4,0},{8,4},{12,8},{16,12},{20,16},{24,20},{28,24},{32,28}... | collective-permute-start | bytes 98312 | tf_op jit(solution)/shard_map/ppermute | solution.py:424
  98.0 7.1 %collective-permute-start.24 = (f32[32,256]{1,0:T(8,128)S(1)}, f32[32,256]{1,0:T(8,128)S(1)}, u32[]{:S(2)}, u32[]{:S(2)}) collective-permute-start(f32[32,256]{1,0:T(8,128)S(1)} %get-tuple-element.552), channel_id=1, source_target_pairs={{0,4},{4,8},{8,12},{12,16},{16,20},{20,24},{24,28},{28,32},{32,36}... | collective-permute-start | bytes 98312 | tf_op jit(solution)/shard_map/ppermute | solution.py:424
  98.1 7.1 %collective-permute-start.25 = (f32[32,256]{1,0:T(8,128)S(1)}, f32[32,256]{1,0:T(8,128)S(1)}, u32[]{:S(2)}, u32[]{:S(2)}) collective-permute-start(f32[32,256]{1,0:T(8,128)S(1)} %get-tuple-element.553), channel_id=1, source_target_pairs={{0,252},{4,0},{8,4},{12,8},{16,12},{20,16},{24,20},{28,24},{32,28}... | collective-permute-start | bytes 98312 | tf_op jit(solution)/shard_map/ppermute | solution.py:424
  107.0 47.1 %copy-start.3 = (f32[128,64]{0,1:T(8,128)S(1)}, f32[128,64]{0,1:T(8,128)}, u32[]{:S(2)}) copy-start(f32[128,64]{0,1:T(8,128)} %param.14) | copy-start | bytes 98308
  107.0 47.1 %copy-start.4 = (s32[4,7]{1,0:T(4,128)S(1)}, s32[4,7]{1,0:T(4,128)}, u32[]{:S(2)}) copy-start(s32[4,7]{1,0:T(4,128)} %cols.1) | copy-start | bytes 340
  122.2 10.4 %all-to-all-start.2 = ((f32[8,48,128]{2,1,0:T(8,128)}), f32[8,48,128]{2,1,0:T(8,128)S(1)}, u32[]{:S(2)}, u32[]{:S(2)}) async-start(f32[8,48,128]{2,1,0:T(8,128)} %shard_map.87), calls=%async_computation.2 | async-start | bytes 393216 | tf_op jit(solution)/shard_map/all_to_all | solution.py:417
  133.8 19.0 %collective-permute-start.26 = (f32[72,128]{1,0:T(8,128)S(1)}, f32[72,128]{1,0:T(8,128)S(1)}, u32[]{:S(2)}, u32[]{:S(2)}) collective-permute-start(f32[72,128]{1,0:T(8,128)S(1)} %get-tuple-element.582.other), channel_id=1, source_target_pairs={{0,1},{1,0},{2,3},{3,2},{4,5},{5,4},{6,7},{7,6},{8,9},{9,8},{10,11... | collective-permute-start | bytes 110600 | tf_op jit(solution)/shard_map/ppermute | solution.py:515
  (2 other events, 1.2 us)
where the time goes:
time: 155 us
  starting transfers between devices  102 us (66%)
  waiting for transfers between devices  18.3 us (12%)
  Pallas kernels  16.5 us (11%)
  blocking collectives  14.5 us (9%)
    ppermute x24, starting transfers between devices, passed(): lax.ppermute(value, 'sub', [(i, (i + by) % subs) for i in range(subs)])  72.5 us
    ppermute x1, starting transfers between devices, on_device(): arrived = lax.ppermute(other, 'fold', [(0, 1), (1, 0), (2, 3), (3, 2)])  18.1 us
    pallas_call x31, Pallas kernels, call(): pl.pallas_call(kernel, out_shape=out_shape, in_specs=[SMEM] * len(smem) +...  16.5 us
    all_to_all x1, blocking collectives, exchanged(): return lax.all_to_all(value, 'sub', 0, 0, axis_index_groups=groups)  14.5 us
    ppermute x24, waiting for transfers between devices, passed(): lax.ppermute(value, 'sub', [(i, (i + by) % subs) for i in range(subs)])  10.5 us
    all_to_all x1, starting transfers between devices, on_device(): lax.all_to_all(jnp.concatenate([halves_of_columns] * 2, 0), 'fold', 0, 0)  6.49 us
    all_to_all x1, waiting for transfers between devices, exchanged(): return lax.all_to_all(value, 'sub', 0, 0, axis_index_groups=groups)  5.81 us
    all_to_all x1, starting transfers between devices, exchanged(): return lax.all_to_all(value, 'sub', 0, 0, axis_index_groups=groups)  4.63 us
  transfers between devices with their start and end apart: 27, of which 15 were waited for; matrix products, arithmetic and copies ran while one was open for 0% of the time, Pallas kernels for 5%

commit v1 on v0

--- a/solution.py
+++ b/solution.py
@@ -62,20 +62,15 @@
     return first[:COLS] + (first[COLS : 2 * COLS] + second[:COLS] + small)
 
 
-def mask_kernel(lists, masks):
-    for side in range(2):
-        for slot in range(HALO):
-            for block in range(NB):
-                chosen = jnp.full((SUBLANES, BS), lists[side, slot], jnp.int32) == block
-                masks[side * HALO + slot, block] = jnp.where(chosen, 1.0, 0.0)
-
-
 def operator_kernel(cols, blocks, *refs):
     own, received, dense = refs[:3], refs[3:6], refs[6]
+    turn = HALO * (lax.axis_index("sub") % 2)
     dense[...] = jnp.zeros_like(dense)
     for row in range(NB):
         for slot in range(blocks.shape[1]):
-            start = pl.multiple_of(cols[row, slot] * BS, BS)
+            column = cols[row, slot]
+            swapped = NB + (column - NB + turn) % (2 * HALO)
+            start = pl.multiple_of(jnp.where(column < NB, column, swapped) * BS, BS)
             place = (pl.ds(start, BS), slice(row * BS, (row + 1) * BS))
             dense[place] = dense[place] + blocks[row, slot].T
     unit = (
@@ -93,10 +88,10 @@
                 target[start : start + BS, row * BS : (row + 1) * BS] = part
 
 
-def write_chosen(masks, vector, to_next, to_previous):
+def write_chosen(masks, vector, sends):
     repeats = vector.shape[0] // SUBLANES
-    for slot in range(HALO):
-        for side, target in ((0, to_next), (1, to_previous)):
+    for side, target in enumerate(sends):
+        for slot in range(HALO):
             total = None
             for block in range(NB):
                 mask = jnp.concatenate([masks[side * HALO + slot, block]] * repeats, 0)
@@ -105,18 +100,26 @@
             target[:, slot * BS : (slot + 1) * BS] = total
 
 
-def start_kernel(masks, parts, result, to_next, to_previous):
-    vector = jnp.concatenate([parts[block] for block in range(NB)], 1)
+def start_kernel(lists, gathered, masks, result, *sends):
+    parity = lax.axis_index("sub") % 2
+    first = pl.multiple_of(lax.axis_index("fold") % 2 * COLS, COLS)
+    for side in range(2):
+        for slot in range(HALO):
+            listed = lists[(side + parity + 1) % 2, slot]
+            for block in range(NB):
+                chosen = jnp.full((SUBLANES, BS), listed, jnp.int32) == block
+                masks[side * HALO + slot, block] = jnp.where(chosen, 1.0, 0.0)
+    vector = gathered[pl.ds(first, COLS), :]
     result[...] = vector
-    write_chosen(masks, vector, to_next, to_previous)
-
-
-def step_kernel(masks, partial, from_previous, from_next, *refs):
-    parts, (result, to_next, to_previous) = refs[:3], refs[3:]
-    received = jnp.concatenate([from_previous[...], from_next[...]], 1)
+    write_chosen(masks, vector, sends)
+
+
+def step_kernel(masks, partial, first, second, *refs):
+    parts, (result, *sends) = refs[:3], refs[3:]
+    received = jnp.concatenate([first[...], second[...]], 1)
     vector = partial[...] + product(received, *parts)
     result[...] = vector
-    write_chosen(masks, vector, to_next, to_previous)
+    write_chosen(masks, vector, sends)
 
 
 def small_solve(matrix, target):
@@ -315,7 +318,7 @@
     return result
 
 
-def all_cycles_kernel(fold, parts, *refs):
+def all_cycles_kernel(parts, *refs):
     vectors, own, other = refs[:COUNT], refs[COUNT], refs[COUNT + 1]
     high, low = summed(parts)
     rolled = [(high, low)]
@@ -376,7 +379,7 @@
             total = jnp.where(index == i, value, total)
         stacked.append(total)
     turned = jnp.concatenate(stacked, 0).T
-    place = fold[0]
+    place = lax.axis_index("fold")
     partner = place + 1 - 2 * (place % 2)
     for output in range(2):
         sums = [None, None]
@@ -391,11 +394,12 @@
         other[output * COLS : (output + 1) * COLS] = sums[1]
 
 
-def join_kernel(core, own, other, arrived, correction, residual, bad):
+def join_kernel(own, other, arrived, correction, residual, bad):
+    core = lax.axis_index("fold") % 2
     for output, target in enumerate((correction, residual)):
         place = slice(output * COLS, (output + 1) * COLS)
-        target[pl.ds(pl.multiple_of(core[0] * COLS, COLS), COLS)] = own[place]
-        target[pl.ds(pl.multiple_of((1 - core[0]) * COLS, COLS), COLS)] = arrived[place]
+        target[pl.ds(pl.multiple_of(core * COLS, COLS), COLS)] = own[place]
+        target[pl.ds(pl.multiple_of((1 - core) * COLS, COLS), COLS)] = arrived[place]
     worst = jnp.max(jnp.maximum(other[2 * COLS :], arrived[2 * COLS :]))
     bad[0] = (worst > 0.5).astype(jnp.int32)
 
@@ -419,6 +423,12 @@
     return exchanged
 
 
+def swapped(value, first):
+    subs = lax.axis_size("sub")
+    pairs = [(i, (i + 1) % subs) for i in range(first, subs, 2)]
+    return lax.ppermute(value, "sub", pairs + [(j, i) for i, j in pairs])
+
+
 def passed(value, by):
     subs = lax.axis_size("sub")
     return lax.ppermute(value, "sub", [(i, (i + by) % subs) for i in range(subs)])
@@ -428,7 +438,7 @@
 HALO_PART = f32(COLS, HALO * BS)
 
 
-def cycle_by_cycle(right_side, blocks, block_cols, lists, fold):
+def cycle_by_cycle(right_side, blocks, block_cols, lists):
     gathered = lax.all_gather(right_side, "fold", axis=0, tiled=True)
 
     def applied(vector):
@@ -459,6 +469,7 @@
         correction = correction + sum(weights[i] * basis[i] for i in range(STEPS))
         return correction, sum(left[i] * basis[i] for i in range(STEPS + 1))
 
+    fold = lax.axis_index("fold")
     results = lax.fori_loop(0, CYCLES, cycle, (jnp.zeros_like(gathered), gathered))
     return tuple(lax.dynamic_slice_in_dim(value, fold * BS, BS, 0).T for value in results)
 
@@ -466,11 +477,7 @@
 def on_device(right_side, blocks, block_cols, send_lists):
     subs = lax.axis_size("sub")
     lists = send_lists[0]
-    fold = lax.axis_index("fold").astype(jnp.int32)
-    core = (fold % 2).reshape(1)
-    halves_of_columns = right_side.T.reshape(2, COLS, BS)
-    parts = lax.all_to_all(jnp.concatenate([halves_of_columns] * 2, 0), "fold", 0, 0)
-    masks = call(mask_kernel, f32(2 * HALO, NB, SUBLANES, BS), [lists], [], flops=10**8)
+    gathered = lax.all_gather(right_side.T, "fold", axis=1, tiled=True)
     operator = call(
         operator_kernel,
         (bf16(ROWS, ROWS),) * 6,
@@ -479,7 +486,10 @@
         [pltpu.VMEM((EXT * BS, ROWS), jnp.float32)],
         flops=10**9,
     )
-    sends = call(start_kernel, (VECTOR, HALO_PART, HALO_PART), [], [masks, parts])
+    masks_shape = f32(2 * HALO, NB, SUBLANES, BS)
+    masks, *sends = call(
+        start_kernel, (masks_shape, VECTOR, HALO_PART, HALO_PART), [lists], [gathered]
+    )
     square = f32(BS, BS)
     vectors, earlier, sums = [sends[0]], [], []
     for power in range(COUNT - 1):
@@ -493,7 +503,7 @@
         )
         earlier += [coarse, rest]
         sums += [high, low]
-        received = [passed(sends[1], 1), passed(sends[2], -1)]
+        received = [swapped(sends[1], 1), swapped(sends[2], 0)]
         sends = call(
             step_kernel,
             (VECTOR, HALO_PART, HALO_PART),
@@ -509,14 +519,14 @@
     own, other = call(
         all_cycles_kernel,
         (f32(2 * COLS, BS), f32(2 * COLS + SUBLANES, BS)),
-        [fold.reshape(1)],
+        [],
         [exchanged_over(runs)(sums), *vectors],
     )
     arrived = lax.ppermute(other, "fold", [(0, 1), (1, 0), (2, 3), (3, 2)])
     correction, residual, bad = call(
         join_kernel,
         (f32(2 * COLS, BS), f32(2 * COLS, BS), jax.ShapeDtypeStruct((1,), jnp.int32)),
-        [core],
+        [],
         [own, other, arrived],
         out_specs=(VMEM, VMEM, SMEM),
     )
@@ -530,7 +540,6 @@
         blocks,
         block_cols,
         lists,
-        fold,
     )
     return (correction.T, residual.T)
 

time: 155 us -> 148 us (0.955)
  starting transfers between devices: 102 us -> 64.2 us
  waiting for transfers between devices: 18.3 us -> 35.2 us
  blocking collectives: 14.5 us -> 30.6 us
    ppermute x24, starting transfers between devices: 72.5 us -> 47.3 us  [swapped(): return lax.ppermute(value, 'sub', pairs + [(j, i) for i, j in pairs])]
    ppermute x24, waiting for transfers between devices: 10.5 us -> 34.4 us  [swapped(): return lax.ppermute(value, 'sub', pairs + [(j, i) for i, j in pairs])]
    all_to_all x2 -> x0, starting transfers between devices: 11.1 us -> none  [the longest x1 6.49 us: on_device(): lax.all_to_all(jnp.concatenate([halves_of_columns] * 2, 0), 'fold', 0, 0)]
    all_gather x0 -> x1, blocking collectives: none -> 10.2 us  [on_device(): gathered = lax.all_gather(right_side.T, 'fold', axis=1, tiled=True)]
    all_to_all x2 -> x0, waiting for transfers between devices: 6.98 us -> none  [the longest x1 5.81 us: exchanged(): return lax.all_to_all(value, 'sub', 0, 0, axis_index_groups=groups)]
    all_to_all x1 -> x2, blocking collectives: 14.5 us -> 20.3 us  [exchanged(): return lax.all_to_all(value, 'sub', 0, 0, axis_index_groups=groups)]
    pallas_call x31 -> x30, Pallas kernels: 16.5 us -> 16 us  [call(): pl.pallas_call(kernel, out_shape=out_shape, in_specs=[SMEM] * len(smem) +...]
  transfers between devices with their start and end apart: 27 -> 25, of which waited for: 15 -> 12; matrix products, arithmetic and copies ran while one was open for 0% -> 0% of each run, Pallas kernels for 5% -> 5%
where the time goes in v1:
time: 148 us
  starting transfers between devices  64.2 us (43%)
  waiting for transfers between devices  35.2 us (24%)
  blocking collectives  30.6 us (21%)
  Pallas kernels  16 us (11%)
  between operations  1.54 us (1%)
    ppermute x24, starting transfers between devices, swapped(): return lax.ppermute(value, 'sub', pairs + [(j, i) for i, j in pairs])  47.3 us
    ppermute x24, waiting for transfers between devices, swapped(): return lax.ppermute(value, 'sub', pairs + [(j, i) for i, j in pairs])  34.4 us
    all_to_all x2, blocking collectives, exchanged(): return lax.all_to_all(value, 'sub', 0, 0, axis_index_groups=groups)  20.3 us
    ppermute x1, starting transfers between devices, on_device(): arrived = lax.ppermute(other, 'fold', [(0, 1), (1, 0), (2, 3), (3, 2)])  16.9 us
    pallas_call x30, Pallas kernels, call(): pl.pallas_call(kernel, out_shape=out_shape, in_specs=[SMEM] * len(smem) +...  16 us
    all_gather x1, blocking collectives, on_device(): gathered = lax.all_gather(right_side.T, 'fold', axis=1, tiled=True)  10.2 us
  transfers between devices with their start and end apart: 25, of which 12 were waited for; matrix products, arithmetic and copies ran while one was open for 0% of the time, Pallas kernels for 5%

profile of v1, /device:TPU:1, one launch (start us, length us, event | category | flops | bytes accessed | tf_op | source)
XLA Modules:
  0.0 148.2 jit_solution(17672450755084095834)
XLA Ops:
  0.6 10.2 %all_gather.6.gathered = f32[64,512]{1,0:T(8,128)S(1)} all-gather(f32[64,128]{1,0:T(8,128)} %bitcast.227), channel_id=1, replica_groups=mesh['sub'=64,'fold'=4] {'fold'}, dimensions={1}, use_global_device_ids=true | all-gather | bytes 163840 | tf_op jit(solution)/shard_map/all_gather | solution.py:480
  11.6 7.3 %collective-permute-start.2 = (f32[32,256]{1,0:T(8,128)S(1)}, f32[32,256]{1,0:T(8,128)S(1)}, u32[]{:S(2)}, u32[]{:S(2)}) collective-permute-start(f32[32,256]{1,0:T(8,128)S(1)} %get-tuple-element.482), channel_id=1, source_target_pairs={{4,8},{12,16},{20,24},{28,32},{36,40},{44,48},{52,56},{60,64},{68,... | collective-permute-start | bytes 98312 | tf_op jit(solution)/shard_map/ppermute | solution.py:429
  18.9 3.0 %shard_map.60 = (bf16[512,512]{1,0:T(8,128)(2,1)S(1)}, bf16[512,512]{1,0:T(8,128)(2,1)S(1)}, bf16[512,512]{1,0:T(8,128)(2,1)S(1)}, bf16[512,512]{1,0:T(8,128)(2,...) custom-call(s32[4,7]{1,0:T(4,128)} %cols.1, f32[4,7,128,128]{3,2,1,0:T(8,128)} %blocks.1), custom_call_target="tpu_custom_call" | custom-call | flops 1000000000 | bytes 1048576 | tf_op jit(solution)/shard_map/pallas_call | solution.py:408
  22.7 3.7 %collective-permute-start.4 = (f32[32,256]{1,0:T(8,128)S(1)}, f32[32,256]{1,0:T(8,128)S(1)}, u32[]{:S(2)}, u32[]{:S(2)}) collective-permute-start(f32[32,256]{1,0:T(8,128)S(1)} %get-tuple-element.491), channel_id=1, source_target_pairs={{4,8},{12,16},{20,24},{28,32},{36,40},{44,48},{52,56},{60,64},{68,... | collective-permute-start | bytes 98312 | tf_op jit(solution)/shard_map/ppermute | solution.py:429
  26.7 3.2 %collective-permute-done.4.first = f32[32,256]{1,0:T(8,128)S(1)} collective-permute-done((f32[32,256]{1,0:T(8,128)S(1)}, f32[32,256]{1,0:T(8,128)S(1)}, u32[]{:S(2)}, u32[]{:S(2)}) %collective-permute-start.4) | collective-permute-done | bytes 32800 | tf_op jit(solution)/shard_map/ppermute | solution.py:429
  30.2 3.6 %collective-permute-start.6 = (f32[32,256]{1,0:T(8,128)S(1)}, f32[32,256]{1,0:T(8,128)S(1)}, u32[]{:S(2)}, u32[]{:S(2)}) collective-permute-start(f32[32,256]{1,0:T(8,128)S(1)} %get-tuple-element.497), channel_id=1, source_target_pairs={{4,8},{12,16},{20,24},{28,32},{36,40},{44,48},{52,56},{60,64},{68,... | collective-permute-start | bytes 98312 | tf_op jit(solution)/shard_map/ppermute | solution.py:429
  34.2 3.1 %collective-permute-done.6.first = f32[32,256]{1,0:T(8,128)S(1)} collective-permute-done((f32[32,256]{1,0:T(8,128)S(1)}, f32[32,256]{1,0:T(8,128)S(1)}, u32[]{:S(2)}, u32[]{:S(2)}) %collective-permute-start.6) | collective-permute-done | bytes 32800 | tf_op jit(solution)/shard_map/ppermute | solution.py:429
  37.7 3.6 %collective-permute-start.8 = (f32[32,256]{1,0:T(8,128)S(1)}, f32[32,256]{1,0:T(8,128)S(1)}, u32[]{:S(2)}, u32[]{:S(2)}) collective-permute-start(f32[32,256]{1,0:T(8,128)S(1)} %get-tuple-element.503), channel_id=1, source_target_pairs={{4,8},{12,16},{20,24},{28,32},{36,40},{44,48},{52,56},{60,64},{68,... | collective-permute-start | bytes 98312 | tf_op jit(solution)/shard_map/ppermute | solution.py:429
  41.6 3.1 %collective-permute-done.8.first = f32[32,256]{1,0:T(8,128)S(1)} collective-permute-done((f32[32,256]{1,0:T(8,128)S(1)}, f32[32,256]{1,0:T(8,128)S(1)}, u32[]{:S(2)}, u32[]{:S(2)}) %collective-permute-start.8) | collective-permute-done | bytes 32800 | tf_op jit(solution)/shard_map/ppermute | solution.py:429
  45.1 3.6 %collective-permute-start.10 = (f32[32,256]{1,0:T(8,128)S(1)}, f32[32,256]{1,0:T(8,128)S(1)}, u32[]{:S(2)}, u32[]{:S(2)}) collective-permute-start(f32[32,256]{1,0:T(8,128)S(1)} %get-tuple-element.509), channel_id=1, source_target_pairs={{4,8},{12,16},{20,24},{28,32},{36,40},{44,48},{52,56},{60,64},{68,... | collective-permute-start | bytes 98312 | tf_op jit(solution)/shard_map/ppermute | solution.py:429
  49.1 3.1 %collective-permute-done.10.first = f32[32,256]{1,0:T(8,128)S(1)} collective-permute-done((f32[32,256]{1,0:T(8,128)S(1)}, f32[32,256]{1,0:T(8,128)S(1)}, u32[]{:S(2)}, u32[]{:S(2)}) %collective-permute-start.10) | collective-permute-done | bytes 32800 | tf_op jit(solution)/shard_map/ppermute | solution.py:429
  52.6 3.7 %collective-permute-start.12 = (f32[32,256]{1,0:T(8,128)S(1)}, f32[32,256]{1,0:T(8,128)S(1)}, u32[]{:S(2)}, u32[]{:S(2)}) collective-permute-start(f32[32,256]{1,0:T(8,128)S(1)} %get-tuple-element.515), channel_id=1, source_target_pairs={{4,8},{12,16},{20,24},{28,32},{36,40},{44,48},{52,56},{60,64},{68,... | collective-permute-start | bytes 98312 | tf_op jit(solution)/shard_map/ppermute | solution.py:429
  56.6 3.0 %collective-permute-done.12.first = f32[32,256]{1,0:T(8,128)S(1)} collective-permute-done((f32[32,256]{1,0:T(8,128)S(1)}, f32[32,256]{1,0:T(8,128)S(1)}, u32[]{:S(2)}, u32[]{:S(2)}) %collective-permute-start.12) | collective-permute-done | bytes 32800 | tf_op jit(solution)/shard_map/ppermute | solution.py:429
  60.1 3.7 %collective-permute-start.14 = (f32[32,256]{1,0:T(8,128)S(1)}, f32[32,256]{1,0:T(8,128)S(1)}, u32[]{:S(2)}, u32[]{:S(2)}) collective-permute-start(f32[32,256]{1,0:T(8,128)S(1)} %get-tuple-element.521), channel_id=1, source_target_pairs={{4,8},{12,16},{20,24},{28,32},{36,40},{44,48},{52,56},{60,64},{68,... | collective-permute-start | bytes 98312 | tf_op jit(solution)/shard_map/ppermute | solution.py:429
  64.1 3.0 %collective-permute-done.14.first = f32[32,256]{1,0:T(8,128)S(1)} collective-permute-done((f32[32,256]{1,0:T(8,128)S(1)}, f32[32,256]{1,0:T(8,128)S(1)}, u32[]{:S(2)}, u32[]{:S(2)}) %collective-permute-start.14) | collective-permute-done | bytes 32800 | tf_op jit(solution)/shard_map/ppermute | solution.py:429
  67.5 3.7 %collective-permute-start.16 = (f32[32,256]{1,0:T(8,128)S(1)}, f32[32,256]{1,0:T(8,128)S(1)}, u32[]{:S(2)}, u32[]{:S(2)}) collective-permute-start(f32[32,256]{1,0:T(8,128)S(1)} %get-tuple-element.527), channel_id=1, source_target_pairs={{4,8},{12,16},{20,24},{28,32},{36,40},{44,48},{52,56},{60,64},{68,... | collective-permute-start | bytes 98312 | tf_op jit(solution)/shard_map/ppermute | solution.py:429
  71.6 3.6 %collective-permute-done.16.first = f32[32,256]{1,0:T(8,128)S(1)} collective-permute-done((f32[32,256]{1,0:T(8,128)S(1)}, f32[32,256]{1,0:T(8,128)S(1)}, u32[]{:S(2)}, u32[]{:S(2)}) %collective-permute-start.16) | collective-permute-done | bytes 32800 | tf_op jit(solution)/shard_map/ppermute | solution.py:429
  75.5 3.7 %collective-permute-start.18 = (f32[32,256]{1,0:T(8,128)S(1)}, f32[32,256]{1,0:T(8,128)S(1)}, u32[]{:S(2)}, u32[]{:S(2)}) collective-permute-start(f32[32,256]{1,0:T(8,128)S(1)} %get-tuple-element.533), channel_id=1, source_target_pairs={{4,8},{12,16},{20,24},{28,32},{36,40},{44,48},{52,56},{60,64},{68,... | collective-permute-start | bytes 98312 | tf_op jit(solution)/shard_map/ppermute | solution.py:429
  79.6 3.1 %collective-permute-done.18.first = f32[32,256]{1,0:T(8,128)S(1)} collective-permute-done((f32[32,256]{1,0:T(8,128)S(1)}, f32[32,256]{1,0:T(8,128)S(1)}, u32[]{:S(2)}, u32[]{:S(2)}) %collective-permute-start.18) | collective-permute-done | bytes 32800 | tf_op jit(solution)/shard_map/ppermute | solution.py:429
  83.1 3.6 %collective-permute-start.20 = (f32[32,256]{1,0:T(8,128)S(1)}, f32[32,256]{1,0:T(8,128)S(1)}, u32[]{:S(2)}, u32[]{:S(2)}) collective-permute-start(f32[32,256]{1,0:T(8,128)S(1)} %get-tuple-element.539), channel_id=1, source_target_pairs={{4,8},{12,16},{20,24},{28,32},{36,40},{44,48},{52,56},{60,64},{68,... | collective-permute-start | bytes 98312 | tf_op jit(solution)/shard_map/ppermute | solution.py:429
  87.1 3.0 %collective-permute-done.20.first = f32[32,256]{1,0:T(8,128)S(1)} collective-permute-done((f32[32,256]{1,0:T(8,128)S(1)}, f32[32,256]{1,0:T(8,128)S(1)}, u32[]{:S(2)}, u32[]{:S(2)}) %collective-permute-start.20) | collective-permute-done | bytes 32800 | tf_op jit(solution)/shard_map/ppermute | solution.py:429
  90.5 3.6 %collective-permute-start.22 = (f32[32,256]{1,0:T(8,128)S(1)}, f32[32,256]{1,0:T(8,128)S(1)}, u32[]{:S(2)}, u32[]{:S(2)}) collective-permute-start(f32[32,256]{1,0:T(8,128)S(1)} %get-tuple-element.545), channel_id=1, source_target_pairs={{4,8},{12,16},{20,24},{28,32},{36,40},{44,48},{52,56},{60,64},{68,... | collective-permute-start | bytes 98312 | tf_op jit(solution)/shard_map/ppermute | solution.py:429
  94.6 3.0 %collective-permute-done.22.first = f32[32,256]{1,0:T(8,128)S(1)} collective-permute-done((f32[32,256]{1,0:T(8,128)S(1)}, f32[32,256]{1,0:T(8,128)S(1)}, u32[]{:S(2)}, u32[]{:S(2)}) %collective-permute-start.22) | collective-permute-done | bytes 32800 | tf_op jit(solution)/shard_map/ppermute | solution.py:429
  98.0 3.6 %collective-permute-start.24 = (f32[32,256]{1,0:T(8,128)S(1)}, f32[32,256]{1,0:T(8,128)S(1)}, u32[]{:S(2)}, u32[]{:S(2)}) collective-permute-start(f32[32,256]{1,0:T(8,128)S(1)} %get-tuple-element.551), channel_id=1, source_target_pairs={{4,8},{12,16},{20,24},{28,32},{36,40},{44,48},{52,56},{60,64},{68,... | collective-permute-start | bytes 98312 | tf_op jit(solution)/shard_map/ppermute | solution.py:429
  102.0 3.0 %collective-permute-done.24.first = f32[32,256]{1,0:T(8,128)S(1)} collective-permute-done((f32[32,256]{1,0:T(8,128)S(1)}, f32[32,256]{1,0:T(8,128)S(1)}, u32[]{:S(2)}, u32[]{:S(2)}) %collective-permute-start.24) | collective-permute-done | bytes 32800 | tf_op jit(solution)/shard_map/ppermute | solution.py:429
  105.1 1.0 shard_map.84
  106.1 0.8 shard_map.85
  106.9 11.4 %all_to_all.10.parts = f32[8,48,128]{2,1,0:T(8,128)S(1)} all-to-all(f32[8,48,128]{2,1,0:T(8,128)S(1)} %shard_map.85), channel_id=1, replica_groups={{0,32,64,96,128,160,192,224},{4,36,68,100,132,164,196,228},{8,40,72,104..., dimensions={0} | all-to-all | bytes 393216 | tf_op jit(solution)/shard_map/all_to_all | solution.py:421
  118.4 8.9 %all_to_all.11.parts = f32[8,48,128]{2,1,0:T(8,128)S(1)} all-to-all(f32[8,48,128]{2,1,0:T(8,128)S(1)} %shard_map.86), channel_id=1, replica_groups={{0,4,8,12,16,20,24,28},{32,36,40,44,48,52,56,60},{64,68,72,76,80,84,88,..., dimensions={0} | all-to-all | bytes 393216 | tf_op jit(solution)/shard_map/all_to_all | solution.py:421
  127.3 1.1 shard_map.87
  128.4 16.9 %collective-permute-start.26 = (f32[72,128]{1,0:T(8,128)S(1)}, f32[72,128]{1,0:T(8,128)S(1)}, u32[]{:S(2)}, u32[]{:S(2)}) collective-permute-start(f32[72,128]{1,0:T(8,128)S(1)} %get-tuple-element.581.other), channel_id=1, source_target_pairs={{0,1},{1,0},{2,3},{3,2},{4,5},{5,4},{6,7},{7,6},{8,9},{9,8},{10,11... | collective-permute-start | bytes 110600 | tf_op jit(solution)/shard_map/ppermute | solution.py:525
  145.3 0.9 collective-permute-done.26.arrived
  (64 shorter events, 10.8 us)
Async XLA Ops:
  11.6 10.7 %collective-permute-start.2 = (f32[32,256]{1,0:T(8,128)S(1)}, f32[32,256]{1,0:T(8,128)S(1)}, u32[]{:S(2)}, u32[]{:S(2)}) collective-permute-start(f32[32,256]{1,0:T(8,128)S(1)} %get-tuple-element.482), channel_id=1, source_target_pairs={{4,8},{12,16},{20,24},{28,32},{36,40},{44,48},{52,56},{60,64},{68,... | collective-permute-start | bytes 98312 | tf_op jit(solution)/shard_map/ppermute | solution.py:429
  18.9 3.4 %collective-permute-start.3 = (f32[32,256]{1,0:T(8,128)S(1)}, f32[32,256]{1,0:T(8,128)S(1)}, u32[]{:S(2)}, u32[]{:S(2)}) collective-permute-start(f32[32,256]{1,0:T(8,128)S(1)} %get-tuple-element.483), channel_id=1, source_target_pairs={{0,4},{8,12},{16,20},{24,28},{32,36},{40,44},{48,52},{56,60},{64,6... | collective-permute-start | bytes 98312 | tf_op jit(solution)/shard_map/ppermute | solution.py:429
  22.7 7.2 %collective-permute-start.4 = (f32[32,256]{1,0:T(8,128)S(1)}, f32[32,256]{1,0:T(8,128)S(1)}, u32[]{:S(2)}, u32[]{:S(2)}) collective-permute-start(f32[32,256]{1,0:T(8,128)S(1)} %get-tuple-element.491), channel_id=1, source_target_pairs={{4,8},{12,16},{20,24},{28,32},{36,40},{44,48},{52,56},{60,64},{68,... | collective-permute-start | bytes 98312 | tf_op jit(solution)/shard_map/ppermute | solution.py:429
  26.3 3.5 %collective-permute-start.5 = (f32[32,256]{1,0:T(8,128)S(1)}, f32[32,256]{1,0:T(8,128)S(1)}, u32[]{:S(2)}, u32[]{:S(2)}) collective-permute-start(f32[32,256]{1,0:T(8,128)S(1)} %get-tuple-element.492), channel_id=1, source_target_pairs={{0,4},{8,12},{16,20},{24,28},{32,36},{40,44},{48,52},{56,60},{64,6... | collective-permute-start | bytes 98312 | tf_op jit(solution)/shard_map/ppermute | solution.py:429
  30.2 7.1 %collective-permute-start.6 = (f32[32,256]{1,0:T(8,128)S(1)}, f32[32,256]{1,0:T(8,128)S(1)}, u32[]{:S(2)}, u32[]{:S(2)}) collective-permute-start(f32[32,256]{1,0:T(8,128)S(1)} %get-tuple-element.497), channel_id=1, source_target_pairs={{4,8},{12,16},{20,24},{28,32},{36,40},{44,48},{52,56},{60,64},{68,... | collective-permute-start | bytes 98312 | tf_op jit(solution)/shard_map/ppermute | solution.py:429
  33.8 3.5 %collective-permute-start.7 = (f32[32,256]{1,0:T(8,128)S(1)}, f32[32,256]{1,0:T(8,128)S(1)}, u32[]{:S(2)}, u32[]{:S(2)}) collective-permute-start(f32[32,256]{1,0:T(8,128)S(1)} %get-tuple-element.498), channel_id=1, source_target_pairs={{0,4},{8,12},{16,20},{24,28},{32,36},{40,44},{48,52},{56,60},{64,6... | collective-permute-start | bytes 98312 | tf_op jit(solution)/shard_map/ppermute | solution.py:429
  37.7 7.1 %collective-permute-start.8 = (f32[32,256]{1,0:T(8,128)S(1)}, f32[32,256]{1,0:T(8,128)S(1)}, u32[]{:S(2)}, u32[]{:S(2)}) collective-permute-start(f32[32,256]{1,0:T(8,128)S(1)} %get-tuple-element.503), channel_id=1, source_target_pairs={{4,8},{12,16},{20,24},{28,32},{36,40},{44,48},{52,56},{60,64},{68,... | collective-permute-start | bytes 98312 | tf_op jit(solution)/shard_map/ppermute | solution.py:429
  41.2 3.5 %collective-permute-start.9 = (f32[32,256]{1,0:T(8,128)S(1)}, f32[32,256]{1,0:T(8,128)S(1)}, u32[]{:S(2)}, u32[]{:S(2)}) collective-permute-start(f32[32,256]{1,0:T(8,128)S(1)} %get-tuple-element.504), channel_id=1, source_target_pairs={{0,4},{8,12},{16,20},{24,28},{32,36},{40,44},{48,52},{56,60},{64,6... | collective-permute-start | bytes 98312 | tf_op jit(solution)/shard_map/ppermute | solution.py:429
  45.1 7.1 %collective-permute-start.10 = (f32[32,256]{1,0:T(8,128)S(1)}, f32[32,256]{1,0:T(8,128)S(1)}, u32[]{:S(2)}, u32[]{:S(2)}) collective-permute-start(f32[32,256]{1,0:T(8,128)S(1)} %get-tuple-element.509), channel_id=1, source_target_pairs={{4,8},{12,16},{20,24},{28,32},{36,40},{44,48},{52,56},{60,64},{68,... | collective-permute-start | bytes 98312 | tf_op jit(solution)/shard_map/ppermute | solution.py:429
  48.7 3.5 %collective-permute-start.11 = (f32[32,256]{1,0:T(8,128)S(1)}, f32[32,256]{1,0:T(8,128)S(1)}, u32[]{:S(2)}, u32[]{:S(2)}) collective-permute-start(f32[32,256]{1,0:T(8,128)S(1)} %get-tuple-element.510), channel_id=1, source_target_pairs={{0,4},{8,12},{16,20},{24,28},{32,36},{40,44},{48,52},{56,60},{64,6... | collective-permute-start | bytes 98312 | tf_op jit(solution)/shard_map/ppermute | solution.py:429
  52.6 7.1 %collective-permute-start.12 = (f32[32,256]{1,0:T(8,128)S(1)}, f32[32,256]{1,0:T(8,128)S(1)}, u32[]{:S(2)}, u32[]{:S(2)}) collective-permute-start(f32[32,256]{1,0:T(8,128)S(1)} %get-tuple-element.515), channel_id=1, source_target_pairs={{4,8},{12,16},{20,24},{28,32},{36,40},{44,48},{52,56},{60,64},{68,... | collective-permute-start | bytes 98312 | tf_op jit(solution)/shard_map/ppermute | solution.py:429
  56.3 3.4 %collective-permute-start.13 = (f32[32,256]{1,0:T(8,128)S(1)}, f32[32,256]{1,0:T(8,128)S(1)}, u32[]{:S(2)}, u32[]{:S(2)}) collective-permute-start(f32[32,256]{1,0:T(8,128)S(1)} %get-tuple-element.516), channel_id=1, source_target_pairs={{0,4},{8,12},{16,20},{24,28},{32,36},{40,44},{48,52},{56,60},{64,6... | collective-permute-start | bytes 98312 | tf_op jit(solution)/shard_map/ppermute | solution.py:429
  60.1 7.1 %collective-permute-start.14 = (f32[32,256]{1,0:T(8,128)S(1)}, f32[32,256]{1,0:T(8,128)S(1)}, u32[]{:S(2)}, u32[]{:S(2)}) collective-permute-start(f32[32,256]{1,0:T(8,128)S(1)} %get-tuple-element.521), channel_id=1, source_target_pairs={{4,8},{12,16},{20,24},{28,32},{36,40},{44,48},{52,56},{60,64},{68,... | collective-permute-start | bytes 98312 | tf_op jit(solution)/shard_map/ppermute | solution.py:429
  63.7 3.4 %collective-permute-start.15 = (f32[32,256]{1,0:T(8,128)S(1)}, f32[32,256]{1,0:T(8,128)S(1)}, u32[]{:S(2)}, u32[]{:S(2)}) collective-permute-start(f32[32,256]{1,0:T(8,128)S(1)} %get-tuple-element.522), channel_id=1, source_target_pairs={{0,4},{8,12},{16,20},{24,28},{32,36},{40,44},{48,52},{56,60},{64,6... | collective-permute-start | bytes 98312 | tf_op jit(solution)/shard_map/ppermute | solution.py:429
  67.5 7.6 %collective-permute-start.16 = (f32[32,256]{1,0:T(8,128)S(1)}, f32[32,256]{1,0:T(8,128)S(1)}, u32[]{:S(2)}, u32[]{:S(2)}) collective-permute-start(f32[32,256]{1,0:T(8,128)S(1)} %get-tuple-element.527), channel_id=1, source_target_pairs={{4,8},{12,16},{20,24},{28,32},{36,40},{44,48},{52,56},{60,64},{68,... | collective-permute-start | bytes 98312 | tf_op jit(solution)/shard_map/ppermute | solution.py:429
  71.2 4.0 %collective-permute-start.17 = (f32[32,256]{1,0:T(8,128)S(1)}, f32[32,256]{1,0:T(8,128)S(1)}, u32[]{:S(2)}, u32[]{:S(2)}) collective-permute-start(f32[32,256]{1,0:T(8,128)S(1)} %get-tuple-element.528), channel_id=1, source_target_pairs={{0,4},{8,12},{16,20},{24,28},{32,36},{40,44},{48,52},{56,60},{64,6... | collective-permute-start | bytes 98312 | tf_op jit(solution)/shard_map/ppermute | solution.py:429
  75.5 7.2 %collective-permute-start.18 = (f32[32,256]{1,0:T(8,128)S(1)}, f32[32,256]{1,0:T(8,128)S(1)}, u32[]{:S(2)}, u32[]{:S(2)}) collective-permute-start(f32[32,256]{1,0:T(8,128)S(1)} %get-tuple-element.533), channel_id=1, source_target_pairs={{4,8},{12,16},{20,24},{28,32},{36,40},{44,48},{52,56},{60,64},{68,... | collective-permute-start | bytes 98312 | tf_op jit(solution)/shard_map/ppermute | solution.py:429
  79.3 3.4 %collective-permute-start.19 = (f32[32,256]{1,0:T(8,128)S(1)}, f32[32,256]{1,0:T(8,128)S(1)}, u32[]{:S(2)}, u32[]{:S(2)}) collective-permute-start(f32[32,256]{1,0:T(8,128)S(1)} %get-tuple-element.534), channel_id=1, source_target_pairs={{0,4},{8,12},{16,20},{24,28},{32,36},{40,44},{48,52},{56,60},{64,6... | collective-permute-start | bytes 98312 | tf_op jit(solution)/shard_map/ppermute | solution.py:429
  83.1 7.1 %collective-permute-start.20 = (f32[32,256]{1,0:T(8,128)S(1)}, f32[32,256]{1,0:T(8,128)S(1)}, u32[]{:S(2)}, u32[]{:S(2)}) collective-permute-start(f32[32,256]{1,0:T(8,128)S(1)} %get-tuple-element.539), channel_id=1, source_target_pairs={{4,8},{12,16},{20,24},{28,32},{36,40},{44,48},{52,56},{60,64},{68,... | collective-permute-start | bytes 98312 | tf_op jit(solution)/shard_map/ppermute | solution.py:429
  86.7 3.4 %collective-permute-start.21 = (f32[32,256]{1,0:T(8,128)S(1)}, f32[32,256]{1,0:T(8,128)S(1)}, u32[]{:S(2)}, u32[]{:S(2)}) collective-permute-start(f32[32,256]{1,0:T(8,128)S(1)} %get-tuple-element.540), channel_id=1, source_target_pairs={{0,4},{8,12},{16,20},{24,28},{32,36},{40,44},{48,52},{56,60},{64,6... | collective-permute-start | bytes 98312 | tf_op jit(solution)/shard_map/ppermute | solution.py:429
  90.5 7.1 %collective-permute-start.22 = (f32[32,256]{1,0:T(8,128)S(1)}, f32[32,256]{1,0:T(8,128)S(1)}, u32[]{:S(2)}, u32[]{:S(2)}) collective-permute-start(f32[32,256]{1,0:T(8,128)S(1)} %get-tuple-element.545), channel_id=1, source_target_pairs={{4,8},{12,16},{20,24},{28,32},{36,40},{44,48},{52,56},{60,64},{68,... | collective-permute-start | bytes 98312 | tf_op jit(solution)/shard_map/ppermute | solution.py:429
  94.2 3.4 %collective-permute-start.23 = (f32[32,256]{1,0:T(8,128)S(1)}, f32[32,256]{1,0:T(8,128)S(1)}, u32[]{:S(2)}, u32[]{:S(2)}) collective-permute-start(f32[32,256]{1,0:T(8,128)S(1)} %get-tuple-element.546), channel_id=1, source_target_pairs={{0,4},{8,12},{16,20},{24,28},{32,36},{40,44},{48,52},{56,60},{64,6... | collective-permute-start | bytes 98312 | tf_op jit(solution)/shard_map/ppermute | solution.py:429
  98.0 7.1 %collective-permute-start.24 = (f32[32,256]{1,0:T(8,128)S(1)}, f32[32,256]{1,0:T(8,128)S(1)}, u32[]{:S(2)}, u32[]{:S(2)}) collective-permute-start(f32[32,256]{1,0:T(8,128)S(1)} %get-tuple-element.551), channel_id=1, source_target_pairs={{4,8},{12,16},{20,24},{28,32},{36,40},{44,48},{52,56},{60,64},{68,... | collective-permute-start | bytes 98312 | tf_op jit(solution)/shard_map/ppermute | solution.py:429
  101.6 3.4 %collective-permute-start.25 = (f32[32,256]{1,0:T(8,128)S(1)}, f32[32,256]{1,0:T(8,128)S(1)}, u32[]{:S(2)}, u32[]{:S(2)}) collective-permute-start(f32[32,256]{1,0:T(8,128)S(1)} %get-tuple-element.552), channel_id=1, source_target_pairs={{0,4},{8,12},{16,20},{24,28},{32,36},{40,44},{48,52},{56,60},{64,6... | collective-permute-start | bytes 98312 | tf_op jit(solution)/shard_map/ppermute | solution.py:429
  106.9 40.6 %copy-start = (f32[4,7,128,128]{3,2,1,0:T(8,128)S(1)}, f32[4,7,128,128]{3,2,1,0:T(8,128)}, u32[]{:S(2)}) copy-start(f32[4,7,128,128]{3,2,1,0:T(8,128)} %blocks.1) | copy-start | bytes 5505028
  106.9 40.6 %copy-start.1 = (s32[1,2,2]{2,1,0:T(2,128)S(1)}, s32[1,2,2]{2,1,0:T(2,128)}, u32[]{:S(2)}) copy-start(s32[1,2,2]{2,1,0:T(2,128)} %param.17) | copy-start | bytes 52
  106.9 40.6 %copy-start.2 = (f32[128,64]{0,1:T(8,128)S(1)}, f32[128,64]{0,1:T(8,128)}, u32[]{:S(2)}) copy-start(f32[128,64]{0,1:T(8,128)} %param.14) | copy-start | bytes 98308
  106.9 40.6 %copy-start.3 = (s32[4,7]{1,0:T(4,128)S(1)}, s32[4,7]{1,0:T(4,128)}, u32[]{:S(2)}) copy-start(s32[4,7]{1,0:T(4,128)} %cols.1) | copy-start | bytes 340
  128.4 17.7 %collective-permute-start.26 = (f32[72,128]{1,0:T(8,128)S(1)}, f32[72,128]{1,0:T(8,128)S(1)}, u32[]{:S(2)}, u32[]{:S(2)}) collective-permute-start(f32[72,128]{1,0:T(8,128)S(1)} %get-tuple-element.581.other), channel_id=1, source_target_pairs={{0,1},{1,0},{2,3},{3,2},{4,5},{5,4},{6,7},{7,6},{8,9},{9,8},{10,11... | collective-permute-start | bytes 110600 | tf_op jit(solution)/shard_map/ppermute | solution.py:525
  147.5 0.6 copy-start.4
  147.5 0.6 copy-start.5

commit v2 on v1

--- a/solution.py
+++ b/solution.py
@@ -27,6 +27,9 @@
 TILES = -(-COUNT * (COUNT + 1) // 2 // (SUBLANES * GROUP))
 SUM_ROWS = TILES * SUBLANES
 LIMIT = 2000.0
+SINGLE = 4
+CHUNKS = SINGLE - 1
+SHARED = (EXT * BS + NB * SUBLANES) // CHUNKS
 
 VMEM = pl.BlockSpec(memory_space=pltpu.VMEM)
 SMEM = pl.BlockSpec(memory_space=pltpu.SMEM)
@@ -62,8 +65,16 @@
     return first[:COLS] + (first[COLS : 2 * COLS] + second[:COLS] + small)
 
 
-def operator_kernel(cols, blocks, *refs):
-    own, received, dense = refs[:3], refs[3:6], refs[6]
+def sent_block(lists, side, slot):
+    return lists[(side + lax.axis_index("sub") + 1) % 2, slot]
+
+
+def chosen_block(listed, block):
+    return jnp.where(jnp.full((SUBLANES, BS), listed, jnp.int32) == block, 1.0, 0.0)
+
+
+def operator_kernel(cols, lists, blocks, *refs):
+    own, received, chunks, dense = refs[:3], refs[3:6], refs[6:-1], refs[-1]
     turn = HALO * (lax.axis_index("sub") % 2)
     dense[...] = jnp.zeros_like(dense)
     for row in range(NB):
@@ -82,36 +93,64 @@
             value = dense[place]
             if row == column:
                 value = value - CENTER * unit
+            value = value * (1.0 / RADIUS)
+            dense[place] = value
             targets = own if column < NB else received
             start = (column % NB) * BS
-            for target, part in zip(targets, split(value * (1.0 / RADIUS))):
+            for target, part in zip(targets, split(value)):
                 target[start : start + BS, row * BS : (row + 1) * BS] = part
-
-
-def write_chosen(masks, vector, sends):
+    listed = sent_block(lists, 0, lax.axis_index("fold") % 2)
+    masks = [chosen_block(listed, block) for block in range(NB)]
+    start = pl.multiple_of(listed * BS, BS)
+    shared = jnp.concatenate([dense[:, pl.ds(start, BS)], *masks], 0)
+    for index, chunk in enumerate(chunks):
+        chunk[...] = shared[index * SHARED : (index + 1) * SHARED]
+
+
+def ghost_kernel(*refs):
+    mine, others = (
+        jnp.concatenate([ref[...] for ref in half], 0)
+        for half in (refs[:CHUNKS], refs[CHUNKS : 2 * CHUNKS])
+    )
+    parts, masks = refs[2 * CHUNKS : -1], refs[-1]
+    even = lax.axis_index("fold") % 2 == 0
+    for slot in range(HALO):
+        one, other = (mine, others) if slot == 0 else (others, mine)
+        value = jnp.where(even, one, other)
+        place = slice(slot * BS, (slot + 1) * BS)
+        for target, part in zip(parts, split(value[: EXT * BS])):
+            target[:, place] = part
+        for block in range(NB):
+            start = EXT * BS + block * SUBLANES
+            masks[slot, block] = value[start : start + SUBLANES]
+
+
+def write_chosen(masks, vector, target):
     repeats = vector.shape[0] // SUBLANES
+    for slot in range(HALO):
+        total = None
+        for block in range(NB):
+            mask = jnp.concatenate([masks[slot, block]] * repeats, 0)
+            value = vector[:, block * BS : (block + 1) * BS]
+            total = value if total is None else jnp.where(mask > 0.5, value, total)
+        target[:, slot * BS : (slot + 1) * BS] = total
+
+
+def write_sends(masks, vector, sends):
     for side, target in enumerate(sends):
-        for slot in range(HALO):
-            total = None
-            for block in range(NB):
-                mask = jnp.concatenate([masks[side * HALO + slot, block]] * repeats, 0)
-                value = vector[:, block * BS : (block + 1) * BS]
-                total = value if total is None else jnp.where(mask > 0.5, value, total)
-            target[:, slot * BS : (slot + 1) * BS] = total
+        write_chosen(masks.at[side], vector, target)
 
 
 def start_kernel(lists, gathered, masks, result, *sends):
-    parity = lax.axis_index("sub") % 2
     first = pl.multiple_of(lax.axis_index("fold") % 2 * COLS, COLS)
     for side in range(2):
         for slot in range(HALO):
-            listed = lists[(side + parity + 1) % 2, slot]
+            listed = sent_block(lists, side, slot)
             for block in range(NB):
-                chosen = jnp.full((SUBLANES, BS), listed, jnp.int32) == block
-                masks[side * HALO + slot, block] = jnp.where(chosen, 1.0, 0.0)
+                masks[side, slot, block] = chosen_block(listed, block)
     vector = gathered[pl.ds(first, COLS), :]
     result[...] = vector
-    write_chosen(masks, vector, sends)
+    write_sends(masks, vector, sends)
 
 
 def step_kernel(masks, partial, first, second, *refs):
@@ -119,7 +158,18 @@
     received = jnp.concatenate([first[...], second[...]], 1)
     vector = partial[...] + product(received, *parts)
     result[...] = vector
-    write_chosen(masks, vector, sends)
+    write_sends(masks, vector, sends)
+
+
+def ahead_kernel(masks, partner_masks, partial, whole, across, near, sent, *refs):
+    parts, ghost_parts, (result, send, ghost, first) = refs[:3], refs[3:6], refs[6:]
+    write_chosen(partner_masks, whole, first)
+    received = jnp.concatenate([first[...], near[...]], 1)
+    vector = partial[...] + product(received, *parts)
+    result[...] = vector
+    write_chosen(masks.at[1], vector, send)
+    extended = jnp.concatenate([whole[...], sent[...], across[...]], 1)
+    ghost[...] = product(extended, *ghost_parts)
 
 
 def small_solve(matrix, target):
@@ -429,6 +479,16 @@
     return lax.ppermute(value, "sub", pairs + [(j, i) for i, j in pairs])
 
 
+def sent_across(value):
+    subs = lax.axis_size("sub")
+    pairs = [(i, (i + 2 if i % 2 == 0 else i - 2) % subs) for i in range(subs)]
+    return lax.ppermute(value, "sub", pairs)
+
+
+def core_swapped(value):
+    return lax.ppermute(value, "fold", [(0, 1), (1, 0), (2, 3), (3, 2)])
+
+
 def passed(value, by):
     subs = lax.axis_size("sub")
     return lax.ppermute(value, "sub", [(i, (i + by) % subs) for i in range(subs)])
@@ -480,37 +540,75 @@
     gathered = lax.all_gather(right_side.T, "fold", axis=1, tiled=True)
     operator = call(
         operator_kernel,
-        (bf16(ROWS, ROWS),) * 6,
-        [block_cols],
+        (bf16(ROWS, ROWS),) * 6 + (f32(SHARED, BS),) * CHUNKS,
+        [block_cols, lists],
         [blocks],
         [pltpu.VMEM((EXT * BS, ROWS), jnp.float32)],
         flops=10**9,
     )
-    masks_shape = f32(2 * HALO, NB, SUBLANES, BS)
+    operator, chunks = operator[:6], operator[6:]
+    masks_shape = f32(2, HALO, NB, SUBLANES, BS)
     masks, *sends = call(
         start_kernel, (masks_shape, VECTOR, HALO_PART, HALO_PART), [lists], [gathered]
     )
     square = f32(BS, BS)
-    vectors, earlier, sums = [sends[0]], [], []
-    for power in range(COUNT - 1):
-        row = f32(power + 1, SUBLANES, BS)
+    vectors, earlier, sums = [], [], []
+
+    def own_part(vector):
+        row = f32(len(vectors) + 1, SUBLANES, BS)
         partial, coarse, rest, high, low = call(
             round_kernel,
             (VECTOR, square, square, row, row),
             [],
-            [sends[0], *operator[:3], *earlier],
+            [vector, *operator[:3], *earlier],
             flops=10**9,
         )
-        earlier += [coarse, rest]
-        sums += [high, low]
-        received = [swapped(sends[1], 1), swapped(sends[2], 0)]
-        sends = call(
-            step_kernel,
+        vectors.append(vector)
+        earlier.extend([coarse, rest])
+        sums.extend([high, low])
+        return partial
+
+    def stepped(partial, first, second):
+        return list(
+            call(
+                step_kernel,
+                (VECTOR, HALO_PART, HALO_PART),
+                [],
+                [masks, partial, first, second, *operator[3:]],
+            )
+        )
+
+    shared = []
+    for power in range(SINGLE):
+        if power < CHUNKS:
+            chunk, partial = lax.optimization_barrier((chunks[power], own_part(sends[0])))
+            shared.append(swapped(chunk, 1))
+        else:
+            shared, sends[0] = lax.optimization_barrier((shared, sends[0]))
+            others = [core_swapped(chunk) for chunk in shared]
+            partial = own_part(sends[0])
+        sends = stepped(partial, swapped(sends[1], 1), swapped(sends[2], 0))
+    *ghost_operator, partner_masks = call(
+        ghost_kernel,
+        (bf16(EXT * BS, HALO * BS),) * 3 + (f32(HALO, NB, SUBLANES, BS),),
+        [],
+        [*shared, *others],
+        flops=10**8,
+    )
+    for power in range(SINGLE, COUNT - 1, 2):
+        vector, between, within = sends
+        partial = own_part(vector)
+        arrived = [swapped(vector, 1), sent_across(within), swapped(within, 0)]
+        vector, within, ghost = call(
+            ahead_kernel,
             (VECTOR, HALO_PART, HALO_PART),
             [],
-            [masks, partial, *received, *operator[3:]],
+            [masks, partner_masks, partial, *arrived, between, *operator[3:], *ghost_operator],
+            [pltpu.VMEM((COLS, HALO * BS), jnp.float32)],
         )
-        vectors.append(sends[0])
+        partial = own_part(vector)
+        sends = stepped(partial, ghost, swapped(within, 0))
+    vectors.append(sends[0])
     packed = f32(PART, 2 * SUM_ROWS, BS)
     sums = call(pack_kernel, packed, [], [vectors[-1], *earlier, *sums])
     strided = [[i + PART * j for j in range(subs // PART)] for i in range(PART)]
@@ -522,7 +620,7 @@
         [],
         [exchanged_over(runs)(sums), *vectors],
     )
-    arrived = lax.ppermute(other, "fold", [(0, 1), (1, 0), (2, 3), (3, 2)])
+    arrived = core_swapped(other)
     correction, residual, bad = call(
         join_kernel,
         (f32(2 * COLS, BS), f32(2 * COLS, BS), jax.ShapeDtypeStruct((1,), jnp.int32)),

time: 148 us -> 141 us (0.953)
  starting transfers between devices: 64.2 us -> 50.9 us
  waiting for transfers between devices: 35.2 us -> 39.8 us
  Pallas kernels: 16 us -> 17.6 us
    ppermute x24 -> x23, starting transfers between devices: 47.3 us -> 33.8 us  [swapped(): return lax.ppermute(value, 'sub', pairs + [(j, i) for i, j in pairs])]
    ppermute x1 -> x8, waiting for transfers between devices: 0.87 us -> 13.1 us  [the longest x4 12.2 us: sent_across(): return lax.ppermute(value, 'sub', pairs)]
    ppermute x24 -> x23, waiting for transfers between devices: 34.4 us -> 26.7 us  [swapped(): return lax.ppermute(value, 'sub', pairs + [(j, i) for i, j in pairs])]
    pallas_call x30 -> x31, Pallas kernels: 16 us -> 17.6 us  [call(): pl.pallas_call(kernel, out_shape=out_shape, in_specs=[SMEM] * len(smem) +...]
    ppermute x1 -> x8, starting transfers between devices: 16.9 us -> 17.1 us  [the longest x4 16.6 us: core_swapped(): return lax.ppermute(value, 'fold', [(0, 1), (1, 0), (2, 3), (3, 2)])]
  transfers between devices with their start and end apart: 25 -> 31, of which waited for: 12 -> 16; matrix products, arithmetic and copies ran while one was open for 0% -> 0% of each run, Pallas kernels for 5% -> 7%
where the time goes in v2:
time: 141 us; the launch traced here: 140 us
  starting transfers between devices  50.9 us (36%)
  waiting for transfers between devices  39.8 us (28%)
  blocking collectives  29.7 us (21%)
  Pallas kernels  17.6 us (12%)
  between operations  1.65 us (1%)
    ppermute x23, starting transfers between devices, swapped(): return lax.ppermute(value, 'sub', pairs + [(j, i) for i, j in pairs])  33.8 us
    ppermute x23, waiting for transfers between devices, swapped(): return lax.ppermute(value, 'sub', pairs + [(j, i) for i, j in pairs])  26.7 us
    all_to_all x2, blocking collectives, exchanged(): return lax.all_to_all(value, 'sub', 0, 0, axis_index_groups=groups)  19.5 us
    pallas_call x31, Pallas kernels, call(): pl.pallas_call(kernel, out_shape=out_shape, in_specs=[SMEM] * len(smem) +...  17.6 us
    ppermute x4, starting transfers between devices, core_swapped(): return lax.ppermute(value, 'fold', [(0, 1), (1, 0), (2, 3), (3, 2)])  16.6 us
    ppermute x4, waiting for transfers between devices, sent_across(): return lax.ppermute(value, 'sub', pairs)  12.2 us
    all_gather x1, blocking collectives, on_device(): gathered = lax.all_gather(right_side.T, 'fold', axis=1, tiled=True)  10.2 us
  transfers between devices with their start and end apart: 31, of which 16 were waited for; matrix products, arithmetic and copies ran while one was open for 0% of the time, Pallas kernels for 7%

profile of v2, /device:TPU:1, one launch (start us, length us, event | category | flops | bytes accessed | tf_op | source)
XLA Modules:
  0.0 140.3 jit_solution(7373157867833577257)
XLA Ops:
  0.6 10.2 %all_gather.6.gathered = f32[64,512]{1,0:T(8,128)S(1)} all-gather(f32[64,128]{1,0:T(8,128)} %bitcast.228), channel_id=1, replica_groups=mesh['sub'=64,'fold'=4] {'fold'}, dimensions={1}, use_global_device_ids=true | all-gather | bytes 163840 | tf_op jit(solution)/shard_map/all_gather | solution.py:540
  11.6 7.3 %collective-permute-start.3 = (f32[32,256]{1,0:T(8,128)S(1)}, f32[32,256]{1,0:T(8,128)S(1)}, u32[]{:S(2)}, u32[]{:S(2)}) collective-permute-start(f32[32,256]{1,0:T(8,128)S(1)} %get-tuple-element.503), channel_id=1, source_target_pairs={{4,8},{12,16},{20,24},{28,32},{36,40},{44,48},{52,56},{60,64},{68,... | collective-permute-start | bytes 98312 | tf_op jit(solution)/shard_map/ppermute | solution.py:479
  18.9 3.2 %shard_map.60 = (bf16[512,512]{1,0:T(8,128)(2,1)S(1)}, bf16[512,512]{1,0:T(8,128)(2,1)S(1)}, bf16[512,512]{1,0:T(8,128)(2,1)S(1)}, bf16[512,512]{1,0:T(8,128)(2,...) custom-call(s32[4,7]{1,0:T(4,128)} %cols.1, ...), custom_call_target="tpu_custom_call" | custom-call | flops 1000000000 | bytes 1048576 | tf_op jit(solution)/shard_map/pallas_call | solution.py:458
  22.4 1.6 %collective-permute-start.2 = (f32[352,128]{1,0:T(8,128)S(1)}, f32[352,128]{1,0:T(8,128)S(1)}, u32[]{:S(2)}, u32[]{:S(2)}) collective-permute-start(f32[352,128]{1,0:T(8,128)S(1)} %get-tuple-element.500), channel_id=1, source_target_pairs={{4,8},{12,16},{20,24},{28,32},{36,40},{44,48},{52,56},{60,64},{68,... | collective-permute-start | bytes 540680 | tf_op jit(solution)/shard_map/ppermute | solution.py:479
  24.5 4.1 %collective-permute-start.6 = (f32[32,256]{1,0:T(8,128)S(1)}, f32[32,256]{1,0:T(8,128)S(1)}, u32[]{:S(2)}, u32[]{:S(2)}) collective-permute-start(f32[32,256]{1,0:T(8,128)S(1)} %get-tuple-element.515), channel_id=1, source_target_pairs={{4,8},{12,16},{20,24},{28,32},{36,40},{44,48},{52,56},{60,64},{68,... | collective-permute-start | bytes 98312 | tf_op jit(solution)/shard_map/ppermute | solution.py:479
  29.0 1.7 %collective-permute-start.5 = (f32[352,128]{1,0:T(8,128)S(1)}, f32[352,128]{1,0:T(8,128)S(1)}, u32[]{:S(2)}, u32[]{:S(2)}) collective-permute-start(f32[352,128]{1,0:T(8,128)S(1)} %get-tuple-element.512), channel_id=1, source_target_pairs={{4,8},{12,16},{20,24},{28,32},{36,40},{44,48},{52,56},{60,64},{68,... | collective-permute-start | bytes 540680 | tf_op jit(solution)/shard_map/ppermute | solution.py:479
  30.6 2.4 %collective-permute-done.6.first = f32[32,256]{1,0:T(8,128)S(1)} collective-permute-done((f32[32,256]{1,0:T(8,128)S(1)}, f32[32,256]{1,0:T(8,128)S(1)}, u32[]{:S(2)}, u32[]{:S(2)}) %collective-permute-start.6) | collective-permute-done | bytes 32800 | tf_op jit(solution)/shard_map/ppermute | solution.py:479
  33.8 2.6 %collective-permute-start.8 = (f32[352,128]{1,0:T(8,128)S(1)}, f32[352,128]{1,0:T(8,128)S(1)}, u32[]{:S(2)}, u32[]{:S(2)}) collective-permute-start(f32[352,128]{1,0:T(8,128)S(1)} %get-tuple-element.521), channel_id=1, source_target_pairs={{4,8},{12,16},{20,24},{28,32},{36,40},{44,48},{52,56},{60,64},{68,... | collective-permute-start | bytes 540680 | tf_op jit(solution)/shard_map/ppermute | solution.py:479
  36.4 3.1 %collective-permute-start.9 = (f32[32,256]{1,0:T(8,128)S(1)}, f32[32,256]{1,0:T(8,128)S(1)}, u32[]{:S(2)}, u32[]{:S(2)}) collective-permute-start(f32[32,256]{1,0:T(8,128)S(1)} %get-tuple-element.523), channel_id=1, source_target_pairs={{4,8},{12,16},{20,24},{28,32},{36,40},{44,48},{52,56},{60,64},{68,... | collective-permute-start | bytes 98312 | tf_op jit(solution)/shard_map/ppermute | solution.py:479
  39.5 4.5 %collective-permute-done.9.first = f32[32,256]{1,0:T(8,128)S(1)} collective-permute-done((f32[32,256]{1,0:T(8,128)S(1)}, f32[32,256]{1,0:T(8,128)S(1)}, u32[]{:S(2)}, u32[]{:S(2)}) %collective-permute-start.9) | collective-permute-done | bytes 32800 | tf_op jit(solution)/shard_map/ppermute | solution.py:479
  44.4 2.7 %collective-permute-start.11 = (f32[352,128]{1,0:T(8,128)S(1)}, f32[352,128]{1,0:T(8,128)S(1)}, u32[]{:S(2)}, u32[]{:S(2)}) collective-permute-start(f32[352,128]{1,0:T(8,128)S(1)} %collective-permute-done.2.refs_0_), channel_id=1, source_target_pairs={{0,1},{1,0},{2,3},{3,2},{4,5},{5,4},{6,7},{7,6},{8,9},{9,8},{10,11... | collective-permute-start | bytes 540680 | tf_op jit(solution)/shard_map/ppermute | solution.py:489
  47.1 2.6 %collective-permute-start.14 = (f32[32,256]{1,0:T(8,128)S(1)}, f32[32,256]{1,0:T(8,128)S(1)}, u32[]{:S(2)}, u32[]{:S(2)}) collective-permute-start(f32[32,256]{1,0:T(8,128)S(1)} %get-tuple-element.534), channel_id=1, source_target_pairs={{4,8},{12,16},{20,24},{28,32},{36,40},{44,48},{52,56},{60,64},{68,... | collective-permute-start | bytes 98312 | tf_op jit(solution)/shard_map/ppermute | solution.py:479
  50.6 3.5 %collective-permute-done.14.first = f32[32,256]{1,0:T(8,128)S(1)} collective-permute-done((f32[32,256]{1,0:T(8,128)S(1)}, f32[32,256]{1,0:T(8,128)S(1)}, u32[]{:S(2)}, u32[]{:S(2)}) %collective-permute-start.14) | collective-permute-done | bytes 32800 | tf_op jit(solution)/shard_map/ppermute | solution.py:479
  54.9 2.7 %collective-permute-start.16 = (f32[32,512]{1,0:T(8,128)S(1)}, f32[32,512]{1,0:T(8,128)S(1)}, u32[]{:S(2)}, u32[]{:S(2)}) collective-permute-start(f32[32,512]{1,0:T(8,128)S(1)} %get-tuple-element.536.refs_0_.refs_4_), channel_id=1, source_target_pairs={{4,8},{12,16},{20,24},{28,32},{36,40},{44,48},{52,56},{60,64},{68,... | collective-permute-start | bytes 196616 | tf_op jit(solution)/shard_map/ppermute | solution.py:479
  58.4 2.6 %collective-permute-done.17.across = f32[32,256]{1,0:T(8,128)S(1)} collective-permute-done((f32[32,256]{1,0:T(8,128)S(1)}, f32[32,256]{1,0:T(8,128)S(1)}, u32[]{:S(2)}, u32[]{:S(2)}) %collective-permute-start.17) | collective-permute-done | bytes 32800 | tf_op jit(solution)/shard_map/ppermute | solution.py:485
  61.0 1.5 %collective-permute-done.16.whole = f32[32,512]{1,0:T(8,128)S(1)} collective-permute-done((f32[32,512]{1,0:T(8,128)S(1)}, f32[32,512]{1,0:T(8,128)S(1)}, u32[]{:S(2)}, u32[]{:S(2)}) %collective-permute-start.16) | collective-permute-done | bytes 65568 | tf_op jit(solution)/shard_map/ppermute | solution.py:479
  63.6 2.4 %collective-permute-done.19.second = f32[32,256]{1,0:T(8,128)S(1)} collective-permute-done((f32[32,256]{1,0:T(8,128)S(1)}, f32[32,256]{1,0:T(8,128)S(1)}, u32[]{:S(2)}, u32[]{:S(2)}) %collective-permute-start.19) | collective-permute-done | bytes 32800 | tf_op jit(solution)/shard_map/ppermute | solution.py:479
  66.5 2.5 %collective-permute-start.20 = (f32[32,512]{1,0:T(8,128)S(1)}, f32[32,512]{1,0:T(8,128)S(1)}, u32[]{:S(2)}, u32[]{:S(2)}) collective-permute-start(f32[32,512]{1,0:T(8,128)S(1)} %get-tuple-element.551.refs_0_.refs_6_), channel_id=1, source_target_pairs={{4,8},{12,16},{20,24},{28,32},{36,40},{44,48},{52,56},{60,64},{68,... | collective-permute-start | bytes 196616 | tf_op jit(solution)/shard_map/ppermute | solution.py:479
  69.4 3.2 %collective-permute-done.21.across = f32[32,256]{1,0:T(8,128)S(1)} collective-permute-done((f32[32,256]{1,0:T(8,128)S(1)}, f32[32,256]{1,0:T(8,128)S(1)}, u32[]{:S(2)}, u32[]{:S(2)}) %collective-permute-start.21) | collective-permute-done | bytes 32800 | tf_op jit(solution)/shard_map/ppermute | solution.py:485
  72.6 1.4 collective-permute-done.20.whole
  75.1 2.7 %collective-permute-done.23.second = f32[32,256]{1,0:T(8,128)S(1)} collective-permute-done((f32[32,256]{1,0:T(8,128)S(1)}, f32[32,256]{1,0:T(8,128)S(1)}, u32[]{:S(2)}, u32[]{:S(2)}) %collective-permute-start.23) | collective-permute-done | bytes 32800 | tf_op jit(solution)/shard_map/ppermute | solution.py:479
  78.3 2.5 %collective-permute-start.24 = (f32[32,512]{1,0:T(8,128)S(1)}, f32[32,512]{1,0:T(8,128)S(1)}, u32[]{:S(2)}, u32[]{:S(2)}) collective-permute-start(f32[32,512]{1,0:T(8,128)S(1)} %get-tuple-element.563.refs_0_.refs_8_), channel_id=1, source_target_pairs={{4,8},{12,16},{20,24},{28,32},{36,40},{44,48},{52,56},{60,64},{68,... | collective-permute-start | bytes 196616 | tf_op jit(solution)/shard_map/ppermute | solution.py:479
  81.2 3.2 %collective-permute-done.25.across = f32[32,256]{1,0:T(8,128)S(1)} collective-permute-done((f32[32,256]{1,0:T(8,128)S(1)}, f32[32,256]{1,0:T(8,128)S(1)}, u32[]{:S(2)}, u32[]{:S(2)}) %collective-permute-start.25) | collective-permute-done | bytes 32800 | tf_op jit(solution)/shard_map/ppermute | solution.py:485
  84.4 1.4 collective-permute-done.24.whole
  86.8 3.0 %collective-permute-done.27.second = f32[32,256]{1,0:T(8,128)S(1)} collective-permute-done((f32[32,256]{1,0:T(8,128)S(1)}, f32[32,256]{1,0:T(8,128)S(1)}, u32[]{:S(2)}, u32[]{:S(2)}) %collective-permute-start.27) | collective-permute-done | bytes 32800 | tf_op jit(solution)/shard_map/ppermute | solution.py:479
  90.4 2.4 %collective-permute-start.28 = (f32[32,512]{1,0:T(8,128)S(1)}, f32[32,512]{1,0:T(8,128)S(1)}, u32[]{:S(2)}, u32[]{:S(2)}) collective-permute-start(f32[32,512]{1,0:T(8,128)S(1)} %get-tuple-element.575.refs_0_.refs_10_), channel_id=1, source_target_pairs={{4,8},{12,16},{20,24},{28,32},{36,40},{44,48},{52,56},{60,64},{68,... | collective-permute-start | bytes 196616 | tf_op jit(solution)/shard_map/ppermute | solution.py:479
  93.2 3.2 %collective-permute-done.29.across = f32[32,256]{1,0:T(8,128)S(1)} collective-permute-done((f32[32,256]{1,0:T(8,128)S(1)}, f32[32,256]{1,0:T(8,128)S(1)}, u32[]{:S(2)}, u32[]{:S(2)}) %collective-permute-start.29) | collective-permute-done | bytes 32800 | tf_op jit(solution)/shard_map/ppermute | solution.py:485
  96.5 1.6 %collective-permute-done.28.whole = f32[32,512]{1,0:T(8,128)S(1)} collective-permute-done((f32[32,512]{1,0:T(8,128)S(1)}, f32[32,512]{1,0:T(8,128)S(1)}, u32[]{:S(2)}, u32[]{:S(2)}) %collective-permute-start.28) | collective-permute-done | bytes 65568 | tf_op jit(solution)/shard_map/ppermute | solution.py:479
  99.2 2.3 %collective-permute-done.31.second = f32[32,256]{1,0:T(8,128)S(1)} collective-permute-done((f32[32,256]{1,0:T(8,128)S(1)}, f32[32,256]{1,0:T(8,128)S(1)}, u32[]{:S(2)}, u32[]{:S(2)}) %collective-permute-start.31) | collective-permute-done | bytes 32800 | tf_op jit(solution)/shard_map/ppermute | solution.py:479
  103.4 11.2 %all_to_all.10.parts = f32[8,48,128]{2,1,0:T(8,128)S(1)} all-to-all(f32[8,48,128]{2,1,0:T(8,128)S(1)} %shard_map.86), channel_id=1, replica_groups={{0,32,64,96,128,160,192,224},{4,36,68,100,132,164,196,228},{8,40,72,104..., dimensions={0} | all-to-all | bytes 393216 | tf_op jit(solution)/shard_map/all_to_all | solution.py:471
  114.6 8.3 %all_to_all.11.parts = f32[8,48,128]{2,1,0:T(8,128)S(1)} all-to-all(f32[8,48,128]{2,1,0:T(8,128)S(1)} %shard_map.87), channel_id=1, replica_groups={{0,4,8,12,16,20,24,28},{32,36,40,44,48,52,56,60},{64,68,72,76,80,84,88,..., dimensions={0} | all-to-all | bytes 393216 | tf_op jit(solution)/shard_map/all_to_all | solution.py:471
  124.0 13.4 %collective-permute-start.32 = (f32[72,128]{1,0:T(8,128)S(1)}, f32[72,128]{1,0:T(8,128)S(1)}, u32[]{:S(2)}, u32[]{:S(2)}) collective-permute-start(f32[72,128]{1,0:T(8,128)S(1)} %get-tuple-element.615.other), channel_id=1, source_target_pairs={{0,1},{1,0},{2,3},{3,2},{4,5},{5,4},{6,7},{7,6},{8,9},{9,8},{10,11... | collective-permute-start | bytes 110600 | tf_op jit(solution)/shard_map/ppermute | solution.py:489
  (77 shorter events, 17.7 us)
Async XLA Ops:
  11.6 12.5 %collective-permute-start.3 = (f32[32,256]{1,0:T(8,128)S(1)}, f32[32,256]{1,0:T(8,128)S(1)}, u32[]{:S(2)}, u32[]{:S(2)}) collective-permute-start(f32[32,256]{1,0:T(8,128)S(1)} %get-tuple-element.503), channel_id=1, source_target_pairs={{4,8},{12,16},{20,24},{28,32},{36,40},{44,48},{52,56},{60,64},{68,... | collective-permute-start | bytes 98312 | tf_op jit(solution)/shard_map/ppermute | solution.py:479
  18.9 5.2 %collective-permute-start.4 = (f32[32,256]{1,0:T(8,128)S(1)}, f32[32,256]{1,0:T(8,128)S(1)}, u32[]{:S(2)}, u32[]{:S(2)}) collective-permute-start(f32[32,256]{1,0:T(8,128)S(1)} %get-tuple-element.504), channel_id=1, source_target_pairs={{0,4},{8,12},{16,20},{24,28},{32,36},{40,44},{48,52},{56,60},{64,6... | collective-permute-start | bytes 98312 | tf_op jit(solution)/shard_map/ppermute | solution.py:479
  22.4 22.0 %collective-permute-start.2 = (f32[352,128]{1,0:T(8,128)S(1)}, f32[352,128]{1,0:T(8,128)S(1)}, u32[]{:S(2)}, u32[]{:S(2)}) collective-permute-start(f32[352,128]{1,0:T(8,128)S(1)} %get-tuple-element.500), channel_id=1, source_target_pairs={{4,8},{12,16},{20,24},{28,32},{36,40},{44,48},{52,56},{60,64},{68,... | collective-permute-start | bytes 540680 | tf_op jit(solution)/shard_map/ppermute | solution.py:479
  24.5 8.6 %collective-permute-start.6 = (f32[32,256]{1,0:T(8,128)S(1)}, f32[32,256]{1,0:T(8,128)S(1)}, u32[]{:S(2)}, u32[]{:S(2)}) collective-permute-start(f32[32,256]{1,0:T(8,128)S(1)} %get-tuple-element.515), channel_id=1, source_target_pairs={{4,8},{12,16},{20,24},{28,32},{36,40},{44,48},{52,56},{60,64},{68,... | collective-permute-start | bytes 98312 | tf_op jit(solution)/shard_map/ppermute | solution.py:479
  28.6 4.4 %collective-permute-start.7 = (f32[32,256]{1,0:T(8,128)S(1)}, f32[32,256]{1,0:T(8,128)S(1)}, u32[]{:S(2)}, u32[]{:S(2)}) collective-permute-start(f32[32,256]{1,0:T(8,128)S(1)} %get-tuple-element.516), channel_id=1, source_target_pairs={{0,4},{8,12},{16,20},{24,28},{32,36},{40,44},{48,52},{56,60},{64,6... | collective-permute-start | bytes 98312 | tf_op jit(solution)/shard_map/ppermute | solution.py:479
  29.0 15.4 %collective-permute-start.5 = (f32[352,128]{1,0:T(8,128)S(1)}, f32[352,128]{1,0:T(8,128)S(1)}, u32[]{:S(2)}, u32[]{:S(2)}) collective-permute-start(f32[352,128]{1,0:T(8,128)S(1)} %get-tuple-element.512), channel_id=1, source_target_pairs={{4,8},{12,16},{20,24},{28,32},{36,40},{44,48},{52,56},{60,64},{68,... | collective-permute-start | bytes 540680 | tf_op jit(solution)/shard_map/ppermute | solution.py:479
  33.8 10.6 %collective-permute-start.8 = (f32[352,128]{1,0:T(8,128)S(1)}, f32[352,128]{1,0:T(8,128)S(1)}, u32[]{:S(2)}, u32[]{:S(2)}) collective-permute-start(f32[352,128]{1,0:T(8,128)S(1)} %get-tuple-element.521), channel_id=1, source_target_pairs={{4,8},{12,16},{20,24},{28,32},{36,40},{44,48},{52,56},{60,64},{68,... | collective-permute-start | bytes 540680 | tf_op jit(solution)/shard_map/ppermute | solution.py:479
  36.4 7.6 %collective-permute-start.9 = (f32[32,256]{1,0:T(8,128)S(1)}, f32[32,256]{1,0:T(8,128)S(1)}, u32[]{:S(2)}, u32[]{:S(2)}) collective-permute-start(f32[32,256]{1,0:T(8,128)S(1)} %get-tuple-element.523), channel_id=1, source_target_pairs={{4,8},{12,16},{20,24},{28,32},{36,40},{44,48},{52,56},{60,64},{68,... | collective-permute-start | bytes 98312 | tf_op jit(solution)/shard_map/ppermute | solution.py:479
  39.5 4.5 %collective-permute-start.10 = (f32[32,256]{1,0:T(8,128)S(1)}, f32[32,256]{1,0:T(8,128)S(1)}, u32[]{:S(2)}, u32[]{:S(2)}) collective-permute-start(f32[32,256]{1,0:T(8,128)S(1)} %get-tuple-element.524), channel_id=1, source_target_pairs={{0,4},{8,12},{16,20},{24,28},{32,36},{40,44},{48,52},{56,60},{64,6... | collective-permute-start | bytes 98312 | tf_op jit(solution)/shard_map/ppermute | solution.py:479
  44.4 10.5 %collective-permute-start.11 = (f32[352,128]{1,0:T(8,128)S(1)}, f32[352,128]{1,0:T(8,128)S(1)}, u32[]{:S(2)}, u32[]{:S(2)}) collective-permute-start(f32[352,128]{1,0:T(8,128)S(1)} %collective-permute-done.2.refs_0_), channel_id=1, source_target_pairs={{0,1},{1,0},{2,3},{3,2},{4,5},{5,4},{6,7},{7,6},{8,9},{9,8},{10,11... | collective-permute-start | bytes 540680 | tf_op jit(solution)/shard_map/ppermute | solution.py:489
  47.1 7.0 %collective-permute-start.14 = (f32[32,256]{1,0:T(8,128)S(1)}, f32[32,256]{1,0:T(8,128)S(1)}, u32[]{:S(2)}, u32[]{:S(2)}) collective-permute-start(f32[32,256]{1,0:T(8,128)S(1)} %get-tuple-element.534), channel_id=1, source_target_pairs={{4,8},{12,16},{20,24},{28,32},{36,40},{44,48},{52,56},{60,64},{68,... | collective-permute-start | bytes 98312 | tf_op jit(solution)/shard_map/ppermute | solution.py:479
  49.7 4.4 %collective-permute-start.15 = (f32[32,256]{1,0:T(8,128)S(1)}, f32[32,256]{1,0:T(8,128)S(1)}, u32[]{:S(2)}, u32[]{:S(2)}) collective-permute-start(f32[32,256]{1,0:T(8,128)S(1)} %get-tuple-element.535), channel_id=1, source_target_pairs={{0,4},{8,12},{16,20},{24,28},{32,36},{40,44},{48,52},{56,60},{64,6... | collective-permute-start | bytes 98312 | tf_op jit(solution)/shard_map/ppermute | solution.py:479
  49.7 8.2 %collective-permute-start.12 = (f32[352,128]{1,0:T(8,128)S(1)}, f32[352,128]{1,0:T(8,128)S(1)}, u32[]{:S(2)}, u32[]{:S(2)}) collective-permute-start(f32[352,128]{1,0:T(8,128)S(1)} %collective-permute-done.5.refs_1_), channel_id=1, source_target_pairs={{0,1},{1,0},{2,3},{3,2},{4,5},{5,4},{6,7},{7,6},{8,9},{9,8},{10,11... | collective-permute-start | bytes 540680 | tf_op jit(solution)/shard_map/ppermute | solution.py:489
  50.1 7.9 %collective-permute-start.13 = (f32[352,128]{1,0:T(8,128)S(1)}, f32[352,128]{1,0:T(8,128)S(1)}, u32[]{:S(2)}, u32[]{:S(2)}) collective-permute-start(f32[352,128]{1,0:T(8,128)S(1)} %collective-permute-done.8.refs_2_), channel_id=1, source_target_pairs={{0,1},{1,0},{2,3},{3,2},{4,5},{5,4},{6,7},{7,6},{8,9},{9,8},{10,11... | collective-permute-start | bytes 540680 | tf_op jit(solution)/shard_map/ppermute | solution.py:489
  54.5 3.9 %collective-permute-start.18 = (f32[32,256]{1,0:T(8,128)S(1)}, f32[32,256]{1,0:T(8,128)S(1)}, u32[]{:S(2)}, u32[]{:S(2)}) collective-permute-start(f32[32,256]{1,0:T(8,128)S(1)} %get-tuple-element.540), channel_id=1, source_target_pairs={{0,4},{8,12},{16,20},{24,28},{32,36},{40,44},{48,52},{56,60},{64,6... | collective-permute-start | bytes 98312 | tf_op jit(solution)/shard_map/ppermute | solution.py:479
  54.6 6.3 %collective-permute-start.17 = (f32[32,256]{1,0:T(8,128)S(1)}, f32[32,256]{1,0:T(8,128)S(1)}, u32[]{:S(2)}, u32[]{:S(2)}) collective-permute-start(f32[32,256]{1,0:T(8,128)S(1)} %get-tuple-element.540), channel_id=1, source_target_pairs={{0,8},{4,252},{8,16},{12,4},{16,24},{20,12},{24,32},{28,20},{32,40... | collective-permute-start | bytes 98312 | tf_op jit(solution)/shard_map/ppermute | solution.py:485
  54.9 7.6 %collective-permute-start.16 = (f32[32,512]{1,0:T(8,128)S(1)}, f32[32,512]{1,0:T(8,128)S(1)}, u32[]{:S(2)}, u32[]{:S(2)}) collective-permute-start(f32[32,512]{1,0:T(8,128)S(1)} %get-tuple-element.536.refs_0_.refs_4_), channel_id=1, source_target_pairs={{4,8},{12,16},{20,24},{28,32},{36,40},{44,48},{52,56},{60,64},{68,... | collective-permute-start | bytes 196616 | tf_op jit(solution)/shard_map/ppermute | solution.py:479
  63.1 2.8 %collective-permute-start.19 = (f32[32,256]{1,0:T(8,128)S(1)}, f32[32,256]{1,0:T(8,128)S(1)}, u32[]{:S(2)}, u32[]{:S(2)}) collective-permute-start(f32[32,256]{1,0:T(8,128)S(1)} %get-tuple-element.550), channel_id=1, source_target_pairs={{0,4},{8,12},{16,20},{24,28},{32,36},{40,44},{48,52},{56,60},{64,6... | collective-permute-start | bytes 98312 | tf_op jit(solution)/shard_map/ppermute | solution.py:479
  66.4 3.1 %collective-permute-start.22 = (f32[32,256]{1,0:T(8,128)S(1)}, f32[32,256]{1,0:T(8,128)S(1)}, u32[]{:S(2)}, u32[]{:S(2)}) collective-permute-start(f32[32,256]{1,0:T(8,128)S(1)} %get-tuple-element.555), channel_id=1, source_target_pairs={{0,4},{8,12},{16,20},{24,28},{32,36},{40,44},{48,52},{56,60},{64,6... | collective-permute-start | bytes 98312 | tf_op jit(solution)/shard_map/ppermute | solution.py:479
  66.5 6.2 %collective-permute-start.21 = (f32[32,256]{1,0:T(8,128)S(1)}, f32[32,256]{1,0:T(8,128)S(1)}, u32[]{:S(2)}, u32[]{:S(2)}) collective-permute-start(f32[32,256]{1,0:T(8,128)S(1)} %get-tuple-element.555), channel_id=1, source_target_pairs={{0,8},{4,252},{8,16},{12,4},{16,24},{20,12},{24,32},{28,20},{32,40... | collective-permute-start | bytes 98312 | tf_op jit(solution)/shard_map/ppermute | solution.py:485
  66.5 7.4 %collective-permute-start.20 = (f32[32,512]{1,0:T(8,128)S(1)}, f32[32,512]{1,0:T(8,128)S(1)}, u32[]{:S(2)}, u32[]{:S(2)}) collective-permute-start(f32[32,512]{1,0:T(8,128)S(1)} %get-tuple-element.551.refs_0_.refs_6_), channel_id=1, source_target_pairs={{4,8},{12,16},{20,24},{28,32},{36,40},{44,48},{52,56},{60,64},{68,... | collective-permute-start | bytes 196616 | tf_op jit(solution)/shard_map/ppermute | solution.py:479
  74.6 3.1 %collective-permute-start.23 = (f32[32,256]{1,0:T(8,128)S(1)}, f32[32,256]{1,0:T(8,128)S(1)}, u32[]{:S(2)}, u32[]{:S(2)}) collective-permute-start(f32[32,256]{1,0:T(8,128)S(1)} %get-tuple-element.562), channel_id=1, source_target_pairs={{0,4},{8,12},{16,20},{24,28},{32,36},{40,44},{48,52},{56,60},{64,6... | collective-permute-start | bytes 98312 | tf_op jit(solution)/shard_map/ppermute | solution.py:479
  78.1 3.1 %collective-permute-start.26 = (f32[32,256]{1,0:T(8,128)S(1)}, f32[32,256]{1,0:T(8,128)S(1)}, u32[]{:S(2)}, u32[]{:S(2)}) collective-permute-start(f32[32,256]{1,0:T(8,128)S(1)} %get-tuple-element.567), channel_id=1, source_target_pairs={{0,4},{8,12},{16,20},{24,28},{32,36},{40,44},{48,52},{56,60},{64,6... | collective-permute-start | bytes 98312 | tf_op jit(solution)/shard_map/ppermute | solution.py:479
  78.2 6.2 %collective-permute-start.25 = (f32[32,256]{1,0:T(8,128)S(1)}, f32[32,256]{1,0:T(8,128)S(1)}, u32[]{:S(2)}, u32[]{:S(2)}) collective-permute-start(f32[32,256]{1,0:T(8,128)S(1)} %get-tuple-element.567), channel_id=1, source_target_pairs={{0,8},{4,252},{8,16},{12,4},{16,24},{20,12},{24,32},{28,20},{32,40... | collective-permute-start | bytes 98312 | tf_op jit(solution)/shard_map/ppermute | solution.py:485
  78.3 7.4 %collective-permute-start.24 = (f32[32,512]{1,0:T(8,128)S(1)}, f32[32,512]{1,0:T(8,128)S(1)}, u32[]{:S(2)}, u32[]{:S(2)}) collective-permute-start(f32[32,512]{1,0:T(8,128)S(1)} %get-tuple-element.563.refs_0_.refs_8_), channel_id=1, source_target_pairs={{4,8},{12,16},{20,24},{28,32},{36,40},{44,48},{52,56},{60,64},{68,... | collective-permute-start | bytes 196616 | tf_op jit(solution)/shard_map/ppermute | solution.py:479
  86.4 3.5 %collective-permute-start.27 = (f32[32,256]{1,0:T(8,128)S(1)}, f32[32,256]{1,0:T(8,128)S(1)}, u32[]{:S(2)}, u32[]{:S(2)}) collective-permute-start(f32[32,256]{1,0:T(8,128)S(1)} %get-tuple-element.574), channel_id=1, source_target_pairs={{0,4},{8,12},{16,20},{24,28},{32,36},{40,44},{48,52},{56,60},{64,6... | collective-permute-start | bytes 98312 | tf_op jit(solution)/shard_map/ppermute | solution.py:479
  90.2 3.0 %collective-permute-start.30 = (f32[32,256]{1,0:T(8,128)S(1)}, f32[32,256]{1,0:T(8,128)S(1)}, u32[]{:S(2)}, u32[]{:S(2)}) collective-permute-start(f32[32,256]{1,0:T(8,128)S(1)} %get-tuple-element.579), channel_id=1, source_target_pairs={{0,4},{8,12},{16,20},{24,28},{32,36},{40,44},{48,52},{56,60},{64,6... | collective-permute-start | bytes 98312 | tf_op jit(solution)/shard_map/ppermute | solution.py:479
  90.3 6.2 %collective-permute-start.29 = (f32[32,256]{1,0:T(8,128)S(1)}, f32[32,256]{1,0:T(8,128)S(1)}, u32[]{:S(2)}, u32[]{:S(2)}) collective-permute-start(f32[32,256]{1,0:T(8,128)S(1)} %get-tuple-element.579), channel_id=1, source_target_pairs={{0,8},{4,252},{8,16},{12,4},{16,24},{20,12},{24,32},{28,20},{32,40... | collective-permute-start | bytes 98312 | tf_op jit(solution)/shard_map/ppermute | solution.py:485
  90.4 7.7 %collective-permute-start.28 = (f32[32,512]{1,0:T(8,128)S(1)}, f32[32,512]{1,0:T(8,128)S(1)}, u32[]{:S(2)}, u32[]{:S(2)}) collective-permute-start(f32[32,512]{1,0:T(8,128)S(1)} %get-tuple-element.575.refs_0_.refs_10_), channel_id=1, source_target_pairs={{4,8},{12,16},{20,24},{28,32},{36,40},{44,48},{52,56},{60,64},{68,... | collective-permute-start | bytes 196616 | tf_op jit(solution)/shard_map/ppermute | solution.py:479
  98.7 2.8 %collective-permute-start.31 = (f32[32,256]{1,0:T(8,128)S(1)}, f32[32,256]{1,0:T(8,128)S(1)}, u32[]{:S(2)}, u32[]{:S(2)}) collective-permute-start(f32[32,256]{1,0:T(8,128)S(1)} %get-tuple-element.586), channel_id=1, source_target_pairs={{0,4},{8,12},{16,20},{24,28},{32,36},{40,44},{48,52},{56,60},{64,6... | collective-permute-start | bytes 98312 | tf_op jit(solution)/shard_map/ppermute | solution.py:479
  103.3 36.3 %copy-start.1 = (s32[1,2,2]{2,1,0:T(2,128)S(1)}, s32[1,2,2]{2,1,0:T(2,128)}, u32[]{:S(2)}) copy-start(s32[1,2,2]{2,1,0:T(2,128)} %param.17) | copy-start | bytes 52
  124.0 14.3 %collective-permute-start.32 = (f32[72,128]{1,0:T(8,128)S(1)}, f32[72,128]{1,0:T(8,128)S(1)}, u32[]{:S(2)}, u32[]{:S(2)}) collective-permute-start(f32[72,128]{1,0:T(8,128)S(1)} %get-tuple-element.615.other), channel_id=1, source_target_pairs={{0,1},{1,0},{2,3},{3,2},{4,5},{5,4},{6,7},{7,6},{8,9},{9,8},{10,11... | collective-permute-start | bytes 110600 | tf_op jit(solution)/shard_map/ppermute | solution.py:489
  (5 other events, 110.0 us)

commit v3 on v2

--- a/solution.py
+++ b/solution.py
@@ -580,13 +580,14 @@
 
     shared = []
     for power in range(SINGLE):
-        if power < CHUNKS:
-            chunk, partial = lax.optimization_barrier((chunks[power], own_part(sends[0])))
-            shared.append(swapped(chunk, 1))
-        else:
+        if power == SINGLE - 1:
             shared, sends[0] = lax.optimization_barrier((shared, sends[0]))
             others = [core_swapped(chunk) for chunk in shared]
-            partial = own_part(sends[0])
+        partial = own_part(sends[0])
+        if power < 2:
+            due = chunks[:1] if power == 0 else chunks[1:]
+            due, partial = lax.optimization_barrier((due, partial))
+            shared += [swapped(chunk, 1) for chunk in due]
         sends = stepped(partial, swapped(sends[1], 1), swapped(sends[2], 0))
     *ghost_operator, partner_masks = call(
         ghost_kernel,

time: 141 us -> 147 us (1.043)
  waiting for transfers between devices: 39.8 us -> 44.1 us
  starting transfers between devices: 50.9 us -> 52.9 us
    ppermute x23, waiting for transfers between devices: 26.7 us -> 30.2 us  [swapped(): return lax.ppermute(value, 'sub', pairs + [(j, i) for i, j in pairs])]
    ppermute x4, starting transfers between devices: 16.6 us -> 19.4 us  [core_swapped(): return lax.ppermute(value, 'fold', [(0, 1), (1, 0), (2, 3), (3, 2)])]
where the time goes in v3:
time: 147 us; the launch traced here: 146 us
  starting transfers between devices  52.9 us (36%)
  waiting for transfers between devices  44.1 us (30%)
  blocking collectives  29.6 us (20%)
  Pallas kernels  17.6 us (12%)
  between operations  1.63 us (1%)
    ppermute x23, starting transfers between devices, swapped(): return lax.ppermute(value, 'sub', pairs + [(j, i) for i, j in pairs])  33 us
    ppermute x23, waiting for transfers between devices, swapped(): return lax.ppermute(value, 'sub', pairs + [(j, i) for i, j in pairs])  30.2 us
    ppermute x4, starting transfers between devices, core_swapped(): return lax.ppermute(value, 'fold', [(0, 1), (1, 0), (2, 3), (3, 2)])  19.4 us
    all_to_all x2, blocking collectives, exchanged(): return lax.all_to_all(value, 'sub', 0, 0, axis_index_groups=groups)  19.4 us
    pallas_call x31, Pallas kernels, call(): pl.pallas_call(kernel, out_shape=out_shape, in_specs=[SMEM] * len(smem) +...  17.6 us
    ppermute x4, waiting for transfers between devices, sent_across(): return lax.ppermute(value, 'sub', pairs)  13.1 us
    all_gather x1, blocking collectives, on_device(): gathered = lax.all_gather(right_side.T, 'fold', axis=1, tiled=True)  10.2 us
  transfers between devices with their start and end apart: 31, of which 16 were waited for; matrix products, arithmetic and copies ran while one was open for 0% of the time, Pallas kernels for 7%

profile of v3, /device:TPU:1, one launch (start us, length us, event | category | flops | bytes accessed | tf_op | source)
XLA Modules:
  0.0 146.5 jit_solution(3050111703729973855)
XLA Ops:
  0.6 10.2 %all_gather.6.gathered = f32[64,512]{1,0:T(8,128)S(1)} all-gather(f32[64,128]{1,0:T(8,128)} %bitcast.228), channel_id=1, replica_groups=mesh['sub'=64,'fold'=4] {'fold'}, dimensions={1}, use_global_device_ids=true | all-gather | bytes 163840 | tf_op jit(solution)/shard_map/all_gather | solution.py:540
  11.6 7.3 %collective-permute-start.3 = (f32[32,256]{1,0:T(8,128)S(1)}, f32[32,256]{1,0:T(8,128)S(1)}, u32[]{:S(2)}, u32[]{:S(2)}) collective-permute-start(f32[32,256]{1,0:T(8,128)S(1)} %get-tuple-element.503), channel_id=1, source_target_pairs={{4,8},{12,16},{20,24},{28,32},{36,40},{44,48},{52,56},{60,64},{68,... | collective-permute-start | bytes 98312 | tf_op jit(solution)/shard_map/ppermute | solution.py:479
  18.9 3.2 %shard_map.60 = (bf16[512,512]{1,0:T(8,128)(2,1)S(1)}, bf16[512,512]{1,0:T(8,128)(2,1)S(1)}, bf16[512,512]{1,0:T(8,128)(2,1)S(1)}, bf16[512,512]{1,0:T(8,128)(2,...) custom-call(s32[4,7]{1,0:T(4,128)} %cols.1, ...), custom_call_target="tpu_custom_call" | custom-call | flops 1000000000 | bytes 1048576 | tf_op jit(solution)/shard_map/pallas_call | solution.py:458
  22.4 1.6 %collective-permute-start.2 = (f32[352,128]{1,0:T(8,128)S(1)}, f32[352,128]{1,0:T(8,128)S(1)}, u32[]{:S(2)}, u32[]{:S(2)}) collective-permute-start(f32[352,128]{1,0:T(8,128)S(1)} %get-tuple-element.499), channel_id=1, source_target_pairs={{4,8},{12,16},{20,24},{28,32},{36,40},{44,48},{52,56},{60,64},{68,... | collective-permute-start | bytes 540680 | tf_op jit(solution)/shard_map/ppermute | solution.py:479
  24.8 4.1 %collective-permute-start.5 = (f32[352,128]{1,0:T(8,128)S(1)}, f32[352,128]{1,0:T(8,128)S(1)}, u32[]{:S(2)}, u32[]{:S(2)}) collective-permute-start(f32[352,128]{1,0:T(8,128)S(1)} %get-tuple-element.512), channel_id=1, source_target_pairs={{4,8},{12,16},{20,24},{28,32},{36,40},{44,48},{52,56},{60,64},{68,... | collective-permute-start | bytes 540680 | tf_op jit(solution)/shard_map/ppermute | solution.py:479
  28.9 1.6 %collective-permute-start.6 = (f32[352,128]{1,0:T(8,128)S(1)}, f32[352,128]{1,0:T(8,128)S(1)}, u32[]{:S(2)}, u32[]{:S(2)}) collective-permute-start(f32[352,128]{1,0:T(8,128)S(1)} %get-tuple-element.513), channel_id=1, source_target_pairs={{4,8},{12,16},{20,24},{28,32},{36,40},{44,48},{52,56},{60,64},{68,... | collective-permute-start | bytes 540680 | tf_op jit(solution)/shard_map/ppermute | solution.py:479
  30.5 4.0 %collective-permute-start.7 = (f32[32,256]{1,0:T(8,128)S(1)}, f32[32,256]{1,0:T(8,128)S(1)}, u32[]{:S(2)}, u32[]{:S(2)}) collective-permute-start(f32[32,256]{1,0:T(8,128)S(1)} %get-tuple-element.515), channel_id=1, source_target_pairs={{4,8},{12,16},{20,24},{28,32},{36,40},{44,48},{52,56},{60,64},{68,... | collective-permute-start | bytes 98312 | tf_op jit(solution)/shard_map/ppermute | solution.py:479
  34.6 6.2 %collective-permute-done.7.first = f32[32,256]{1,0:T(8,128)S(1)} collective-permute-done((f32[32,256]{1,0:T(8,128)S(1)}, f32[32,256]{1,0:T(8,128)S(1)}, u32[]{:S(2)}, u32[]{:S(2)}) %collective-permute-start.7) | collective-permute-done | bytes 32800 | tf_op jit(solution)/shard_map/ppermute | solution.py:479
  41.2 2.4 %collective-permute-start.9 = (f32[32,256]{1,0:T(8,128)S(1)}, f32[32,256]{1,0:T(8,128)S(1)}, u32[]{:S(2)}, u32[]{:S(2)}) collective-permute-start(f32[32,256]{1,0:T(8,128)S(1)} %get-tuple-element.521), channel_id=1, source_target_pairs={{4,8},{12,16},{20,24},{28,32},{36,40},{44,48},{52,56},{60,64},{68,... | collective-permute-start | bytes 98312 | tf_op jit(solution)/shard_map/ppermute | solution.py:479
  43.9 4.3 %collective-permute-done.9.first = f32[32,256]{1,0:T(8,128)S(1)} collective-permute-done((f32[32,256]{1,0:T(8,128)S(1)}, f32[32,256]{1,0:T(8,128)S(1)}, u32[]{:S(2)}, u32[]{:S(2)}) %collective-permute-start.9) | collective-permute-done | bytes 32800 | tf_op jit(solution)/shard_map/ppermute | solution.py:479
  48.7 3.8 %collective-permute-start.11 = (f32[352,128]{1,0:T(8,128)S(1)}, f32[352,128]{1,0:T(8,128)S(1)}, u32[]{:S(2)}, u32[]{:S(2)}) collective-permute-start(f32[352,128]{1,0:T(8,128)S(1)} %collective-permute-done.2.refs_0_), channel_id=1, source_target_pairs={{0,1},{1,0},{2,3},{3,2},{4,5},{5,4},{6,7},{7,6},{8,9},{9,8},{10,11... | collective-permute-start | bytes 540680 | tf_op jit(solution)/shard_map/ppermute | solution.py:489
  52.5 1.8 %collective-permute-start.14 = (f32[32,256]{1,0:T(8,128)S(1)}, f32[32,256]{1,0:T(8,128)S(1)}, u32[]{:S(2)}, u32[]{:S(2)}) collective-permute-start(f32[32,256]{1,0:T(8,128)S(1)} %get-tuple-element.532), channel_id=1, source_target_pairs={{4,8},{12,16},{20,24},{28,32},{36,40},{44,48},{52,56},{60,64},{68,... | collective-permute-start | bytes 98312 | tf_op jit(solution)/shard_map/ppermute | solution.py:479
  55.1 4.4 %collective-permute-done.14.first = f32[32,256]{1,0:T(8,128)S(1)} collective-permute-done((f32[32,256]{1,0:T(8,128)S(1)}, f32[32,256]{1,0:T(8,128)S(1)}, u32[]{:S(2)}, u32[]{:S(2)}) %collective-permute-start.14) | collective-permute-done | bytes 32800 | tf_op jit(solution)/shard_map/ppermute | solution.py:479
  60.3 1.8 %collective-permute-start.16 = (f32[32,512]{1,0:T(8,128)S(1)}, f32[32,512]{1,0:T(8,128)S(1)}, u32[]{:S(2)}, u32[]{:S(2)}) collective-permute-start(f32[32,512]{1,0:T(8,128)S(1)} %get-tuple-element.534.refs_0_.refs_4_), channel_id=1, source_target_pairs={{4,8},{12,16},{20,24},{28,32},{36,40},{44,48},{52,56},{60,64},{68,... | collective-permute-start | bytes 196616 | tf_op jit(solution)/shard_map/ppermute | solution.py:479
  62.9 3.4 %collective-permute-done.17.across = f32[32,256]{1,0:T(8,128)S(1)} collective-permute-done((f32[32,256]{1,0:T(8,128)S(1)}, f32[32,256]{1,0:T(8,128)S(1)}, u32[]{:S(2)}, u32[]{:S(2)}) %collective-permute-start.17) | collective-permute-done | bytes 32800 | tf_op jit(solution)/shard_map/ppermute | solution.py:485
  66.3 1.4 collective-permute-done.16.whole
  68.8 2.4 %collective-permute-done.19.second = f32[32,256]{1,0:T(8,128)S(1)} collective-permute-done((f32[32,256]{1,0:T(8,128)S(1)}, f32[32,256]{1,0:T(8,128)S(1)}, u32[]{:S(2)}, u32[]{:S(2)}) %collective-permute-start.19) | collective-permute-done | bytes 32800 | tf_op jit(solution)/shard_map/ppermute | solution.py:479
  71.7 2.4 %collective-permute-start.20 = (f32[32,512]{1,0:T(8,128)S(1)}, f32[32,512]{1,0:T(8,128)S(1)}, u32[]{:S(2)}, u32[]{:S(2)}) collective-permute-start(f32[32,512]{1,0:T(8,128)S(1)} %get-tuple-element.549.refs_0_.refs_6_), channel_id=1, source_target_pairs={{4,8},{12,16},{20,24},{28,32},{36,40},{44,48},{52,56},{60,64},{68,... | collective-permute-start | bytes 196616 | tf_op jit(solution)/shard_map/ppermute | solution.py:479
  74.5 3.3 %collective-permute-done.21.across = f32[32,256]{1,0:T(8,128)S(1)} collective-permute-done((f32[32,256]{1,0:T(8,128)S(1)}, f32[32,256]{1,0:T(8,128)S(1)}, u32[]{:S(2)}, u32[]{:S(2)}) %collective-permute-start.21) | collective-permute-done | bytes 32800 | tf_op jit(solution)/shard_map/ppermute | solution.py:485
  77.8 1.4 collective-permute-done.20.whole
  80.3 2.7 %collective-permute-done.23.second = f32[32,256]{1,0:T(8,128)S(1)} collective-permute-done((f32[32,256]{1,0:T(8,128)S(1)}, f32[32,256]{1,0:T(8,128)S(1)}, u32[]{:S(2)}, u32[]{:S(2)}) %collective-permute-start.23) | collective-permute-done | bytes 32800 | tf_op jit(solution)/shard_map/ppermute | solution.py:479
  83.5 2.5 %collective-permute-start.24 = (f32[32,512]{1,0:T(8,128)S(1)}, f32[32,512]{1,0:T(8,128)S(1)}, u32[]{:S(2)}, u32[]{:S(2)}) collective-permute-start(f32[32,512]{1,0:T(8,128)S(1)} %get-tuple-element.561.refs_0_.refs_8_), channel_id=1, source_target_pairs={{4,8},{12,16},{20,24},{28,32},{36,40},{44,48},{52,56},{60,64},{68,... | collective-permute-start | bytes 196616 | tf_op jit(solution)/shard_map/ppermute | solution.py:479
  86.3 3.2 %collective-permute-done.25.across = f32[32,256]{1,0:T(8,128)S(1)} collective-permute-done((f32[32,256]{1,0:T(8,128)S(1)}, f32[32,256]{1,0:T(8,128)S(1)}, u32[]{:S(2)}, u32[]{:S(2)}) %collective-permute-start.25) | collective-permute-done | bytes 32800 | tf_op jit(solution)/shard_map/ppermute | solution.py:485
  89.6 1.4 collective-permute-done.24.whole
  92.1 2.4 %collective-permute-done.27.second = f32[32,256]{1,0:T(8,128)S(1)} collective-permute-done((f32[32,256]{1,0:T(8,128)S(1)}, f32[32,256]{1,0:T(8,128)S(1)}, u32[]{:S(2)}, u32[]{:S(2)}) %collective-permute-start.27) | collective-permute-done | bytes 32800 | tf_op jit(solution)/shard_map/ppermute | solution.py:479
  95.2 2.5 %collective-permute-start.28 = (f32[32,512]{1,0:T(8,128)S(1)}, f32[32,512]{1,0:T(8,128)S(1)}, u32[]{:S(2)}, u32[]{:S(2)}) collective-permute-start(f32[32,512]{1,0:T(8,128)S(1)} %get-tuple-element.573.refs_0_.refs_10_), channel_id=1, source_target_pairs={{4,8},{12,16},{20,24},{28,32},{36,40},{44,48},{52,56},{60,64},{68,... | collective-permute-start | bytes 196616 | tf_op jit(solution)/shard_map/ppermute | solution.py:479
  98.1 3.2 %collective-permute-done.29.across = f32[32,256]{1,0:T(8,128)S(1)} collective-permute-done((f32[32,256]{1,0:T(8,128)S(1)}, f32[32,256]{1,0:T(8,128)S(1)}, u32[]{:S(2)}, u32[]{:S(2)}) %collective-permute-start.29) | collective-permute-done | bytes 32800 | tf_op jit(solution)/shard_map/ppermute | solution.py:485
  101.3 1.3 collective-permute-done.28.whole
  103.8 2.3 %collective-permute-done.31.second = f32[32,256]{1,0:T(8,128)S(1)} collective-permute-done((f32[32,256]{1,0:T(8,128)S(1)}, f32[32,256]{1,0:T(8,128)S(1)}, u32[]{:S(2)}, u32[]{:S(2)}) %collective-permute-start.31) | collective-permute-done | bytes 32800 | tf_op jit(solution)/shard_map/ppermute | solution.py:479
  107.9 11.2 %all_to_all.10.parts = f32[8,48,128]{2,1,0:T(8,128)S(1)} all-to-all(f32[8,48,128]{2,1,0:T(8,128)S(1)} %shard_map.86), channel_id=1, replica_groups={{0,32,64,96,128,160,192,224},{4,36,68,100,132,164,196,228},{8,40,72,104..., dimensions={0} | all-to-all | bytes 393216 | tf_op jit(solution)/shard_map/all_to_all | solution.py:471
  119.1 8.2 %all_to_all.11.parts = f32[8,48,128]{2,1,0:T(8,128)S(1)} all-to-all(f32[8,48,128]{2,1,0:T(8,128)S(1)} %shard_map.87), channel_id=1, replica_groups={{0,4,8,12,16,20,24,28},{32,36,40,44,48,52,56,60},{64,68,72,76,80,84,88,..., dimensions={0} | all-to-all | bytes 393216 | tf_op jit(solution)/shard_map/all_to_all | solution.py:471
  128.5 15.1 %collective-permute-start.32 = (f32[72,128]{1,0:T(8,128)S(1)}, f32[72,128]{1,0:T(8,128)S(1)}, u32[]{:S(2)}, u32[]{:S(2)}) collective-permute-start(f32[72,128]{1,0:T(8,128)S(1)} %get-tuple-element.613.other), channel_id=1, source_target_pairs={{0,1},{1,0},{2,3},{3,2},{4,5},{5,4},{6,7},{7,6},{8,9},{9,8},{10,11... | collective-permute-start | bytes 110600 | tf_op jit(solution)/shard_map/ppermute | solution.py:489
  (77 shorter events, 17.9 us)
Async XLA Ops:
  11.6 12.5 %collective-permute-start.3 = (f32[32,256]{1,0:T(8,128)S(1)}, f32[32,256]{1,0:T(8,128)S(1)}, u32[]{:S(2)}, u32[]{:S(2)}) collective-permute-start(f32[32,256]{1,0:T(8,128)S(1)} %get-tuple-element.503), channel_id=1, source_target_pairs={{4,8},{12,16},{20,24},{28,32},{36,40},{44,48},{52,56},{60,64},{68,... | collective-permute-start | bytes 98312 | tf_op jit(solution)/shard_map/ppermute | solution.py:479
  18.9 5.2 %collective-permute-start.4 = (f32[32,256]{1,0:T(8,128)S(1)}, f32[32,256]{1,0:T(8,128)S(1)}, u32[]{:S(2)}, u32[]{:S(2)}) collective-permute-start(f32[32,256]{1,0:T(8,128)S(1)} %get-tuple-element.504), channel_id=1, source_target_pairs={{0,4},{8,12},{16,20},{24,28},{32,36},{40,44},{48,52},{56,60},{64,6... | collective-permute-start | bytes 98312 | tf_op jit(solution)/shard_map/ppermute | solution.py:479
  22.4 26.2 %collective-permute-start.2 = (f32[352,128]{1,0:T(8,128)S(1)}, f32[352,128]{1,0:T(8,128)S(1)}, u32[]{:S(2)}, u32[]{:S(2)}) collective-permute-start(f32[352,128]{1,0:T(8,128)S(1)} %get-tuple-element.499), channel_id=1, source_target_pairs={{4,8},{12,16},{20,24},{28,32},{36,40},{44,48},{52,56},{60,64},{68,... | collective-permute-start | bytes 540680 | tf_op jit(solution)/shard_map/ppermute | solution.py:479
  24.8 23.8 %collective-permute-start.5 = (f32[352,128]{1,0:T(8,128)S(1)}, f32[352,128]{1,0:T(8,128)S(1)}, u32[]{:S(2)}, u32[]{:S(2)}) collective-permute-start(f32[352,128]{1,0:T(8,128)S(1)} %get-tuple-element.512), channel_id=1, source_target_pairs={{4,8},{12,16},{20,24},{28,32},{36,40},{44,48},{52,56},{60,64},{68,... | collective-permute-start | bytes 540680 | tf_op jit(solution)/shard_map/ppermute | solution.py:479
  28.9 19.8 %collective-permute-start.6 = (f32[352,128]{1,0:T(8,128)S(1)}, f32[352,128]{1,0:T(8,128)S(1)}, u32[]{:S(2)}, u32[]{:S(2)}) collective-permute-start(f32[352,128]{1,0:T(8,128)S(1)} %get-tuple-element.513), channel_id=1, source_target_pairs={{4,8},{12,16},{20,24},{28,32},{36,40},{44,48},{52,56},{60,64},{68,... | collective-permute-start | bytes 540680 | tf_op jit(solution)/shard_map/ppermute | solution.py:479
  30.5 10.3 %collective-permute-start.7 = (f32[32,256]{1,0:T(8,128)S(1)}, f32[32,256]{1,0:T(8,128)S(1)}, u32[]{:S(2)}, u32[]{:S(2)}) collective-permute-start(f32[32,256]{1,0:T(8,128)S(1)} %get-tuple-element.515), channel_id=1, source_target_pairs={{4,8},{12,16},{20,24},{28,32},{36,40},{44,48},{52,56},{60,64},{68,... | collective-permute-start | bytes 98312 | tf_op jit(solution)/shard_map/ppermute | solution.py:479
  34.6 6.2 %collective-permute-start.8 = (f32[32,256]{1,0:T(8,128)S(1)}, f32[32,256]{1,0:T(8,128)S(1)}, u32[]{:S(2)}, u32[]{:S(2)}) collective-permute-start(f32[32,256]{1,0:T(8,128)S(1)} %get-tuple-element.516), channel_id=1, source_target_pairs={{0,4},{8,12},{16,20},{24,28},{32,36},{40,44},{48,52},{56,60},{64,6... | collective-permute-start | bytes 98312 | tf_op jit(solution)/shard_map/ppermute | solution.py:479
  41.2 7.1 %collective-permute-start.9 = (f32[32,256]{1,0:T(8,128)S(1)}, f32[32,256]{1,0:T(8,128)S(1)}, u32[]{:S(2)}, u32[]{:S(2)}) collective-permute-start(f32[32,256]{1,0:T(8,128)S(1)} %get-tuple-element.521), channel_id=1, source_target_pairs={{4,8},{12,16},{20,24},{28,32},{36,40},{44,48},{52,56},{60,64},{68,... | collective-permute-start | bytes 98312 | tf_op jit(solution)/shard_map/ppermute | solution.py:479
  43.5 4.7 %collective-permute-start.10 = (f32[32,256]{1,0:T(8,128)S(1)}, f32[32,256]{1,0:T(8,128)S(1)}, u32[]{:S(2)}, u32[]{:S(2)}) collective-permute-start(f32[32,256]{1,0:T(8,128)S(1)} %get-tuple-element.522), channel_id=1, source_target_pairs={{0,4},{8,12},{16,20},{24,28},{32,36},{40,44},{48,52},{56,60},{64,6... | collective-permute-start | bytes 98312 | tf_op jit(solution)/shard_map/ppermute | solution.py:479
  48.7 11.6 %collective-permute-start.11 = (f32[352,128]{1,0:T(8,128)S(1)}, f32[352,128]{1,0:T(8,128)S(1)}, u32[]{:S(2)}, u32[]{:S(2)}) collective-permute-start(f32[352,128]{1,0:T(8,128)S(1)} %collective-permute-done.2.refs_0_), channel_id=1, source_target_pairs={{0,1},{1,0},{2,3},{3,2},{4,5},{5,4},{6,7},{7,6},{8,9},{9,8},{10,11... | collective-permute-start | bytes 540680 | tf_op jit(solution)/shard_map/ppermute | solution.py:489
  52.5 7.0 %collective-permute-start.14 = (f32[32,256]{1,0:T(8,128)S(1)}, f32[32,256]{1,0:T(8,128)S(1)}, u32[]{:S(2)}, u32[]{:S(2)}) collective-permute-start(f32[32,256]{1,0:T(8,128)S(1)} %get-tuple-element.532), channel_id=1, source_target_pairs={{4,8},{12,16},{20,24},{28,32},{36,40},{44,48},{52,56},{60,64},{68,... | collective-permute-start | bytes 98312 | tf_op jit(solution)/shard_map/ppermute | solution.py:479
  54.2 5.2 %collective-permute-start.15 = (f32[32,256]{1,0:T(8,128)S(1)}, f32[32,256]{1,0:T(8,128)S(1)}, u32[]{:S(2)}, u32[]{:S(2)}) collective-permute-start(f32[32,256]{1,0:T(8,128)S(1)} %get-tuple-element.533), channel_id=1, source_target_pairs={{0,4},{8,12},{16,20},{24,28},{32,36},{40,44},{48,52},{56,60},{64,6... | collective-permute-start | bytes 98312 | tf_op jit(solution)/shard_map/ppermute | solution.py:479
  54.3 8.2 %collective-permute-start.12 = (f32[352,128]{1,0:T(8,128)S(1)}, f32[352,128]{1,0:T(8,128)S(1)}, u32[]{:S(2)}, u32[]{:S(2)}) collective-permute-start(f32[352,128]{1,0:T(8,128)S(1)} %collective-permute-done.5.refs_1_), channel_id=1, source_target_pairs={{0,1},{1,0},{2,3},{3,2},{4,5},{5,4},{6,7},{7,6},{8,9},{9,8},{10,11... | collective-permute-start | bytes 540680 | tf_op jit(solution)/shard_map/ppermute | solution.py:489
  54.6 7.9 %collective-permute-start.13 = (f32[352,128]{1,0:T(8,128)S(1)}, f32[352,128]{1,0:T(8,128)S(1)}, u32[]{:S(2)}, u32[]{:S(2)}) collective-permute-start(f32[352,128]{1,0:T(8,128)S(1)} %collective-permute-done.6.refs_2_), channel_id=1, source_target_pairs={{0,1},{1,0},{2,3},{3,2},{4,5},{5,4},{6,7},{7,6},{8,9},{9,8},{10,11... | collective-permute-start | bytes 540680 | tf_op jit(solution)/shard_map/ppermute | solution.py:489
  59.9 3.0 %collective-permute-start.18 = (f32[32,256]{1,0:T(8,128)S(1)}, f32[32,256]{1,0:T(8,128)S(1)}, u32[]{:S(2)}, u32[]{:S(2)}) collective-permute-start(f32[32,256]{1,0:T(8,128)S(1)} %get-tuple-element.538), channel_id=1, source_target_pairs={{0,4},{8,12},{16,20},{24,28},{32,36},{40,44},{48,52},{56,60},{64,6... | collective-permute-start | bytes 98312 | tf_op jit(solution)/shard_map/ppermute | solution.py:479
  60.0 6.3 %collective-permute-start.17 = (f32[32,256]{1,0:T(8,128)S(1)}, f32[32,256]{1,0:T(8,128)S(1)}, u32[]{:S(2)}, u32[]{:S(2)}) collective-permute-start(f32[32,256]{1,0:T(8,128)S(1)} %get-tuple-element.538), channel_id=1, source_target_pairs={{0,8},{4,252},{8,16},{12,4},{16,24},{20,12},{24,32},{28,20},{32,40... | collective-permute-start | bytes 98312 | tf_op jit(solution)/shard_map/ppermute | solution.py:485
  60.3 7.4 %collective-permute-start.16 = (f32[32,512]{1,0:T(8,128)S(1)}, f32[32,512]{1,0:T(8,128)S(1)}, u32[]{:S(2)}, u32[]{:S(2)}) collective-permute-start(f32[32,512]{1,0:T(8,128)S(1)} %get-tuple-element.534.refs_0_.refs_4_), channel_id=1, source_target_pairs={{4,8},{12,16},{20,24},{28,32},{36,40},{44,48},{52,56},{60,64},{68,... | collective-permute-start | bytes 196616 | tf_op jit(solution)/shard_map/ppermute | solution.py:479
  68.3 2.8 %collective-permute-start.19 = (f32[32,256]{1,0:T(8,128)S(1)}, f32[32,256]{1,0:T(8,128)S(1)}, u32[]{:S(2)}, u32[]{:S(2)}) collective-permute-start(f32[32,256]{1,0:T(8,128)S(1)} %get-tuple-element.548), channel_id=1, source_target_pairs={{0,4},{8,12},{16,20},{24,28},{32,36},{40,44},{48,52},{56,60},{64,6... | collective-permute-start | bytes 98312 | tf_op jit(solution)/shard_map/ppermute | solution.py:479
  71.5 3.0 %collective-permute-start.22 = (f32[32,256]{1,0:T(8,128)S(1)}, f32[32,256]{1,0:T(8,128)S(1)}, u32[]{:S(2)}, u32[]{:S(2)}) collective-permute-start(f32[32,256]{1,0:T(8,128)S(1)} %get-tuple-element.553), channel_id=1, source_target_pairs={{0,4},{8,12},{16,20},{24,28},{32,36},{40,44},{48,52},{56,60},{64,6... | collective-permute-start | bytes 98312 | tf_op jit(solution)/shard_map/ppermute | solution.py:479
  71.6 6.2 %collective-permute-start.21 = (f32[32,256]{1,0:T(8,128)S(1)}, f32[32,256]{1,0:T(8,128)S(1)}, u32[]{:S(2)}, u32[]{:S(2)}) collective-permute-start(f32[32,256]{1,0:T(8,128)S(1)} %get-tuple-element.553), channel_id=1, source_target_pairs={{0,8},{4,252},{8,16},{12,4},{16,24},{20,12},{24,32},{28,20},{32,40... | collective-permute-start | bytes 98312 | tf_op jit(solution)/shard_map/ppermute | solution.py:485
  71.7 7.4 %collective-permute-start.20 = (f32[32,512]{1,0:T(8,128)S(1)}, f32[32,512]{1,0:T(8,128)S(1)}, u32[]{:S(2)}, u32[]{:S(2)}) collective-permute-start(f32[32,512]{1,0:T(8,128)S(1)} %get-tuple-element.549.refs_0_.refs_6_), channel_id=1, source_target_pairs={{4,8},{12,16},{20,24},{28,32},{36,40},{44,48},{52,56},{60,64},{68,... | collective-permute-start | bytes 196616 | tf_op jit(solution)/shard_map/ppermute | solution.py:479
  79.8 3.1 %collective-permute-start.23 = (f32[32,256]{1,0:T(8,128)S(1)}, f32[32,256]{1,0:T(8,128)S(1)}, u32[]{:S(2)}, u32[]{:S(2)}) collective-permute-start(f32[32,256]{1,0:T(8,128)S(1)} %get-tuple-element.560), channel_id=1, source_target_pairs={{0,4},{8,12},{16,20},{24,28},{32,36},{40,44},{48,52},{56,60},{64,6... | collective-permute-start | bytes 98312 | tf_op jit(solution)/shard_map/ppermute | solution.py:479
  83.3 3.0 %collective-permute-start.26 = (f32[32,256]{1,0:T(8,128)S(1)}, f32[32,256]{1,0:T(8,128)S(1)}, u32[]{:S(2)}, u32[]{:S(2)}) collective-permute-start(f32[32,256]{1,0:T(8,128)S(1)} %get-tuple-element.565), channel_id=1, source_target_pairs={{0,4},{8,12},{16,20},{24,28},{32,36},{40,44},{48,52},{56,60},{64,6... | collective-permute-start | bytes 98312 | tf_op jit(solution)/shard_map/ppermute | solution.py:479
  83.4 6.2 %collective-permute-start.25 = (f32[32,256]{1,0:T(8,128)S(1)}, f32[32,256]{1,0:T(8,128)S(1)}, u32[]{:S(2)}, u32[]{:S(2)}) collective-permute-start(f32[32,256]{1,0:T(8,128)S(1)} %get-tuple-element.565), channel_id=1, source_target_pairs={{0,8},{4,252},{8,16},{12,4},{16,24},{20,12},{24,32},{28,20},{32,40... | collective-permute-start | bytes 98312 | tf_op jit(solution)/shard_map/ppermute | solution.py:485
  83.5 7.5 %collective-permute-start.24 = (f32[32,512]{1,0:T(8,128)S(1)}, f32[32,512]{1,0:T(8,128)S(1)}, u32[]{:S(2)}, u32[]{:S(2)}) collective-permute-start(f32[32,512]{1,0:T(8,128)S(1)} %get-tuple-element.561.refs_0_.refs_8_), channel_id=1, source_target_pairs={{4,8},{12,16},{20,24},{28,32},{36,40},{44,48},{52,56},{60,64},{68,... | collective-permute-start | bytes 196616 | tf_op jit(solution)/shard_map/ppermute | solution.py:479
  91.6 2.8 %collective-permute-start.27 = (f32[32,256]{1,0:T(8,128)S(1)}, f32[32,256]{1,0:T(8,128)S(1)}, u32[]{:S(2)}, u32[]{:S(2)}) collective-permute-start(f32[32,256]{1,0:T(8,128)S(1)} %get-tuple-element.572), channel_id=1, source_target_pairs={{0,4},{8,12},{16,20},{24,28},{32,36},{40,44},{48,52},{56,60},{64,6... | collective-permute-start | bytes 98312 | tf_op jit(solution)/shard_map/ppermute | solution.py:479
  94.8 3.3 %collective-permute-start.30 = (f32[32,256]{1,0:T(8,128)S(1)}, f32[32,256]{1,0:T(8,128)S(1)}, u32[]{:S(2)}, u32[]{:S(2)}) collective-permute-start(f32[32,256]{1,0:T(8,128)S(1)} %get-tuple-element.577), channel_id=1, source_target_pairs={{0,4},{8,12},{16,20},{24,28},{32,36},{40,44},{48,52},{56,60},{64,6... | collective-permute-start | bytes 98312 | tf_op jit(solution)/shard_map/ppermute | solution.py:479
  95.2 6.1 %collective-permute-start.29 = (f32[32,256]{1,0:T(8,128)S(1)}, f32[32,256]{1,0:T(8,128)S(1)}, u32[]{:S(2)}, u32[]{:S(2)}) collective-permute-start(f32[32,256]{1,0:T(8,128)S(1)} %get-tuple-element.577), channel_id=1, source_target_pairs={{0,8},{4,252},{8,16},{12,4},{16,24},{20,12},{24,32},{28,20},{32,40... | collective-permute-start | bytes 98312 | tf_op jit(solution)/shard_map/ppermute | solution.py:485
  95.2 7.4 %collective-permute-start.28 = (f32[32,512]{1,0:T(8,128)S(1)}, f32[32,512]{1,0:T(8,128)S(1)}, u32[]{:S(2)}, u32[]{:S(2)}) collective-permute-start(f32[32,512]{1,0:T(8,128)S(1)} %get-tuple-element.573.refs_0_.refs_10_), channel_id=1, source_target_pairs={{4,8},{12,16},{20,24},{28,32},{36,40},{44,48},{52,56},{60,64},{68,... | collective-permute-start | bytes 196616 | tf_op jit(solution)/shard_map/ppermute | solution.py:479
  103.3 2.8 %collective-permute-start.31 = (f32[32,256]{1,0:T(8,128)S(1)}, f32[32,256]{1,0:T(8,128)S(1)}, u32[]{:S(2)}, u32[]{:S(2)}) collective-permute-start(f32[32,256]{1,0:T(8,128)S(1)} %get-tuple-element.584), channel_id=1, source_target_pairs={{0,4},{8,12},{16,20},{24,28},{32,36},{40,44},{48,52},{56,60},{64,6... | collective-permute-start | bytes 98312 | tf_op jit(solution)/shard_map/ppermute | solution.py:479
  107.9 37.9 %copy-start.1 = (s32[1,2,2]{2,1,0:T(2,128)S(1)}, s32[1,2,2]{2,1,0:T(2,128)}, u32[]{:S(2)}) copy-start(s32[1,2,2]{2,1,0:T(2,128)} %param.17) | copy-start | bytes 52
  128.5 16.0 %collective-permute-start.32 = (f32[72,128]{1,0:T(8,128)S(1)}, f32[72,128]{1,0:T(8,128)S(1)}, u32[]{:S(2)}, u32[]{:S(2)}) collective-permute-start(f32[72,128]{1,0:T(8,128)S(1)} %get-tuple-element.613.other), channel_id=1, source_target_pairs={{0,1},{1,0},{2,3},{3,2},{4,5},{5,4},{6,7},{7,6},{8,9},{9,8},{10,11... | collective-permute-start | bytes 110600 | tf_op jit(solution)/shard_map/ppermute | solution.py:489
  (5 other events, 114.9 us)

commit v4 on v2

--- a/solution.py
+++ b/solution.py
@@ -568,11 +568,11 @@
         sums.extend([high, low])
         return partial
 
-    def stepped(partial, first, second):
+    def stepped(partial, first, second, last=False):
         return list(
             call(
                 step_kernel,
-                (VECTOR, HALO_PART, HALO_PART),
+                (VECTOR,) if last else (VECTOR, HALO_PART, HALO_PART),
                 [],
                 [masks, partial, first, second, *operator[3:]],
             )
@@ -607,7 +607,7 @@
             [pltpu.VMEM((COLS, HALO * BS), jnp.float32)],
         )
         partial = own_part(vector)
-        sends = stepped(partial, ghost, swapped(within, 0))
+        sends = stepped(partial, ghost, swapped(within, 0), power + 2 == COUNT - 1)
     vectors.append(sends[0])
     packed = f32(PART, 2 * SUM_ROWS, BS)
     sums = call(pack_kernel, packed, [], [vectors[-1], *earlier, *sums])

time: 141 us -> 140 us (level)
  no operation moved by 1% of the time
where the time goes in v4:
time: 140 us
  starting transfers between devices  50.9 us (36%)
  waiting for transfers between devices  39.8 us (28%)
  blocking collectives  29.7 us (21%)
  Pallas kernels  16.9 us (12%)
  between operations  1.65 us (1%)
    ppermute x23, starting transfers between devices, swapped(): return lax.ppermute(value, 'sub', pairs + [(j, i) for i, j in pairs])  33.7 us
    ppermute x23, waiting for transfers between devices, swapped(): return lax.ppermute(value, 'sub', pairs + [(j, i) for i, j in pairs])  26.7 us
    all_to_all x2, blocking collectives, exchanged(): return lax.all_to_all(value, 'sub', 0, 0, axis_index_groups=groups)  19.5 us
    pallas_call x31, Pallas kernels, call(): pl.pallas_call(kernel, out_shape=out_shape, in_specs=[SMEM] * len(smem) +...  16.9 us
    ppermute x4, starting transfers between devices, core_swapped(): return lax.ppermute(value, 'fold', [(0, 1), (1, 0), (2, 3), (3, 2)])  16.6 us
    ppermute x4, waiting for transfers between devices, sent_across(): return lax.ppermute(value, 'sub', pairs)  12.2 us
    all_gather x1, blocking collectives, on_device(): gathered = lax.all_gather(right_side.T, 'fold', axis=1, tiled=True)  10.2 us
  transfers between devices with their start and end apart: 31, of which 16 were waited for; matrix products, arithmetic and copies ran while one was open for 0% of the time, Pallas kernels for 7%

profile of v4, /device:TPU:1, one launch (start us, length us, event | category | flops | bytes accessed | tf_op | source)
XLA Modules:
  0.0 139.7 jit_solution(15115005225064863736)
XLA Ops:
  0.6 10.2 %all_gather.6.gathered = f32[64,512]{1,0:T(8,128)S(1)} all-gather(f32[64,128]{1,0:T(8,128)} %bitcast.228), channel_id=1, replica_groups=mesh['sub'=64,'fold'=4] {'fold'}, dimensions={1}, use_global_device_ids=true | all-gather | bytes 163840 | tf_op jit(solution)/shard_map/all_gather | solution.py:540
  11.6 7.3 %collective-permute-start.3 = (f32[32,256]{1,0:T(8,128)S(1)}, f32[32,256]{1,0:T(8,128)S(1)}, u32[]{:S(2)}, u32[]{:S(2)}) collective-permute-start(f32[32,256]{1,0:T(8,128)S(1)} %get-tuple-element.502), channel_id=1, source_target_pairs={{4,8},{12,16},{20,24},{28,32},{36,40},{44,48},{52,56},{60,64},{68,... | collective-permute-start | bytes 98312 | tf_op jit(solution)/shard_map/ppermute | solution.py:479
  18.9 3.2 %shard_map.60 = (bf16[512,512]{1,0:T(8,128)(2,1)S(1)}, bf16[512,512]{1,0:T(8,128)(2,1)S(1)}, bf16[512,512]{1,0:T(8,128)(2,1)S(1)}, bf16[512,512]{1,0:T(8,128)(2,...) custom-call(s32[4,7]{1,0:T(4,128)} %cols.1, ...), custom_call_target="tpu_custom_call" | custom-call | flops 1000000000 | bytes 1048576 | tf_op jit(solution)/shard_map/pallas_call | solution.py:458
  22.4 1.6 %collective-permute-start.2 = (f32[352,128]{1,0:T(8,128)S(1)}, f32[352,128]{1,0:T(8,128)S(1)}, u32[]{:S(2)}, u32[]{:S(2)}) collective-permute-start(f32[352,128]{1,0:T(8,128)S(1)} %get-tuple-element.499), channel_id=1, source_target_pairs={{4,8},{12,16},{20,24},{28,32},{36,40},{44,48},{52,56},{60,64},{68,... | collective-permute-start | bytes 540680 | tf_op jit(solution)/shard_map/ppermute | solution.py:479
  24.5 4.1 %collective-permute-start.6 = (f32[32,256]{1,0:T(8,128)S(1)}, f32[32,256]{1,0:T(8,128)S(1)}, u32[]{:S(2)}, u32[]{:S(2)}) collective-permute-start(f32[32,256]{1,0:T(8,128)S(1)} %get-tuple-element.514), channel_id=1, source_target_pairs={{4,8},{12,16},{20,24},{28,32},{36,40},{44,48},{52,56},{60,64},{68,... | collective-permute-start | bytes 98312 | tf_op jit(solution)/shard_map/ppermute | solution.py:479
  29.0 1.7 %collective-permute-start.5 = (f32[352,128]{1,0:T(8,128)S(1)}, f32[352,128]{1,0:T(8,128)S(1)}, u32[]{:S(2)}, u32[]{:S(2)}) collective-permute-start(f32[352,128]{1,0:T(8,128)S(1)} %get-tuple-element.511), channel_id=1, source_target_pairs={{4,8},{12,16},{20,24},{28,32},{36,40},{44,48},{52,56},{60,64},{68,... | collective-permute-start | bytes 540680 | tf_op jit(solution)/shard_map/ppermute | solution.py:479
  30.6 2.4 %collective-permute-done.6.first = f32[32,256]{1,0:T(8,128)S(1)} collective-permute-done((f32[32,256]{1,0:T(8,128)S(1)}, f32[32,256]{1,0:T(8,128)S(1)}, u32[]{:S(2)}, u32[]{:S(2)}) %collective-permute-start.6) | collective-permute-done | bytes 32800 | tf_op jit(solution)/shard_map/ppermute | solution.py:479
  33.8 2.6 %collective-permute-start.8 = (f32[352,128]{1,0:T(8,128)S(1)}, f32[352,128]{1,0:T(8,128)S(1)}, u32[]{:S(2)}, u32[]{:S(2)}) collective-permute-start(f32[352,128]{1,0:T(8,128)S(1)} %get-tuple-element.520), channel_id=1, source_target_pairs={{4,8},{12,16},{20,24},{28,32},{36,40},{44,48},{52,56},{60,64},{68,... | collective-permute-start | bytes 540680 | tf_op jit(solution)/shard_map/ppermute | solution.py:479
  36.4 3.1 %collective-permute-start.9 = (f32[32,256]{1,0:T(8,128)S(1)}, f32[32,256]{1,0:T(8,128)S(1)}, u32[]{:S(2)}, u32[]{:S(2)}) collective-permute-start(f32[32,256]{1,0:T(8,128)S(1)} %get-tuple-element.522), channel_id=1, source_target_pairs={{4,8},{12,16},{20,24},{28,32},{36,40},{44,48},{52,56},{60,64},{68,... | collective-permute-start | bytes 98312 | tf_op jit(solution)/shard_map/ppermute | solution.py:479
  39.5 4.5 %collective-permute-done.9.first = f32[32,256]{1,0:T(8,128)S(1)} collective-permute-done((f32[32,256]{1,0:T(8,128)S(1)}, f32[32,256]{1,0:T(8,128)S(1)}, u32[]{:S(2)}, u32[]{:S(2)}) %collective-permute-start.9) | collective-permute-done | bytes 32800 | tf_op jit(solution)/shard_map/ppermute | solution.py:479
  44.4 2.7 %collective-permute-start.11 = (f32[352,128]{1,0:T(8,128)S(1)}, f32[352,128]{1,0:T(8,128)S(1)}, u32[]{:S(2)}, u32[]{:S(2)}) collective-permute-start(f32[352,128]{1,0:T(8,128)S(1)} %collective-permute-done.2.refs_0_), channel_id=1, source_target_pairs={{0,1},{1,0},{2,3},{3,2},{4,5},{5,4},{6,7},{7,6},{8,9},{9,8},{10,11... | collective-permute-start | bytes 540680 | tf_op jit(solution)/shard_map/ppermute | solution.py:489
  47.1 2.6 %collective-permute-start.14 = (f32[32,256]{1,0:T(8,128)S(1)}, f32[32,256]{1,0:T(8,128)S(1)}, u32[]{:S(2)}, u32[]{:S(2)}) collective-permute-start(f32[32,256]{1,0:T(8,128)S(1)} %get-tuple-element.533), channel_id=1, source_target_pairs={{4,8},{12,16},{20,24},{28,32},{36,40},{44,48},{52,56},{60,64},{68,... | collective-permute-start | bytes 98312 | tf_op jit(solution)/shard_map/ppermute | solution.py:479
  50.6 3.6 %collective-permute-done.14.first = f32[32,256]{1,0:T(8,128)S(1)} collective-permute-done((f32[32,256]{1,0:T(8,128)S(1)}, f32[32,256]{1,0:T(8,128)S(1)}, u32[]{:S(2)}, u32[]{:S(2)}) %collective-permute-start.14) | collective-permute-done | bytes 32800 | tf_op jit(solution)/shard_map/ppermute | solution.py:479
  54.9 2.7 %collective-permute-start.16 = (f32[32,512]{1,0:T(8,128)S(1)}, f32[32,512]{1,0:T(8,128)S(1)}, u32[]{:S(2)}, u32[]{:S(2)}) collective-permute-start(f32[32,512]{1,0:T(8,128)S(1)} %get-tuple-element.535.refs_0_.refs_4_), channel_id=1, source_target_pairs={{4,8},{12,16},{20,24},{28,32},{36,40},{44,48},{52,56},{60,64},{68,... | collective-permute-start | bytes 196616 | tf_op jit(solution)/shard_map/ppermute | solution.py:479
  58.4 2.6 %collective-permute-done.17.across = f32[32,256]{1,0:T(8,128)S(1)} collective-permute-done((f32[32,256]{1,0:T(8,128)S(1)}, f32[32,256]{1,0:T(8,128)S(1)}, u32[]{:S(2)}, u32[]{:S(2)}) %collective-permute-start.17) | collective-permute-done | bytes 32800 | tf_op jit(solution)/shard_map/ppermute | solution.py:485
  61.0 1.5 %collective-permute-done.16.whole = f32[32,512]{1,0:T(8,128)S(1)} collective-permute-done((f32[32,512]{1,0:T(8,128)S(1)}, f32[32,512]{1,0:T(8,128)S(1)}, u32[]{:S(2)}, u32[]{:S(2)}) %collective-permute-start.16) | collective-permute-done | bytes 65568 | tf_op jit(solution)/shard_map/ppermute | solution.py:479
  63.6 2.4 %collective-permute-done.19.second = f32[32,256]{1,0:T(8,128)S(1)} collective-permute-done((f32[32,256]{1,0:T(8,128)S(1)}, f32[32,256]{1,0:T(8,128)S(1)}, u32[]{:S(2)}, u32[]{:S(2)}) %collective-permute-start.19) | collective-permute-done | bytes 32800 | tf_op jit(solution)/shard_map/ppermute | solution.py:479
  66.5 2.5 %collective-permute-start.20 = (f32[32,512]{1,0:T(8,128)S(1)}, f32[32,512]{1,0:T(8,128)S(1)}, u32[]{:S(2)}, u32[]{:S(2)}) collective-permute-start(f32[32,512]{1,0:T(8,128)S(1)} %get-tuple-element.550.refs_0_.refs_6_), channel_id=1, source_target_pairs={{4,8},{12,16},{20,24},{28,32},{36,40},{44,48},{52,56},{60,64},{68,... | collective-permute-start | bytes 196616 | tf_op jit(solution)/shard_map/ppermute | solution.py:479
  69.4 3.2 %collective-permute-done.21.across = f32[32,256]{1,0:T(8,128)S(1)} collective-permute-done((f32[32,256]{1,0:T(8,128)S(1)}, f32[32,256]{1,0:T(8,128)S(1)}, u32[]{:S(2)}, u32[]{:S(2)}) %collective-permute-start.21) | collective-permute-done | bytes 32800 | tf_op jit(solution)/shard_map/ppermute | solution.py:485
  72.6 1.4 collective-permute-done.20.whole
  75.1 2.7 %collective-permute-done.23.second = f32[32,256]{1,0:T(8,128)S(1)} collective-permute-done((f32[32,256]{1,0:T(8,128)S(1)}, f32[32,256]{1,0:T(8,128)S(1)}, u32[]{:S(2)}, u32[]{:S(2)}) %collective-permute-start.23) | collective-permute-done | bytes 32800 | tf_op jit(solution)/shard_map/ppermute | solution.py:479
  78.3 2.5 %collective-permute-start.24 = (f32[32,512]{1,0:T(8,128)S(1)}, f32[32,512]{1,0:T(8,128)S(1)}, u32[]{:S(2)}, u32[]{:S(2)}) collective-permute-start(f32[32,512]{1,0:T(8,128)S(1)} %get-tuple-element.562.refs_0_.refs_8_), channel_id=1, source_target_pairs={{4,8},{12,16},{20,24},{28,32},{36,40},{44,48},{52,56},{60,64},{68,... | collective-permute-start | bytes 196616 | tf_op jit(solution)/shard_map/ppermute | solution.py:479
  81.2 3.2 %collective-permute-done.25.across = f32[32,256]{1,0:T(8,128)S(1)} collective-permute-done((f32[32,256]{1,0:T(8,128)S(1)}, f32[32,256]{1,0:T(8,128)S(1)}, u32[]{:S(2)}, u32[]{:S(2)}) %collective-permute-start.25) | collective-permute-done | bytes 32800 | tf_op jit(solution)/shard_map/ppermute | solution.py:485
  84.4 1.4 collective-permute-done.24.whole
  86.8 3.0 %collective-permute-done.27.second = f32[32,256]{1,0:T(8,128)S(1)} collective-permute-done((f32[32,256]{1,0:T(8,128)S(1)}, f32[32,256]{1,0:T(8,128)S(1)}, u32[]{:S(2)}, u32[]{:S(2)}) %collective-permute-start.27) | collective-permute-done | bytes 32800 | tf_op jit(solution)/shard_map/ppermute | solution.py:479
  90.4 2.4 %collective-permute-start.28 = (f32[32,512]{1,0:T(8,128)S(1)}, f32[32,512]{1,0:T(8,128)S(1)}, u32[]{:S(2)}, u32[]{:S(2)}) collective-permute-start(f32[32,512]{1,0:T(8,128)S(1)} %get-tuple-element.574.refs_0_.refs_10_), channel_id=1, source_target_pairs={{4,8},{12,16},{20,24},{28,32},{36,40},{44,48},{52,56},{60,64},{68,... | collective-permute-start | bytes 196616 | tf_op jit(solution)/shard_map/ppermute | solution.py:479
  93.2 3.2 %collective-permute-done.29.across = f32[32,256]{1,0:T(8,128)S(1)} collective-permute-done((f32[32,256]{1,0:T(8,128)S(1)}, f32[32,256]{1,0:T(8,128)S(1)}, u32[]{:S(2)}, u32[]{:S(2)}) %collective-permute-start.29) | collective-permute-done | bytes 32800 | tf_op jit(solution)/shard_map/ppermute | solution.py:485
  96.5 1.6 %collective-permute-done.28.whole = f32[32,512]{1,0:T(8,128)S(1)} collective-permute-done((f32[32,512]{1,0:T(8,128)S(1)}, f32[32,512]{1,0:T(8,128)S(1)}, u32[]{:S(2)}, u32[]{:S(2)}) %collective-permute-start.28) | collective-permute-done | bytes 65568 | tf_op jit(solution)/shard_map/ppermute | solution.py:479
  99.2 2.3 %collective-permute-done.31.second = f32[32,256]{1,0:T(8,128)S(1)} collective-permute-done((f32[32,256]{1,0:T(8,128)S(1)}, f32[32,256]{1,0:T(8,128)S(1)}, u32[]{:S(2)}, u32[]{:S(2)}) %collective-permute-start.31) | collective-permute-done | bytes 32800 | tf_op jit(solution)/shard_map/ppermute | solution.py:479
  102.7 11.2 %all_to_all.10.parts = f32[8,48,128]{2,1,0:T(8,128)S(1)} all-to-all(f32[8,48,128]{2,1,0:T(8,128)S(1)} %shard_map.86), channel_id=1, replica_groups={{0,32,64,96,128,160,192,224},{4,36,68,100,132,164,196,228},{8,40,72,104..., dimensions={0} | all-to-all | bytes 393216 | tf_op jit(solution)/shard_map/all_to_all | solution.py:471
  113.9 8.3 %all_to_all.11.parts = f32[8,48,128]{2,1,0:T(8,128)S(1)} all-to-all(f32[8,48,128]{2,1,0:T(8,128)S(1)} %shard_map.87), channel_id=1, replica_groups={{0,4,8,12,16,20,24,28},{32,36,40,44,48,52,56,60},{64,68,72,76,80,84,88,..., dimensions={0} | all-to-all | bytes 393216 | tf_op jit(solution)/shard_map/all_to_all | solution.py:471
  123.4 13.4 %collective-permute-start.32 = (f32[72,128]{1,0:T(8,128)S(1)}, f32[72,128]{1,0:T(8,128)S(1)}, u32[]{:S(2)}, u32[]{:S(2)}) collective-permute-start(f32[72,128]{1,0:T(8,128)S(1)} %get-tuple-element.613.other), channel_id=1, source_target_pairs={{0,1},{1,0},{2,3},{3,2},{4,5},{5,4},{6,7},{7,6},{8,9},{9,8},{10,11... | collective-permute-start | bytes 110600 | tf_op jit(solution)/shard_map/ppermute | solution.py:489
  (77 shorter events, 17.0 us)
Async XLA Ops:
  11.6 12.5 %collective-permute-start.3 = (f32[32,256]{1,0:T(8,128)S(1)}, f32[32,256]{1,0:T(8,128)S(1)}, u32[]{:S(2)}, u32[]{:S(2)}) collective-permute-start(f32[32,256]{1,0:T(8,128)S(1)} %get-tuple-element.502), channel_id=1, source_target_pairs={{4,8},{12,16},{20,24},{28,32},{36,40},{44,48},{52,56},{60,64},{68,... | collective-permute-start | bytes 98312 | tf_op jit(solution)/shard_map/ppermute | solution.py:479
  18.9 5.2 %collective-permute-start.4 = (f32[32,256]{1,0:T(8,128)S(1)}, f32[32,256]{1,0:T(8,128)S(1)}, u32[]{:S(2)}, u32[]{:S(2)}) collective-permute-start(f32[32,256]{1,0:T(8,128)S(1)} %get-tuple-element.503), channel_id=1, source_target_pairs={{0,4},{8,12},{16,20},{24,28},{32,36},{40,44},{48,52},{56,60},{64,6... | collective-permute-start | bytes 98312 | tf_op jit(solution)/shard_map/ppermute | solution.py:479
  22.4 22.0 %collective-permute-start.2 = (f32[352,128]{1,0:T(8,128)S(1)}, f32[352,128]{1,0:T(8,128)S(1)}, u32[]{:S(2)}, u32[]{:S(2)}) collective-permute-start(f32[352,128]{1,0:T(8,128)S(1)} %get-tuple-element.499), channel_id=1, source_target_pairs={{4,8},{12,16},{20,24},{28,32},{36,40},{44,48},{52,56},{60,64},{68,... | collective-permute-start | bytes 540680 | tf_op jit(solution)/shard_map/ppermute | solution.py:479
  24.5 8.6 %collective-permute-start.6 = (f32[32,256]{1,0:T(8,128)S(1)}, f32[32,256]{1,0:T(8,128)S(1)}, u32[]{:S(2)}, u32[]{:S(2)}) collective-permute-start(f32[32,256]{1,0:T(8,128)S(1)} %get-tuple-element.514), channel_id=1, source_target_pairs={{4,8},{12,16},{20,24},{28,32},{36,40},{44,48},{52,56},{60,64},{68,... | collective-permute-start | bytes 98312 | tf_op jit(solution)/shard_map/ppermute | solution.py:479
  28.6 4.4 %collective-permute-start.7 = (f32[32,256]{1,0:T(8,128)S(1)}, f32[32,256]{1,0:T(8,128)S(1)}, u32[]{:S(2)}, u32[]{:S(2)}) collective-permute-start(f32[32,256]{1,0:T(8,128)S(1)} %get-tuple-element.515), channel_id=1, source_target_pairs={{0,4},{8,12},{16,20},{24,28},{32,36},{40,44},{48,52},{56,60},{64,6... | collective-permute-start | bytes 98312 | tf_op jit(solution)/shard_map/ppermute | solution.py:479
  29.0 15.4 %collective-permute-start.5 = (f32[352,128]{1,0:T(8,128)S(1)}, f32[352,128]{1,0:T(8,128)S(1)}, u32[]{:S(2)}, u32[]{:S(2)}) collective-permute-start(f32[352,128]{1,0:T(8,128)S(1)} %get-tuple-element.511), channel_id=1, source_target_pairs={{4,8},{12,16},{20,24},{28,32},{36,40},{44,48},{52,56},{60,64},{68,... | collective-permute-start | bytes 540680 | tf_op jit(solution)/shard_map/ppermute | solution.py:479
  33.8 10.6 %collective-permute-start.8 = (f32[352,128]{1,0:T(8,128)S(1)}, f32[352,128]{1,0:T(8,128)S(1)}, u32[]{:S(2)}, u32[]{:S(2)}) collective-permute-start(f32[352,128]{1,0:T(8,128)S(1)} %get-tuple-element.520), channel_id=1, source_target_pairs={{4,8},{12,16},{20,24},{28,32},{36,40},{44,48},{52,56},{60,64},{68,... | collective-permute-start | bytes 540680 | tf_op jit(solution)/shard_map/ppermute | solution.py:479
  36.4 7.6 %collective-permute-start.9 = (f32[32,256]{1,0:T(8,128)S(1)}, f32[32,256]{1,0:T(8,128)S(1)}, u32[]{:S(2)}, u32[]{:S(2)}) collective-permute-start(f32[32,256]{1,0:T(8,128)S(1)} %get-tuple-element.522), channel_id=1, source_target_pairs={{4,8},{12,16},{20,24},{28,32},{36,40},{44,48},{52,56},{60,64},{68,... | collective-permute-start | bytes 98312 | tf_op jit(solution)/shard_map/ppermute | solution.py:479
  39.5 4.5 %collective-permute-start.10 = (f32[32,256]{1,0:T(8,128)S(1)}, f32[32,256]{1,0:T(8,128)S(1)}, u32[]{:S(2)}, u32[]{:S(2)}) collective-permute-start(f32[32,256]{1,0:T(8,128)S(1)} %get-tuple-element.523), channel_id=1, source_target_pairs={{0,4},{8,12},{16,20},{24,28},{32,36},{40,44},{48,52},{56,60},{64,6... | collective-permute-start | bytes 98312 | tf_op jit(solution)/shard_map/ppermute | solution.py:479
  44.4 10.5 %collective-permute-start.11 = (f32[352,128]{1,0:T(8,128)S(1)}, f32[352,128]{1,0:T(8,128)S(1)}, u32[]{:S(2)}, u32[]{:S(2)}) collective-permute-start(f32[352,128]{1,0:T(8,128)S(1)} %collective-permute-done.2.refs_0_), channel_id=1, source_target_pairs={{0,1},{1,0},{2,3},{3,2},{4,5},{5,4},{6,7},{7,6},{8,9},{9,8},{10,11... | collective-permute-start | bytes 540680 | tf_op jit(solution)/shard_map/ppermute | solution.py:489
  47.1 7.0 %collective-permute-start.14 = (f32[32,256]{1,0:T(8,128)S(1)}, f32[32,256]{1,0:T(8,128)S(1)}, u32[]{:S(2)}, u32[]{:S(2)}) collective-permute-start(f32[32,256]{1,0:T(8,128)S(1)} %get-tuple-element.533), channel_id=1, source_target_pairs={{4,8},{12,16},{20,24},{28,32},{36,40},{44,48},{52,56},{60,64},{68,... | collective-permute-start | bytes 98312 | tf_op jit(solution)/shard_map/ppermute | solution.py:479
  49.7 4.4 %collective-permute-start.15 = (f32[32,256]{1,0:T(8,128)S(1)}, f32[32,256]{1,0:T(8,128)S(1)}, u32[]{:S(2)}, u32[]{:S(2)}) collective-permute-start(f32[32,256]{1,0:T(8,128)S(1)} %get-tuple-element.534), channel_id=1, source_target_pairs={{0,4},{8,12},{16,20},{24,28},{32,36},{40,44},{48,52},{56,60},{64,6... | collective-permute-start | bytes 98312 | tf_op jit(solution)/shard_map/ppermute | solution.py:479
  49.7 8.2 %collective-permute-start.12 = (f32[352,128]{1,0:T(8,128)S(1)}, f32[352,128]{1,0:T(8,128)S(1)}, u32[]{:S(2)}, u32[]{:S(2)}) collective-permute-start(f32[352,128]{1,0:T(8,128)S(1)} %collective-permute-done.5.refs_1_), channel_id=1, source_target_pairs={{0,1},{1,0},{2,3},{3,2},{4,5},{5,4},{6,7},{7,6},{8,9},{9,8},{10,11... | collective-permute-start | bytes 540680 | tf_op jit(solution)/shard_map/ppermute | solution.py:489
  50.1 7.9 %collective-permute-start.13 = (f32[352,128]{1,0:T(8,128)S(1)}, f32[352,128]{1,0:T(8,128)S(1)}, u32[]{:S(2)}, u32[]{:S(2)}) collective-permute-start(f32[352,128]{1,0:T(8,128)S(1)} %collective-permute-done.8.refs_2_), channel_id=1, source_target_pairs={{0,1},{1,0},{2,3},{3,2},{4,5},{5,4},{6,7},{7,6},{8,9},{9,8},{10,11... | collective-permute-start | bytes 540680 | tf_op jit(solution)/shard_map/ppermute | solution.py:489
  54.5 3.9 %collective-permute-start.18 = (f32[32,256]{1,0:T(8,128)S(1)}, f32[32,256]{1,0:T(8,128)S(1)}, u32[]{:S(2)}, u32[]{:S(2)}) collective-permute-start(f32[32,256]{1,0:T(8,128)S(1)} %get-tuple-element.539), channel_id=1, source_target_pairs={{0,4},{8,12},{16,20},{24,28},{32,36},{40,44},{48,52},{56,60},{64,6... | collective-permute-start | bytes 98312 | tf_op jit(solution)/shard_map/ppermute | solution.py:479
  54.6 6.3 %collective-permute-start.17 = (f32[32,256]{1,0:T(8,128)S(1)}, f32[32,256]{1,0:T(8,128)S(1)}, u32[]{:S(2)}, u32[]{:S(2)}) collective-permute-start(f32[32,256]{1,0:T(8,128)S(1)} %get-tuple-element.539), channel_id=1, source_target_pairs={{0,8},{4,252},{8,16},{12,4},{16,24},{20,12},{24,32},{28,20},{32,40... | collective-permute-start | bytes 98312 | tf_op jit(solution)/shard_map/ppermute | solution.py:485
  54.9 7.6 %collective-permute-start.16 = (f32[32,512]{1,0:T(8,128)S(1)}, f32[32,512]{1,0:T(8,128)S(1)}, u32[]{:S(2)}, u32[]{:S(2)}) collective-permute-start(f32[32,512]{1,0:T(8,128)S(1)} %get-tuple-element.535.refs_0_.refs_4_), channel_id=1, source_target_pairs={{4,8},{12,16},{20,24},{28,32},{36,40},{44,48},{52,56},{60,64},{68,... | collective-permute-start | bytes 196616 | tf_op jit(solution)/shard_map/ppermute | solution.py:479
  63.1 2.8 %collective-permute-start.19 = (f32[32,256]{1,0:T(8,128)S(1)}, f32[32,256]{1,0:T(8,128)S(1)}, u32[]{:S(2)}, u32[]{:S(2)}) collective-permute-start(f32[32,256]{1,0:T(8,128)S(1)} %get-tuple-element.549), channel_id=1, source_target_pairs={{0,4},{8,12},{16,20},{24,28},{32,36},{40,44},{48,52},{56,60},{64,6... | collective-permute-start | bytes 98312 | tf_op jit(solution)/shard_map/ppermute | solution.py:479
  66.4 3.1 %collective-permute-start.22 = (f32[32,256]{1,0:T(8,128)S(1)}, f32[32,256]{1,0:T(8,128)S(1)}, u32[]{:S(2)}, u32[]{:S(2)}) collective-permute-start(f32[32,256]{1,0:T(8,128)S(1)} %get-tuple-element.554), channel_id=1, source_target_pairs={{0,4},{8,12},{16,20},{24,28},{32,36},{40,44},{48,52},{56,60},{64,6... | collective-permute-start | bytes 98312 | tf_op jit(solution)/shard_map/ppermute | solution.py:479
  66.5 6.2 %collective-permute-start.21 = (f32[32,256]{1,0:T(8,128)S(1)}, f32[32,256]{1,0:T(8,128)S(1)}, u32[]{:S(2)}, u32[]{:S(2)}) collective-permute-start(f32[32,256]{1,0:T(8,128)S(1)} %get-tuple-element.554), channel_id=1, source_target_pairs={{0,8},{4,252},{8,16},{12,4},{16,24},{20,12},{24,32},{28,20},{32,40... | collective-permute-start | bytes 98312 | tf_op jit(solution)/shard_map/ppermute | solution.py:485
  66.5 7.4 %collective-permute-start.20 = (f32[32,512]{1,0:T(8,128)S(1)}, f32[32,512]{1,0:T(8,128)S(1)}, u32[]{:S(2)}, u32[]{:S(2)}) collective-permute-start(f32[32,512]{1,0:T(8,128)S(1)} %get-tuple-element.550.refs_0_.refs_6_), channel_id=1, source_target_pairs={{4,8},{12,16},{20,24},{28,32},{36,40},{44,48},{52,56},{60,64},{68,... | collective-permute-start | bytes 196616 | tf_op jit(solution)/shard_map/ppermute | solution.py:479
  74.6 3.1 %collective-permute-start.23 = (f32[32,256]{1,0:T(8,128)S(1)}, f32[32,256]{1,0:T(8,128)S(1)}, u32[]{:S(2)}, u32[]{:S(2)}) collective-permute-start(f32[32,256]{1,0:T(8,128)S(1)} %get-tuple-element.561), channel_id=1, source_target_pairs={{0,4},{8,12},{16,20},{24,28},{32,36},{40,44},{48,52},{56,60},{64,6... | collective-permute-start | bytes 98312 | tf_op jit(solution)/shard_map/ppermute | solution.py:479
  78.1 3.0 %collective-permute-start.26 = (f32[32,256]{1,0:T(8,128)S(1)}, f32[32,256]{1,0:T(8,128)S(1)}, u32[]{:S(2)}, u32[]{:S(2)}) collective-permute-start(f32[32,256]{1,0:T(8,128)S(1)} %get-tuple-element.566), channel_id=1, source_target_pairs={{0,4},{8,12},{16,20},{24,28},{32,36},{40,44},{48,52},{56,60},{64,6... | collective-permute-start | bytes 98312 | tf_op jit(solution)/shard_map/ppermute | solution.py:479
  78.2 6.2 %collective-permute-start.25 = (f32[32,256]{1,0:T(8,128)S(1)}, f32[32,256]{1,0:T(8,128)S(1)}, u32[]{:S(2)}, u32[]{:S(2)}) collective-permute-start(f32[32,256]{1,0:T(8,128)S(1)} %get-tuple-element.566), channel_id=1, source_target_pairs={{0,8},{4,252},{8,16},{12,4},{16,24},{20,12},{24,32},{28,20},{32,40... | collective-permute-start | bytes 98312 | tf_op jit(solution)/shard_map/ppermute | solution.py:485
  78.3 7.4 %collective-permute-start.24 = (f32[32,512]{1,0:T(8,128)S(1)}, f32[32,512]{1,0:T(8,128)S(1)}, u32[]{:S(2)}, u32[]{:S(2)}) collective-permute-start(f32[32,512]{1,0:T(8,128)S(1)} %get-tuple-element.562.refs_0_.refs_8_), channel_id=1, source_target_pairs={{4,8},{12,16},{20,24},{28,32},{36,40},{44,48},{52,56},{60,64},{68,... | collective-permute-start | bytes 196616 | tf_op jit(solution)/shard_map/ppermute | solution.py:479
  86.4 3.5 %collective-permute-start.27 = (f32[32,256]{1,0:T(8,128)S(1)}, f32[32,256]{1,0:T(8,128)S(1)}, u32[]{:S(2)}, u32[]{:S(2)}) collective-permute-start(f32[32,256]{1,0:T(8,128)S(1)} %get-tuple-element.573), channel_id=1, source_target_pairs={{0,4},{8,12},{16,20},{24,28},{32,36},{40,44},{48,52},{56,60},{64,6... | collective-permute-start | bytes 98312 | tf_op jit(solution)/shard_map/ppermute | solution.py:479
  90.2 3.0 %collective-permute-start.30 = (f32[32,256]{1,0:T(8,128)S(1)}, f32[32,256]{1,0:T(8,128)S(1)}, u32[]{:S(2)}, u32[]{:S(2)}) collective-permute-start(f32[32,256]{1,0:T(8,128)S(1)} %get-tuple-element.578), channel_id=1, source_target_pairs={{0,4},{8,12},{16,20},{24,28},{32,36},{40,44},{48,52},{56,60},{64,6... | collective-permute-start | bytes 98312 | tf_op jit(solution)/shard_map/ppermute | solution.py:479
  90.3 6.2 %collective-permute-start.29 = (f32[32,256]{1,0:T(8,128)S(1)}, f32[32,256]{1,0:T(8,128)S(1)}, u32[]{:S(2)}, u32[]{:S(2)}) collective-permute-start(f32[32,256]{1,0:T(8,128)S(1)} %get-tuple-element.578), channel_id=1, source_target_pairs={{0,8},{4,252},{8,16},{12,4},{16,24},{20,12},{24,32},{28,20},{32,40... | collective-permute-start | bytes 98312 | tf_op jit(solution)/shard_map/ppermute | solution.py:485
  90.4 7.7 %collective-permute-start.28 = (f32[32,512]{1,0:T(8,128)S(1)}, f32[32,512]{1,0:T(8,128)S(1)}, u32[]{:S(2)}, u32[]{:S(2)}) collective-permute-start(f32[32,512]{1,0:T(8,128)S(1)} %get-tuple-element.574.refs_0_.refs_10_), channel_id=1, source_target_pairs={{4,8},{12,16},{20,24},{28,32},{36,40},{44,48},{52,56},{60,64},{68,... | collective-permute-start | bytes 196616 | tf_op jit(solution)/shard_map/ppermute | solution.py:479
  98.7 2.8 %collective-permute-start.31 = (f32[32,256]{1,0:T(8,128)S(1)}, f32[32,256]{1,0:T(8,128)S(1)}, u32[]{:S(2)}, u32[]{:S(2)}) collective-permute-start(f32[32,256]{1,0:T(8,128)S(1)} %get-tuple-element.585), channel_id=1, source_target_pairs={{0,4},{8,12},{16,20},{24,28},{32,36},{40,44},{48,52},{56,60},{64,6... | collective-permute-start | bytes 98312 | tf_op jit(solution)/shard_map/ppermute | solution.py:479
  102.7 36.3 %copy-start.1 = (s32[1,2,2]{2,1,0:T(2,128)S(1)}, s32[1,2,2]{2,1,0:T(2,128)}, u32[]{:S(2)}) copy-start(s32[1,2,2]{2,1,0:T(2,128)} %param.17) | copy-start | bytes 52
  123.4 14.3 %collective-permute-start.32 = (f32[72,128]{1,0:T(8,128)S(1)}, f32[72,128]{1,0:T(8,128)S(1)}, u32[]{:S(2)}, u32[]{:S(2)}) collective-permute-start(f32[72,128]{1,0:T(8,128)S(1)} %get-tuple-element.613.other), channel_id=1, source_target_pairs={{0,1},{1,0},{2,3},{3,2},{4,5},{5,4},{6,7},{7,6},{8,9},{9,8},{10,11... | collective-permute-start | bytes 110600 | tf_op jit(solution)/shard_map/ppermute | solution.py:489
  (5 other events, 110.1 us)
